TPU v7x, 32 devices: a whole 2x2x4 slice. The times are simulated.
32 devices in a mesh: gx: 4 (over y, x), gy: 2 (over core), gz: 4 (over z).
Axes of the slice: x: 2, y: 2, z: 4, core: 2. Of those that a mesh axis runs over, the one named last changes fastest.
Arguments:
- right_side: float32 [32, 64, 512], P('gx', 'gy', 'gz'), may hold values from -8 to 8
- alpha_coef: float32 [32, 64, 512], P('gx', 'gy', 'gz'), may hold values from 0.25 to 4
- beta_coef: float32 [32, 64, 512], P('gx', 'gy', 'gz'), may hold values from 0.25 to 4
Outputs:
- solution_field: float32 [32, 64, 512], P('gx', 'gy', 'gz')
- residual_field: float32 [32, 64, 512], P('gx', 'gy', 'gz')
All inputs are finite; a program needn't handle non-finite values.
Results may differ from a plain program's by a relative error of at most 0.0003.
Values sent between devices are 32-bit elements; how exact they have to be, the bound alone decides.
No kernel may reach another device: no remote copies, remote signals or barrier semaphores. Data moves between devices by JAX's collectives and lax.ppermute only.
A program may use at most 64 MiB of HBM per device.

v0:
```python
import jax
import jax.numpy as jnp
from jax import lax
from jax.sharding import PartitionSpec as P

LEVELS = 3
SWEEPS = 4
BOTTOM = 12


SHIFT_BASE = 0.01
UPPER_EIG = 2.0
SMOOTH_LOWER = 0.25
BOTTOM_LOWER = 0.02


def with_halo(block, sides, width):
    for axis, dim in sides:
        count = lax.axis_size(axis)
        forward = [(i, i + 1) for i in range(count - 1)]
        backward = [(target, source) for source, target in forward]
        low = lax.ppermute(
            lax.slice_in_dim(block, block.shape[dim] - width, None, axis=dim), axis, forward
        )
        high = lax.ppermute(lax.slice_in_dim(block, 0, width, axis=dim), axis, backward)
        block = jnp.concatenate([low, block, high], axis=dim)
    return block


def partner_2(array, axis, distance):
    return lax.ppermute(array, axis, [(i, i ^ 1 << distance) for i in range(lax.axis_size(axis))])


def split_padded(padded):
    return (
        padded[:-2, 1:-1, 1:-1],
        padded[2:, 1:-1, 1:-1],
        padded[1:-1, :-2, 1:-1],
        padded[1:-1, 2:, 1:-1],
        padded[1:-1, 1:-1, :-2],
        padded[1:-1, 1:-1, 2:],
    )


def zero_pad(field):
    return jnp.pad(field, 1)


def rim_iterate(field):
    return with_halo(field, (("gx", 0), ("gy", 1), ("gz", 2)), 1)


def rim_coefficient(field):
    return with_halo(field, (("gx", 0), ("gy", 1), ("gz", 2)), 1)


def level_operator(beta_level, alpha_level, padded_beta, shift):
    coeffs = tuple((0.5 * (beta_level + other) for other in split_padded(padded_beta)))
    diagonal = shift * alpha_level
    for coeff in coeffs:
        diagonal = diagonal + coeff
    return (coeffs, diagonal)


def apply_operator(field, operator, pad_field):
    coeffs, diagonal = operator
    others = split_padded(pad_field(field))
    total = coeffs[0] * others[0]
    for index in range(1, 6):
        total = total + coeffs[index] * others[index]
    return diagonal * field - total


def chebyshev(iterate, rhs_level, operator, count, lower, zero_start, pad_field):
    diagonal = operator[1]
    center = (UPPER_EIG + lower) / 2.0
    half_width = (UPPER_EIG - lower) / 2.0
    sigma_ratio = center / half_width
    rho_old = 1.0 / sigma_ratio
    if zero_start:
        remain = rhs_level
    else:
        remain = rhs_level - apply_operator(iterate, operator, pad_field)
    update = remain / diagonal / center
    iterate = iterate + update
    for sweep_index in range(count - 1):
        remain = rhs_level - apply_operator(iterate, operator, pad_field)
        rho_new = 1.0 / (2.0 * sigma_ratio - rho_old)
        update = rho_new * rho_old * update + 2.0 * rho_new / half_width * (remain / diagonal)
        iterate = iterate + update
        rho_old = rho_new
    return iterate


def restrict_mean(field):
    first, second, third = field.shape
    blocks = field.reshape(first // 2, 2, second // 2, 2, third // 2, 2)
    return jnp.sum(blocks, axis=(1, 3, 5)) * 0.125


def prolong_copy(field):
    return jnp.repeat(jnp.repeat(jnp.repeat(field, 2, axis=0), 2, axis=1), 2, axis=2)


def join_partner(packed, partner, device_index, bit_index, dim):
    position = device_index // 2**bit_index % 2
    lower_first = jnp.concatenate([packed, partner], axis=dim)
    upper_first = jnp.concatenate([partner, packed], axis=dim)
    return jnp.where(position == 0, lower_first, upper_first)


def shards(right_side, alpha_coef, beta_coef):
    betas = [beta_coef]
    alphas = [alpha_coef]
    for level in range(LEVELS):
        betas.append(restrict_mean(betas[-1]))
        alphas.append(restrict_mean(alphas[-1]))
    operators = []
    for level in range(LEVELS):
        padded_beta = rim_coefficient(betas[level])
        operators.append(
            level_operator(betas[level], alphas[level], padded_beta, SHIFT_BASE * 4.0**level)
        )
    rhs_levels = [right_side]
    smoothed = []
    for level in range(LEVELS):
        iterate = chebyshev(
            jnp.zeros_like(rhs_levels[level]),
            rhs_levels[level],
            operators[level],
            SWEEPS,
            SMOOTH_LOWER,
            True,
            rim_iterate,
        )
        remain = rhs_levels[level] - apply_operator(iterate, operators[level], rim_iterate)
        smoothed.append(iterate)
        rhs_levels.append(4.0 * restrict_mean(remain))
    coarse_rhs = rhs_levels[LEVELS]
    local_shape = coarse_rhs.shape
    packed = jnp.stack([coarse_rhs, betas[LEVELS], alphas[LEVELS]])
    index_x = lax.axis_index("gx")
    index_y = lax.axis_index("gy")
    index_z = lax.axis_index("gz")
    for bit_index in range(lax.axis_size("gx").bit_length() - 1):
        partner = partner_2(packed, "gx", bit_index)
        packed = join_partner(packed, partner, index_x, bit_index, 1)
    for bit_index in range(lax.axis_size("gy").bit_length() - 1):
        partner = partner_2(packed, "gy", bit_index)
        packed = join_partner(packed, partner, index_y, bit_index, 2)
    for bit_index in range(lax.axis_size("gz").bit_length() - 1):
        partner = partner_2(packed, "gz", bit_index)
        packed = join_partner(packed, partner, index_z, bit_index, 3)
    whole_rhs = packed[0]
    whole_beta = packed[1]
    whole_alpha = packed[2]
    bottom_operator = level_operator(
        whole_beta, whole_alpha, zero_pad(whole_beta), SHIFT_BASE * 4.0**LEVELS
    )
    whole_correction = chebyshev(
        jnp.zeros_like(whole_rhs), whole_rhs, bottom_operator, BOTTOM, BOTTOM_LOWER, True, zero_pad
    )
    starts = (index_x * local_shape[0], index_y * local_shape[1], index_z * local_shape[2])
    correction = lax.dynamic_slice(whole_correction, starts, local_shape)
    for level in range(LEVELS - 1, -1, -1):
        start_field = smoothed[level] + prolong_copy(correction)
        correction = chebyshev(
            start_field,
            rhs_levels[level],
            operators[level],
            SWEEPS,
            SMOOTH_LOWER,
            False,
            rim_iterate,
        )
    residual_field = right_side - apply_operator(correction, operators[0], rim_iterate)
    return (correction, residual_field)


def solution(mesh):
    in_specs = (P("gx", "gy", "gz"), P("gx", "gy", "gz"), P("gx", "gy", "gz"))
    out_specs = (P("gx", "gy", "gz"), P("gx", "gy", "gz"))
    return jax.shard_map(shards, mesh=mesh, in_specs=in_specs, out_specs=out_specs, check_vma=False)
```

profile of v0, /device:TPU:0, one launch (start us, length us, event | category | flops | bytes accessed | tf_op | source)
XLA Modules:
  0.0 683.8 jit_solution(4891052850974626831)
XLA Ops:
  1.4 4.8 collective-permute-start
  24.6 4.1 collective-permute-done.5
  31.4 4.9 collective-permute-start.6
  44.3 4.6 collective-permute-start.10
  56.1 5.4 collective-permute-start.12
  69.6 5.0 collective-permute-start.16
  82.2 5.9 collective-permute-start.18
  88.1 9.7 %reshape.99 = f32[4,2,16,2,64,2]{5,4,3,2,1,0:T(8,128)} reshape(f32[8,32,128]{2,1,0:T(8,128)S(1)} %copy-done) | data formatting | bytes 262144 | tf_op jit(solution)/shard_map/reshape | solution.py:97
  97.8 4.0 reduce_sum.104
  108.4 5.0 collective-permute-start.22
  113.5 5.1 collective-permute-start.30
  120.0 9.7 %reshape.98 = f32[4,2,16,2,64,2]{5,4,3,2,1,0:T(8,128)} reshape(f32[8,32,128]{2,1,0:T(8,128)S(1)} %copy-done.1) | data formatting | bytes 262144 | tf_op jit(solution)/shard_map/reshape | solution.py:97
  129.7 4.0 reduce_sum.103
  135.3 5.2 collective-permute-start.24
  149.9 4.6 collective-permute-start.28
  154.6 3.8 collective-permute-start.34
  160.1 9.7 %reshape.97 = f32[4,2,16,2,64,2]{5,4,3,2,1,0:T(8,128)} reshape(f32[8,32,128]{2,1,0:T(8,128)S(1)} %fusion.79) | data formatting | bytes 262144 | tf_op jit(solution)/shard_map/reshape | solution.py:97
  169.8 4.0 reduce_sum.102
  175.3 5.3 collective-permute-start.36
  188.5 5.1 collective-permute-start.40
  197.1 5.4 collective-permute-start.42
  210.4 5.2 collective-permute-start.46
  218.9 5.7 collective-permute-start.48
  230.3 5.1 collective-permute-start.60
  238.1 5.0 collective-permute-start.52
  246.5 6.3 collective-permute-start.54
  262.1 4.9 collective-permute-start.58
  267.1 3.9 collective-permute-start.64
  278.2 5.4 collective-permute-start.66
  291.5 4.5 collective-permute-start.70
  299.1 5.4 collective-permute-start.72
  312.3 4.9 collective-permute-start.76
  320.2 5.7 collective-permute-start.78
  333.7 4.9 collective-permute-start.82
  341.6 5.7 collective-permute-start.84
  355.1 4.9 collective-permute-start.88
  366.7 3.7 collective-permute-start.91
  386.7 4.5 collective-permute-start.95
  399.1 4.5 collective-permute-start.99
  406.6 4.8 collective-permute-start.101
  419.3 4.9 collective-permute-start.105
  427.1 5.4 collective-permute-start.107
  440.4 4.9 collective-permute-start.111
  448.2 5.7 collective-permute-start.113
  461.8 4.9 collective-permute-start.117
  469.9 5.7 collective-permute-start.119
  483.5 4.9 collective-permute-start.123
  491.8 5.7 collective-permute-start.125
  505.4 5.0 collective-permute-start.129
  513.9 5.7 collective-permute-start.131
  527.5 5.0 collective-permute-start.135
  536.0 5.7 collective-permute-start.137
  549.6 5.0 collective-permute-start.141
  558.6 5.7 collective-permute-start.143
  572.3 5.0 collective-permute-start.147
  577.4 3.6 collective-permute-done.148
  583.7 5.7 collective-permute-start.149
  597.5 5.0 collective-permute-start.153
  608.9 5.7 collective-permute-start.155
  622.7 5.0 collective-permute-start.159
  634.1 5.7 collective-permute-start.161
  647.8 5.0 collective-permute-start.165
  659.3 5.7 collective-permute-start.167
  673.0 5.0 collective-permute-start.171
  (496 shorter events, 343.6 us)
Async XLA Ops:
  16.4 8.1 %collective-permute-start.4 = (f32[10,34,1]{2,1,0:T(8,128)S(1)}, f32[10,34,1]{2,1,0:T(8,128)S(1)}, u32[]{:S(2)}, u32[]{:S(2)}) collective-permute-start(f32[10,34,1]{2,1,0:T(8,128)S(1)} %get-tuple-element.104), channel_id=1, source_target_pairs={{0,1},{1,2},{2,3},{4,5},{5,6},{6,7},{8,9},{9,10},{10,11},{12,13},{... | collective-permute-start | bytes 4088 | tf_op jit(solution)/shard_map/ppermute | solution.py:22
  19.9 8.8 %collective-permute-start.5 = (f32[10,34,1]{2,1,0:T(8,128)S(1)}, f32[10,34,1]{2,1,0:T(8,128)S(1)}, u32[]{:S(2)}, u32[]{:S(2)}) collective-permute-start(f32[10,34,1]{2,1,0:T(8,128)S(1)} %get-tuple-element.103), channel_id=1, source_target_pairs={{1,0},{2,1},{3,2},{5,4},{6,5},{7,6},{9,8},{10,9},{11,10},{13,12},{... | collective-permute-start | bytes 4088 | tf_op jit(solution)/shard_map/ppermute | solution.py:25
  43.0 9.2 %collective-permute-start.11 = (f32[10,34,1]{2,1,0:T(8,128)S(1)}, f32[10,34,1]{2,1,0:T(8,128)S(1)}, u32[]{:S(2)}, u32[]{:S(2)}) collective-permute-start(f32[10,34,1]{2,1,0:T(8,128)S(1)} %get-tuple-element.102), channel_id=1, source_target_pairs={{1,0},{2,1},{3,2},{5,4},{6,5},{7,6},{9,8},{10,9},{11,10},{13,12},{... | collective-permute-start | bytes 4088 | tf_op jit(solution)/shard_map/ppermute | solution.py:25
  44.3 9.1 %collective-permute-start.10 = (f32[10,34,1]{2,1,0:T(8,128)S(1)}, f32[10,34,1]{2,1,0:T(8,128)S(1)}, u32[]{:S(2)}, u32[]{:S(2)}) collective-permute-start(f32[10,34,1]{2,1,0:T(8,128)S(1)} %get-tuple-element.101), channel_id=1, source_target_pairs={{0,1},{1,2},{2,3},{4,5},{5,6},{6,7},{8,9},{9,10},{10,11},{12,13},{... | collective-permute-start | bytes 4088 | tf_op jit(solution)/shard_map/ppermute | solution.py:22
  68.3 10.0 %collective-permute-start.17 = (f32[10,34,1]{2,1,0:T(8,128)S(1)}, f32[10,34,1]{2,1,0:T(8,128)S(1)}, u32[]{:S(2)}, u32[]{:S(2)}) collective-permute-start(f32[10,34,1]{2,1,0:T(8,128)S(1)} %get-tuple-element.100), channel_id=1, source_target_pairs={{1,0},{2,1},{3,2},{5,4},{6,5},{7,6},{9,8},{10,9},{11,10},{13,12},{... | collective-permute-start | bytes 4088 | tf_op jit(solution)/shard_map/ppermute | solution.py:25
  69.6 9.8 %collective-permute-start.16 = (f32[10,34,1]{2,1,0:T(8,128)S(1)}, f32[10,34,1]{2,1,0:T(8,128)S(1)}, u32[]{:S(2)}, u32[]{:S(2)}) collective-permute-start(f32[10,34,1]{2,1,0:T(8,128)S(1)} %get-tuple-element.99), channel_id=1, source_target_pairs={{0,1},{1,2},{2,3},{4,5},{5,6},{6,7},{8,9},{9,10},{10,11},{12,13},{... | collective-permute-start | bytes 4088 | tf_op jit(solution)/shard_map/ppermute | solution.py:22
  80.9 20.9 %collective-permute-start.19 = (f32[1,32,128]{2,1,0:T(8,128)S(1)}, f32[1,32,128]{2,1,0:T(8,128)S(1)}, u32[]{:S(2)}, u32[]{:S(2)}) collective-permute-start(f32[1,32,128]{2,1,0:T(8,128)S(1)} %get-tuple-element.138), channel_id=1, source_target_pairs={{8,0},{16,8},{24,16},{9,1},{17,9},{25,17},{10,2},{18,10},{26,18},{... | collective-permute-start | bytes 49160 | tf_op jit(solution)/shard_map/ppermute | solution.py:25
  82.2 19.6 %collective-permute-start.18 = (f32[1,32,128]{2,1,0:T(8,128)S(1)}, f32[1,32,128]{2,1,0:T(8,128)S(1)}, u32[]{:S(2)}, u32[]{:S(2)}) collective-permute-start(f32[1,32,128]{2,1,0:T(8,128)S(1)} %get-tuple-element.137), channel_id=1, source_target_pairs={{0,8},{8,16},{16,24},{1,9},{9,17},{17,25},{2,10},{10,18},{18,26},{... | collective-permute-start | bytes 49160 | tf_op jit(solution)/shard_map/ppermute | solution.py:22
  107.1 26.6 %collective-permute-start.23 = (f32[10,34,1]{2,1,0:T(8,128)S(1)}, f32[10,34,1]{2,1,0:T(8,128)S(1)}, u32[]{:S(2)}, u32[]{:S(2)}) collective-permute-start(f32[10,34,1]{2,1,0:T(8,128)S(1)} %get-tuple-element.98), channel_id=1, source_target_pairs={{1,0},{2,1},{3,2},{5,4},{6,5},{7,6},{9,8},{10,9},{11,10},{13,12},{... | collective-permute-start | bytes 4088 | tf_op jit(solution)/shard_map/ppermute | solution.py:25
  108.4 25.3 %collective-permute-start.22 = (f32[10,34,1]{2,1,0:T(8,128)S(1)}, f32[10,34,1]{2,1,0:T(8,128)S(1)}, u32[]{:S(2)}, u32[]{:S(2)}) collective-permute-start(f32[10,34,1]{2,1,0:T(8,128)S(1)} %get-tuple-element.97), channel_id=1, source_target_pairs={{0,1},{1,2},{2,3},{4,5},{5,6},{6,7},{8,9},{9,10},{10,11},{12,13},{... | collective-permute-start | bytes 4088 | tf_op jit(solution)/shard_map/ppermute | solution.py:22
  113.5 27.1 %collective-permute-start.30 = (f32[1,16,64]{2,1,0:T(8,128)S(1)}, f32[1,16,64]{2,1,0:T(8,128)S(1)}, u32[]{:S(2)}, u32[]{:S(2)}) collective-permute-start(f32[1,16,64]{2,1,0:T(8,128)S(1)} %get-tuple-element.218), channel_id=1, source_target_pairs={{0,8},{8,16},{16,24},{1,9},{9,17},{17,25},{2,10},{10,18},{18,26},{... | collective-permute-start | bytes 12296 | tf_op jit(solution)/shard_map/ppermute | solution.py:22
  118.6 22.0 %collective-permute-start.31 = (f32[1,16,64]{2,1,0:T(8,128)S(1)}, f32[1,16,64]{2,1,0:T(8,128)S(1)}, u32[]{:S(2)}, u32[]{:S(2)}) collective-permute-start(f32[1,16,64]{2,1,0:T(8,128)S(1)} %get-tuple-element.217), channel_id=1, source_target_pairs={{8,0},{16,8},{24,16},{9,1},{17,9},{25,17},{10,2},{18,10},{26,18},{... | collective-permute-start | bytes 12296 | tf_op jit(solution)/shard_map/ppermute | solution.py:25
  134.0 9.2 %collective-permute-start.25 = (f32[1,32,128]{2,1,0:T(8,128)S(1)}, f32[1,32,128]{2,1,0:T(8,128)S(1)}, u32[]{:S(2)}, u32[]{:S(2)}) collective-permute-start(f32[1,32,128]{2,1,0:T(8,128)S(1)} %get-tuple-element.136), channel_id=1, source_target_pairs={{8,0},{16,8},{24,16},{9,1},{17,9},{25,17},{10,2},{18,10},{26,18},{... | collective-permute-start | bytes 49160 | tf_op jit(solution)/shard_map/ppermute | solution.py:25
  135.3 8.0 %collective-permute-start.24 = (f32[1,32,128]{2,1,0:T(8,128)S(1)}, f32[1,32,128]{2,1,0:T(8,128)S(1)}, u32[]{:S(2)}, u32[]{:S(2)}) collective-permute-start(f32[1,32,128]{2,1,0:T(8,128)S(1)} %get-tuple-element.135), channel_id=1, source_target_pairs={{0,8},{8,16},{16,24},{1,9},{9,17},{17,25},{2,10},{10,18},{18,26},{... | collective-permute-start | bytes 49160 | tf_op jit(solution)/shard_map/ppermute | solution.py:22
  140.6 7.1 %collective-permute-start.32 = (f32[6,1,64]{2,1,0:T(1,128)S(1)}, f32[6,1,64]{2,1,0:T(1,128)S(1)}, u32[]{:S(2)}, u32[]{:S(2)}) collective-permute-start(f32[6,1,64]{2,1,0:T(1,128)S(1)} %get-tuple-element.182), channel_id=1, source_target_pairs={{0,4},{1,5},{2,6},{3,7},{8,12},{9,13},{10,14},{11,15},{16,20},{17,... | collective-permute-start | bytes 4616 | tf_op jit(solution)/shard_map/ppermute | solution.py:22
  148.6 11.0 %collective-permute-start.29 = (f32[10,34,1]{2,1,0:T(8,128)S(1)}, f32[10,34,1]{2,1,0:T(8,128)S(1)}, u32[]{:S(2)}, u32[]{:S(2)}) collective-permute-start(f32[10,34,1]{2,1,0:T(8,128)S(1)} %get-tuple-element.96), channel_id=1, source_target_pairs={{1,0},{2,1},{3,2},{5,4},{6,5},{7,6},{9,8},{10,9},{11,10},{13,12},{... | collective-permute-start | bytes 4088 | tf_op jit(solution)/shard_map/ppermute | solution.py:25
  149.9 10.0 %collective-permute-start.28 = (f32[10,34,1]{2,1,0:T(8,128)S(1)}, f32[10,34,1]{2,1,0:T(8,128)S(1)}, u32[]{:S(2)}, u32[]{:S(2)}) collective-permute-start(f32[10,34,1]{2,1,0:T(8,128)S(1)} %get-tuple-element.95), channel_id=1, source_target_pairs={{0,1},{1,2},{2,3},{4,5},{5,6},{6,7},{8,9},{9,10},{10,11},{12,13},{... | collective-permute-start | bytes 4088 | tf_op jit(solution)/shard_map/ppermute | solution.py:22
  154.6 19.3 %collective-permute-start.34 = (f32[6,18,1]{2,1,0:T(8,128)S(1)}, f32[6,18,1]{2,1,0:T(8,128)S(1)}, u32[]{:S(2)}, u32[]{:S(2)}) collective-permute-start(f32[6,18,1]{2,1,0:T(8,128)S(1)} %get-tuple-element.162), channel_id=1, source_target_pairs={{0,1},{1,2},{2,3},{4,5},{5,6},{6,7},{8,9},{9,10},{10,11},{12,13},{... | collective-permute-start | bytes 1304 | tf_op jit(solution)/shard_map/ppermute | solution.py:22
  158.4 15.5 %collective-permute-start.35 = (f32[6,18,1]{2,1,0:T(8,128)S(1)}, f32[6,18,1]{2,1,0:T(8,128)S(1)}, u32[]{:S(2)}, u32[]{:S(2)}) collective-permute-start(f32[6,18,1]{2,1,0:T(8,128)S(1)} %get-tuple-element.161), channel_id=1, source_target_pairs={{1,0},{2,1},{3,2},{5,4},{6,5},{7,6},{9,8},{10,9},{11,10},{13,12},{... | collective-permute-start | bytes 1304 | tf_op jit(solution)/shard_map/ppermute | solution.py:25
  187.2 7.2 %collective-permute-start.41 = (f32[6,18,1]{2,1,0:T(8,128)S(1)}, f32[6,18,1]{2,1,0:T(8,128)S(1)}, u32[]{:S(2)}, u32[]{:S(2)}) collective-permute-start(f32[6,18,1]{2,1,0:T(8,128)S(1)} %get-tuple-element.160), channel_id=1, source_target_pairs={{1,0},{2,1},{3,2},{5,4},{6,5},{7,6},{9,8},{10,9},{11,10},{13,12},{... | collective-permute-start | bytes 1304 | tf_op jit(solution)/shard_map/ppermute | solution.py:25
  188.5 7.1 %collective-permute-start.40 = (f32[6,18,1]{2,1,0:T(8,128)S(1)}, f32[6,18,1]{2,1,0:T(8,128)S(1)}, u32[]{:S(2)}, u32[]{:S(2)}) collective-permute-start(f32[6,18,1]{2,1,0:T(8,128)S(1)} %get-tuple-element.159), channel_id=1, source_target_pairs={{0,1},{1,2},{2,3},{4,5},{5,6},{6,7},{8,9},{9,10},{10,11},{12,13},{... | collective-permute-start | bytes 1304 | tf_op jit(solution)/shard_map/ppermute | solution.py:22
  209.1 7.7 %collective-permute-start.47 = (f32[6,18,1]{2,1,0:T(8,128)S(1)}, f32[6,18,1]{2,1,0:T(8,128)S(1)}, u32[]{:S(2)}, u32[]{:S(2)}) collective-permute-start(f32[6,18,1]{2,1,0:T(8,128)S(1)} %get-tuple-element.158), channel_id=1, source_target_pairs={{1,0},{2,1},{3,2},{5,4},{6,5},{7,6},{9,8},{10,9},{11,10},{13,12},{... | collective-permute-start | bytes 1304 | tf_op jit(solution)/shard_map/ppermute | solution.py:25
  210.4 7.0 %collective-permute-start.46 = (f32[6,18,1]{2,1,0:T(8,128)S(1)}, f32[6,18,1]{2,1,0:T(8,128)S(1)}, u32[]{:S(2)}, u32[]{:S(2)}) collective-permute-start(f32[6,18,1]{2,1,0:T(8,128)S(1)} %get-tuple-element.157), channel_id=1, source_target_pairs={{0,1},{1,2},{2,3},{4,5},{5,6},{6,7},{8,9},{9,10},{10,11},{12,13},{... | collective-permute-start | bytes 1304 | tf_op jit(solution)/shard_map/ppermute | solution.py:22
  217.6 7.0 %collective-permute-start.49 = (f32[1,16,64]{2,1,0:T(8,128)S(1)}, f32[1,16,64]{2,1,0:T(8,128)S(1)}, u32[]{:S(2)}, u32[]{:S(2)}) collective-permute-start(f32[1,16,64]{2,1,0:T(8,128)S(1)} %get-tuple-element.212), channel_id=1, source_target_pairs={{8,0},{16,8},{24,16},{9,1},{17,9},{25,17},{10,2},{18,10},{26,18},{... | collective-permute-start | bytes 12296 | tf_op jit(solution)/shard_map/ppermute | solution.py:25
  218.9 7.1 %collective-permute-start.48 = (f32[1,16,64]{2,1,0:T(8,128)S(1)}, f32[1,16,64]{2,1,0:T(8,128)S(1)}, u32[]{:S(2)}, u32[]{:S(2)}) collective-permute-start(f32[1,16,64]{2,1,0:T(8,128)S(1)} %get-tuple-element.211), channel_id=1, source_target_pairs={{0,8},{8,16},{16,24},{1,9},{9,17},{17,25},{2,10},{10,18},{18,26},{... | collective-permute-start | bytes 12296 | tf_op jit(solution)/shard_map/ppermute | solution.py:22
  226.0 10.7 %collective-permute-start.51 = (f32[6,1,64]{2,1,0:T(1,128)S(1)}, f32[6,1,64]{2,1,0:T(1,128)S(1)}, u32[]{:S(2)}, u32[]{:S(2)}) collective-permute-start(f32[6,1,64]{2,1,0:T(1,128)S(1)} %get-tuple-element.176), channel_id=1, source_target_pairs={{4,0},{5,1},{6,2},{7,3},{12,8},{13,9},{14,10},{15,11},{20,16},{21,... | collective-permute-start | bytes 4616 | tf_op jit(solution)/shard_map/ppermute | solution.py:25
  227.3 9.5 %collective-permute-start.50 = (f32[6,1,64]{2,1,0:T(1,128)S(1)}, f32[6,1,64]{2,1,0:T(1,128)S(1)}, u32[]{:S(2)}, u32[]{:S(2)}) collective-permute-start(f32[6,1,64]{2,1,0:T(1,128)S(1)} %get-tuple-element.175), channel_id=1, source_target_pairs={{0,4},{1,5},{2,6},{3,7},{8,12},{9,13},{10,14},{11,15},{16,20},{17,... | collective-permute-start | bytes 4616 | tf_op jit(solution)/shard_map/ppermute | solution.py:22
  230.3 22.6 %collective-permute-start.60 = (f32[1,8,32]{2,1,0:T(8,128)S(1)}, f32[1,8,32]{2,1,0:T(8,128)S(1)}, u32[]{:S(2)}, u32[]{:S(2)}) collective-permute-start(f32[1,8,32]{2,1,0:T(8,128)S(1)} %get-tuple-element.256), channel_id=1, source_target_pairs={{0,8},{8,16},{16,24},{1,9},{9,17},{17,25},{2,10},{10,18},{18,26},{... | collective-permute-start | bytes 3080 | tf_op jit(solution)/shard_map/ppermute | solution.py:22
  235.4 17.5 %collective-permute-start.61 = (f32[1,8,32]{2,1,0:T(8,128)S(1)}, f32[1,8,32]{2,1,0:T(8,128)S(1)}, u32[]{:S(2)}, u32[]{:S(2)}) collective-permute-start(f32[1,8,32]{2,1,0:T(8,128)S(1)} %get-tuple-element.255), channel_id=1, source_target_pairs={{8,0},{16,8},{24,16},{9,1},{17,9},{25,17},{10,2},{18,10},{26,18},{... | collective-permute-start | bytes 3080 | tf_op jit(solution)/shard_map/ppermute | solution.py:25
  236.8 7.6 %collective-permute-start.53 = (f32[6,18,1]{2,1,0:T(8,128)S(1)}, f32[6,18,1]{2,1,0:T(8,128)S(1)}, u32[]{:S(2)}, u32[]{:S(2)}) collective-permute-start(f32[6,18,1]{2,1,0:T(8,128)S(1)} %get-tuple-element.156), channel_id=1, source_target_pairs={{1,0},{2,1},{3,2},{5,4},{6,5},{7,6},{9,8},{10,9},{11,10},{13,12},{... | collective-permute-start | bytes 1304 | tf_op jit(solution)/shard_map/ppermute | solution.py:25
  245.2 10.3 %collective-permute-start.55 = (f32[1,16,64]{2,1,0:T(8,128)S(1)}, f32[1,16,64]{2,1,0:T(8,128)S(1)}, u32[]{:S(2)}, u32[]{:S(2)}) collective-permute-start(f32[1,16,64]{2,1,0:T(8,128)S(1)} %get-tuple-element.210), channel_id=1, source_target_pairs={{8,0},{16,8},{24,16},{9,1},{17,9},{25,17},{10,2},{18,10},{26,18},{... | collective-permute-start | bytes 12296 | tf_op jit(solution)/shard_map/ppermute | solution.py:25
  246.5 9.0 %collective-permute-start.54 = (f32[1,16,64]{2,1,0:T(8,128)S(1)}, f32[1,16,64]{2,1,0:T(8,128)S(1)}, u32[]{:S(2)}, u32[]{:S(2)}) collective-permute-start(f32[1,16,64]{2,1,0:T(8,128)S(1)} %get-tuple-element.209), channel_id=1, source_target_pairs={{0,8},{8,16},{16,24},{1,9},{9,17},{17,25},{2,10},{10,18},{18,26},{... | collective-permute-start | bytes 12296 | tf_op jit(solution)/shard_map/ppermute | solution.py:22
  260.8 11.5 %collective-permute-start.59 = (f32[6,18,1]{2,1,0:T(8,128)S(1)}, f32[6,18,1]{2,1,0:T(8,128)S(1)}, u32[]{:S(2)}, u32[]{:S(2)}) collective-permute-start(f32[6,18,1]{2,1,0:T(8,128)S(1)} %get-tuple-element.154), channel_id=1, source_target_pairs={{1,0},{2,1},{3,2},{5,4},{6,5},{7,6},{9,8},{10,9},{11,10},{13,12},{... | collective-permute-start | bytes 1304 | tf_op jit(solution)/shard_map/ppermute | solution.py:25
  262.1 10.2 %collective-permute-start.58 = (f32[6,18,1]{2,1,0:T(8,128)S(1)}, f32[6,18,1]{2,1,0:T(8,128)S(1)}, u32[]{:S(2)}, u32[]{:S(2)}) collective-permute-start(f32[6,18,1]{2,1,0:T(8,128)S(1)} %get-tuple-element.153), channel_id=1, source_target_pairs={{0,1},{1,2},{2,3},{4,5},{5,6},{6,7},{8,9},{9,10},{10,11},{12,13},{... | collective-permute-start | bytes 1304 | tf_op jit(solution)/shard_map/ppermute | solution.py:22
  320.2 7.0 %collective-permute-start.78 = (f32[1,8,32]{2,1,0:T(8,128)S(1)}, f32[1,8,32]{2,1,0:T(8,128)S(1)}, u32[]{:S(2)}, u32[]{:S(2)}) collective-permute-start(f32[1,8,32]{2,1,0:T(8,128)S(1)} %get-tuple-element.249), channel_id=1, source_target_pairs={{0,8},{8,16},{16,24},{1,9},{9,17},{17,25},{2,10},{10,18},{18,26},{... | collective-permute-start | bytes 3080 | tf_op jit(solution)/shard_map/ppermute | solution.py:22
  340.3 7.4 %collective-permute-start.85 = (f32[1,8,32]{2,1,0:T(8,128)S(1)}, f32[1,8,32]{2,1,0:T(8,128)S(1)}, u32[]{:S(2)}, u32[]{:S(2)}) collective-permute-start(f32[1,8,32]{2,1,0:T(8,128)S(1)} %get-tuple-element.246), channel_id=1, source_target_pairs={{8,0},{16,8},{24,16},{9,1},{17,9},{25,17},{10,2},{18,10},{26,18},{... | collective-permute-start | bytes 3080 | tf_op jit(solution)/shard_map/ppermute | solution.py:25
  469.9 7.1 %collective-permute-start.119 = (f32[1,16,64]{2,1,0:T(8,128)S(1)}, f32[1,16,64]{2,1,0:T(8,128)S(1)}, u32[]{:S(2)}, u32[]{:S(2)}) collective-permute-start(f32[1,16,64]{2,1,0:T(8,128)S(1)} %get-tuple-element.189), channel_id=1, source_target_pairs={{0,8},{8,16},{16,24},{1,9},{9,17},{17,25},{2,10},{10,18},{18,26},{... | collective-permute-start | bytes 12296 | tf_op jit(solution)/shard_map/ppermute | solution.py:22
  491.8 7.1 %collective-permute-start.125 = (f32[1,16,64]{2,1,0:T(8,128)S(1)}, f32[1,16,64]{2,1,0:T(8,128)S(1)}, u32[]{:S(2)}, u32[]{:S(2)}) collective-permute-start(f32[1,16,64]{2,1,0:T(8,128)S(1)} %get-tuple-element.187), channel_id=1, source_target_pairs={{0,8},{8,16},{16,24},{1,9},{9,17},{17,25},{2,10},{10,18},{18,26},{... | collective-permute-start | bytes 12296 | tf_op jit(solution)/shard_map/ppermute | solution.py:22
  504.1 7.2 %collective-permute-start.130 = (f32[6,18,1]{2,1,0:T(8,128)S(1)}, f32[6,18,1]{2,1,0:T(8,128)S(1)}, u32[]{:S(2)}, u32[]{:S(2)}) collective-permute-start(f32[6,18,1]{2,1,0:T(8,128)S(1)} %get-tuple-element.150), channel_id=1, source_target_pairs={{1,0},{2,1},{3,2},{5,4},{6,5},{7,6},{9,8},{10,9},{11,10},{13,12},{... | collective-permute-start | bytes 1304 | tf_op jit(solution)/shard_map/ppermute | solution.py:25
  505.4 7.0 %collective-permute-start.129 = (f32[6,18,1]{2,1,0:T(8,128)S(1)}, f32[6,18,1]{2,1,0:T(8,128)S(1)}, u32[]{:S(2)}, u32[]{:S(2)}) collective-permute-start(f32[6,18,1]{2,1,0:T(8,128)S(1)} %get-tuple-element.149), channel_id=1, source_target_pairs={{0,1},{1,2},{2,3},{4,5},{5,6},{6,7},{8,9},{9,10},{10,11},{12,13},{... | collective-permute-start | bytes 1304 | tf_op jit(solution)/shard_map/ppermute | solution.py:22
  513.9 7.1 %collective-permute-start.131 = (f32[1,16,64]{2,1,0:T(8,128)S(1)}, f32[1,16,64]{2,1,0:T(8,128)S(1)}, u32[]{:S(2)}, u32[]{:S(2)}) collective-permute-start(f32[1,16,64]{2,1,0:T(8,128)S(1)} %get-tuple-element.185), channel_id=1, source_target_pairs={{0,8},{8,16},{16,24},{1,9},{9,17},{17,25},{2,10},{10,18},{18,26},{... | collective-permute-start | bytes 12296 | tf_op jit(solution)/shard_map/ppermute | solution.py:22
  526.2 7.2 %collective-permute-start.136 = (f32[6,18,1]{2,1,0:T(8,128)S(1)}, f32[6,18,1]{2,1,0:T(8,128)S(1)}, u32[]{:S(2)}, u32[]{:S(2)}) collective-permute-start(f32[6,18,1]{2,1,0:T(8,128)S(1)} %get-tuple-element.148), channel_id=1, source_target_pairs={{1,0},{2,1},{3,2},{5,4},{6,5},{7,6},{9,8},{10,9},{11,10},{13,12},{... | collective-permute-start | bytes 1304 | tf_op jit(solution)/shard_map/ppermute | solution.py:25
  527.5 7.0 %collective-permute-start.135 = (f32[6,18,1]{2,1,0:T(8,128)S(1)}, f32[6,18,1]{2,1,0:T(8,128)S(1)}, u32[]{:S(2)}, u32[]{:S(2)}) collective-permute-start(f32[6,18,1]{2,1,0:T(8,128)S(1)} %get-tuple-element.147), channel_id=1, source_target_pairs={{0,1},{1,2},{2,3},{4,5},{5,6},{6,7},{8,9},{9,10},{10,11},{12,13},{... | collective-permute-start | bytes 1304 | tf_op jit(solution)/shard_map/ppermute | solution.py:22
  536.0 7.1 %collective-permute-start.137 = (f32[1,16,64]{2,1,0:T(8,128)S(1)}, f32[1,16,64]{2,1,0:T(8,128)S(1)}, u32[]{:S(2)}, u32[]{:S(2)}) collective-permute-start(f32[1,16,64]{2,1,0:T(8,128)S(1)} %get-tuple-element.183), channel_id=1, source_target_pairs={{0,8},{8,16},{16,24},{1,9},{9,17},{17,25},{2,10},{10,18},{18,26},{... | collective-permute-start | bytes 12296 | tf_op jit(solution)/shard_map/ppermute | solution.py:22
  548.3 7.2 %collective-permute-start.142 = (f32[6,18,1]{2,1,0:T(8,128)S(1)}, f32[6,18,1]{2,1,0:T(8,128)S(1)}, u32[]{:S(2)}, u32[]{:S(2)}) collective-permute-start(f32[6,18,1]{2,1,0:T(8,128)S(1)} %get-tuple-element.146), channel_id=1, source_target_pairs={{1,0},{2,1},{3,2},{5,4},{6,5},{7,6},{9,8},{10,9},{11,10},{13,12},{... | collective-permute-start | bytes 1304 | tf_op jit(solution)/shard_map/ppermute | solution.py:25
  549.6 7.0 %collective-permute-start.141 = (f32[6,18,1]{2,1,0:T(8,128)S(1)}, f32[6,18,1]{2,1,0:T(8,128)S(1)}, u32[]{:S(2)}, u32[]{:S(2)}) collective-permute-start(f32[6,18,1]{2,1,0:T(8,128)S(1)} %get-tuple-element.145), channel_id=1, source_target_pairs={{0,1},{1,2},{2,3},{4,5},{5,6},{6,7},{8,9},{9,10},{10,11},{12,13},{... | collective-permute-start | bytes 1304 | tf_op jit(solution)/shard_map/ppermute | solution.py:22
  558.6 7.1 %collective-permute-start.143 = (f32[1,32,128]{2,1,0:T(8,128)S(1)}, f32[1,32,128]{2,1,0:T(8,128)S(1)}, u32[]{:S(2)}, u32[]{:S(2)}) collective-permute-start(f32[1,32,128]{2,1,0:T(8,128)S(1)} %get-tuple-element.133), channel_id=1, source_target_pairs={{0,8},{8,16},{16,24},{1,9},{9,17},{17,25},{2,10},{10,18},{18,26},{... | collective-permute-start | bytes 49160 | tf_op jit(solution)/shard_map/ppermute | solution.py:22
  571.0 10.0 %collective-permute-start.148 = (f32[10,34,1]{2,1,0:T(8,128)S(1)}, f32[10,34,1]{2,1,0:T(8,128)S(1)}, u32[]{:S(2)}, u32[]{:S(2)}) collective-permute-start(f32[10,34,1]{2,1,0:T(8,128)S(1)} %get-tuple-element.94), channel_id=1, source_target_pairs={{1,0},{2,1},{3,2},{5,4},{6,5},{7,6},{9,8},{10,9},{11,10},{13,12},{... | collective-permute-start | bytes 4088 | tf_op jit(solution)/shard_map/ppermute | solution.py:25
  572.3 9.8 %collective-permute-start.147 = (f32[10,34,1]{2,1,0:T(8,128)S(1)}, f32[10,34,1]{2,1,0:T(8,128)S(1)}, u32[]{:S(2)}, u32[]{:S(2)}) collective-permute-start(f32[10,34,1]{2,1,0:T(8,128)S(1)} %get-tuple-element.93), channel_id=1, source_target_pairs={{0,1},{1,2},{2,3},{4,5},{5,6},{6,7},{8,9},{9,10},{10,11},{12,13},{... | collective-permute-start | bytes 4088 | tf_op jit(solution)/shard_map/ppermute | solution.py:22
  583.7 7.1 %collective-permute-start.149 = (f32[1,32,128]{2,1,0:T(8,128)S(1)}, f32[1,32,128]{2,1,0:T(8,128)S(1)}, u32[]{:S(2)}, u32[]{:S(2)}) collective-permute-start(f32[1,32,128]{2,1,0:T(8,128)S(1)} %get-tuple-element.131), channel_id=1, source_target_pairs={{0,8},{8,16},{16,24},{1,9},{9,17},{17,25},{2,10},{10,18},{18,26},{... | collective-permute-start | bytes 49160 | tf_op jit(solution)/shard_map/ppermute | solution.py:22
  596.2 10.0 %collective-permute-start.154 = (f32[10,34,1]{2,1,0:T(8,128)S(1)}, f32[10,34,1]{2,1,0:T(8,128)S(1)}, u32[]{:S(2)}, u32[]{:S(2)}) collective-permute-start(f32[10,34,1]{2,1,0:T(8,128)S(1)} %get-tuple-element.92), channel_id=1, source_target_pairs={{1,0},{2,1},{3,2},{5,4},{6,5},{7,6},{9,8},{10,9},{11,10},{13,12},{... | collective-permute-start | bytes 4088 | tf_op jit(solution)/shard_map/ppermute | solution.py:25
  597.5 9.8 %collective-permute-start.153 = (f32[10,34,1]{2,1,0:T(8,128)S(1)}, f32[10,34,1]{2,1,0:T(8,128)S(1)}, u32[]{:S(2)}, u32[]{:S(2)}) collective-permute-start(f32[10,34,1]{2,1,0:T(8,128)S(1)} %get-tuple-element.91), channel_id=1, source_target_pairs={{0,1},{1,2},{2,3},{4,5},{5,6},{6,7},{8,9},{9,10},{10,11},{12,13},{... | collective-permute-start | bytes 4088 | tf_op jit(solution)/shard_map/ppermute | solution.py:22
  607.6 7.0 %collective-permute-start.156 = (f32[1,32,128]{2,1,0:T(8,128)S(1)}, f32[1,32,128]{2,1,0:T(8,128)S(1)}, u32[]{:S(2)}, u32[]{:S(2)}) collective-permute-start(f32[1,32,128]{2,1,0:T(8,128)S(1)} %get-tuple-element.130), channel_id=1, source_target_pairs={{8,0},{16,8},{24,16},{9,1},{17,9},{25,17},{10,2},{18,10},{26,18},{... | collective-permute-start | bytes 49160 | tf_op jit(solution)/shard_map/ppermute | solution.py:25
  608.9 7.2 %collective-permute-start.155 = (f32[1,32,128]{2,1,0:T(8,128)S(1)}, f32[1,32,128]{2,1,0:T(8,128)S(1)}, u32[]{:S(2)}, u32[]{:S(2)}) collective-permute-start(f32[1,32,128]{2,1,0:T(8,128)S(1)} %get-tuple-element.129), channel_id=1, source_target_pairs={{0,8},{8,16},{16,24},{1,9},{9,17},{17,25},{2,10},{10,18},{18,26},{... | collective-permute-start | bytes 49160 | tf_op jit(solution)/shard_map/ppermute | solution.py:22
  621.4 10.0 %collective-permute-start.160 = (f32[10,34,1]{2,1,0:T(8,128)S(1)}, f32[10,34,1]{2,1,0:T(8,128)S(1)}, u32[]{:S(2)}, u32[]{:S(2)}) collective-permute-start(f32[10,34,1]{2,1,0:T(8,128)S(1)} %get-tuple-element.90), channel_id=1, source_target_pairs={{1,0},{2,1},{3,2},{5,4},{6,5},{7,6},{9,8},{10,9},{11,10},{13,12},{... | collective-permute-start | bytes 4088 | tf_op jit(solution)/shard_map/ppermute | solution.py:25
  622.7 9.8 %collective-permute-start.159 = (f32[10,34,1]{2,1,0:T(8,128)S(1)}, f32[10,34,1]{2,1,0:T(8,128)S(1)}, u32[]{:S(2)}, u32[]{:S(2)}) collective-permute-start(f32[10,34,1]{2,1,0:T(8,128)S(1)} %get-tuple-element.89), channel_id=1, source_target_pairs={{0,1},{1,2},{2,3},{4,5},{5,6},{6,7},{8,9},{9,10},{10,11},{12,13},{... | collective-permute-start | bytes 4088 | tf_op jit(solution)/shard_map/ppermute | solution.py:22
  632.8 7.0 %collective-permute-start.162 = (f32[1,32,128]{2,1,0:T(8,128)S(1)}, f32[1,32,128]{2,1,0:T(8,128)S(1)}, u32[]{:S(2)}, u32[]{:S(2)}) collective-permute-start(f32[1,32,128]{2,1,0:T(8,128)S(1)} %get-tuple-element.128), channel_id=1, source_target_pairs={{8,0},{16,8},{24,16},{9,1},{17,9},{25,17},{10,2},{18,10},{26,18},{... | collective-permute-start | bytes 49160 | tf_op jit(solution)/shard_map/ppermute | solution.py:25
  634.1 7.2 %collective-permute-start.161 = (f32[1,32,128]{2,1,0:T(8,128)S(1)}, f32[1,32,128]{2,1,0:T(8,128)S(1)}, u32[]{:S(2)}, u32[]{:S(2)}) collective-permute-start(f32[1,32,128]{2,1,0:T(8,128)S(1)} %get-tuple-element.127), channel_id=1, source_target_pairs={{0,8},{8,16},{16,24},{1,9},{9,17},{17,25},{2,10},{10,18},{18,26},{... | collective-permute-start | bytes 49160 | tf_op jit(solution)/shard_map/ppermute | solution.py:22
  646.5 10.0 %collective-permute-start.166 = (f32[10,34,1]{2,1,0:T(8,128)S(1)}, f32[10,34,1]{2,1,0:T(8,128)S(1)}, u32[]{:S(2)}, u32[]{:S(2)}) collective-permute-start(f32[10,34,1]{2,1,0:T(8,128)S(1)} %get-tuple-element.88), channel_id=1, source_target_pairs={{1,0},{2,1},{3,2},{5,4},{6,5},{7,6},{9,8},{10,9},{11,10},{13,12},{... | collective-permute-start | bytes 4088 | tf_op jit(solution)/shard_map/ppermute | solution.py:25
  647.8 9.8 %collective-permute-start.165 = (f32[10,34,1]{2,1,0:T(8,128)S(1)}, f32[10,34,1]{2,1,0:T(8,128)S(1)}, u32[]{:S(2)}, u32[]{:S(2)}) collective-permute-start(f32[10,34,1]{2,1,0:T(8,128)S(1)} %get-tuple-element.87), channel_id=1, source_target_pairs={{0,1},{1,2},{2,3},{4,5},{5,6},{6,7},{8,9},{9,10},{10,11},{12,13},{... | collective-permute-start | bytes 4088 | tf_op jit(solution)/shard_map/ppermute | solution.py:22
  658.0 7.0 %collective-permute-start.168 = (f32[1,32,128]{2,1,0:T(8,128)S(1)}, f32[1,32,128]{2,1,0:T(8,128)S(1)}, u32[]{:S(2)}, u32[]{:S(2)}) collective-permute-start(f32[1,32,128]{2,1,0:T(8,128)S(1)} %get-tuple-element.126), channel_id=1, source_target_pairs={{8,0},{16,8},{24,16},{9,1},{17,9},{25,17},{10,2},{18,10},{26,18},{... | collective-permute-start | bytes 49160 | tf_op jit(solution)/shard_map/ppermute | solution.py:25
  659.3 7.2 %collective-permute-start.167 = (f32[1,32,128]{2,1,0:T(8,128)S(1)}, f32[1,32,128]{2,1,0:T(8,128)S(1)}, u32[]{:S(2)}, u32[]{:S(2)}) collective-permute-start(f32[1,32,128]{2,1,0:T(8,128)S(1)} %get-tuple-element.125), channel_id=1, source_target_pairs={{0,8},{8,16},{16,24},{1,9},{9,17},{17,25},{2,10},{10,18},{18,26},{... | collective-permute-start | bytes 49160 | tf_op jit(solution)/shard_map/ppermute | solution.py:22
  671.7 10.0 %collective-permute-start.172 = (f32[10,34,1]{2,1,0:T(8,128)S(1)}, f32[10,34,1]{2,1,0:T(8,128)S(1)}, u32[]{:S(2)}, u32[]{:S(2)}) collective-permute-start(f32[10,34,1]{2,1,0:T(8,128)S(1)} %get-tuple-element.86), channel_id=1, source_target_pairs={{1,0},{2,1},{3,2},{5,4},{6,5},{7,6},{9,8},{10,9},{11,10},{13,12},{... | collective-permute-start | bytes 4088 | tf_op jit(solution)/shard_map/ppermute | solution.py:25
  673.0 9.8 %collective-permute-start.171 = (f32[10,34,1]{2,1,0:T(8,128)S(1)}, f32[10,34,1]{2,1,0:T(8,128)S(1)}, u32[]{:S(2)}, u32[]{:S(2)}) collective-permute-start(f32[10,34,1]{2,1,0:T(8,128)S(1)} %get-tuple-element.85), channel_id=1, source_target_pairs={{0,1},{1,2},{2,3},{4,5},{5,6},{6,7},{8,9},{9,10},{10,11},{12,13},{... | collective-permute-start | bytes 4088 | tf_op jit(solution)/shard_map/ppermute | solution.py:22
  (113 other events, 741.0 us)
where the time goes:
time: 692 us; the launch traced here: 684 us
  starting transfers between devices  489 us (71%)
  waiting for transfers between devices  131 us (19%)
  local copies, waits for them, and re-layouts  37.7 us (5%)
  other arithmetic  23.3 us (3%)
    ppermute x84, starting transfers between devices, with_halo(): lax.ppermute(lax.slice_in_dim(block, block.shape[dim] - width, None, axis...  367 us
    ppermute x84, starting transfers between devices, with_halo(): lax.ppermute(lax.slice_in_dim(block, 0, width, axis=dim), axis, backward)  108 us
    ppermute x84, waiting for transfers between devices, with_halo(): lax.ppermute(lax.slice_in_dim(block, block.shape[dim] - width, None, axis...  79.9 us
    ppermute x84, waiting for transfers between devices, with_halo(): lax.ppermute(lax.slice_in_dim(block, 0, width, axis=dim), axis, backward)  41.8 us
    reshape x4, local copies, waits for them, and re-layouts, restrict_mean(): blocks = field.reshape(first // 2, 2, second // 2, 2, third // 2, 2)  30.2 us
  transfers between devices with their start and end apart: 173, of which 92 were waited for; matrix products, arithmetic and copies ran while one was open for 7% of the time, Pallas kernels for 0%

commit v1 on v0

--- a/solution.py
+++ b/solution.py
@@ -1,6 +1,8 @@
 import jax
 import jax.numpy as jnp
 from jax import lax
+from jax.experimental import pallas as pl
+from jax.experimental.pallas import tpu as pltpu
 from jax.sharding import PartitionSpec as P
 
 LEVELS = 3
@@ -177,7 +179,587 @@
     return (correction, residual_field)
 
 
+GX, GY, GZ = 4, 2, 4
+BLOCK = (8, 32, 128)
+RING = ("gx", "gy")
+ALL = ("gx", "gy", "gz")
+TILE = (8, 128)
+PLANES = 24
+PLANES1 = 12
+
+
+def chunk_of(x, y, z):
+    natural = 2 * (x ^ (x >> 1)) + y
+    return natural + (z % 2) * (7 - 2 * natural)
+
+
+def position():
+    return lax.axis_index("gx"), lax.axis_index("gy"), lax.axis_index("gz")
+
+
+def swap_pairs(odd):
+    place = {}
+    for x in range(GX):
+        for y in range(GY):
+            for z in range(GZ):
+                place[8 * z + chunk_of(x, y, z)] = (x * GY + y) * GZ + z
+    count = len(place)
+    if odd:
+        pairs = [(i, i + 1) for i in range(1, count - 1, 2)]
+    else:
+        pairs = [(i, i + 1) for i in range(0, count, 2)]
+    return [(place[a], place[b]) for a, b in pairs] + [(place[b], place[a]) for a, b in pairs]
+
+
+def lane_ids():
+    return lax.broadcasted_iota(jnp.int32, TILE, 1)
+
+
+def row_ids():
+    return lax.broadcasted_iota(jnp.int32, TILE, 0)
+
+
+def lanes(value, shift):
+    return pltpu.roll(value, shift % 128, value.ndim - 1)
+
+
+def rows(value, shift):
+    return pltpu.roll(value, shift % 8, value.ndim - 2)
+
+
+def regroup(tiles, axis, width, ids):
+    move = lanes if axis == 1 else rows
+    low = (ids // width) % 2 == 0
+    high = (ids // (2 * width)) % 2 == 0
+    a, b, c, d = tiles
+    a, b = jnp.where(low, a, move(b, width)), jnp.where(low, move(a, -width), b)
+    c, d = jnp.where(low, c, move(d, width)), jnp.where(low, move(c, -width), d)
+    a, c = jnp.where(high, a, move(c, 2 * width)), jnp.where(high, move(a, -2 * width), c)
+    b, d = jnp.where(high, b, move(d, 2 * width)), jnp.where(high, move(b, -2 * width), d)
+    return [a, b, c, d]
+
+
+def depth_of(k, group):
+    half, part = group // 2, group % 2
+    plane = k + 4 * part
+    return 15 - plane if half else plane
+
+
+def pack_kernel(b_ref, alpha_ref, beta_ref, out_ref, turned, staged):
+    z = lax.axis_index("gz")
+    lane = lane_ids()
+    for a, ref in enumerate((b_ref, alpha_ref, beta_ref)):
+        for xg in range(2):
+            slot = turned.at[2 * a + xg]
+            slot[...] = ref[4 * xg : 4 * xg + 4].reshape(128, 128).T
+            for k in range(4):
+                tiles = [slot[pl.ds(depth_of(k, g), 8, stride=16), :] for g in range(4)]
+                for x4, tile in enumerate(regroup(tiles, 1, 32, lane)):
+                    staged[pl.ds(a * 32 + k * 8 + 2 * x4 + xg, 8, stride=96), :] = tile
+    for x in range(GX):
+        for y in range(GY):
+            start = pl.multiple_of(chunk_of(x, y, z) * 96, 96)
+            out_ref[x * GY + y] = staged[pl.ds(start, 96), :]
+
+
+def pack(b, alpha, beta):
+    return pl.pallas_call(
+        pack_kernel,
+        out_shape=jax.ShapeDtypeStruct((8, 96, 128), jnp.float32),
+        in_specs=[pl.BlockSpec(memory_space=pltpu.VMEM)] * 3,
+        out_specs=pl.BlockSpec(memory_space=pltpu.VMEM),
+        scratch_shapes=[pltpu.VMEM((6, 128, 128), jnp.float32), pltpu.VMEM((768, 128), jnp.float32)],
+        name="pack",
+    )(b, alpha, beta)
+
+
+def slab_kernel(in_ref, out_ref):
+    lane, row = lane_ids(), row_ids()
+    low = (lane // 32) % 2 == 0
+    for a in range(3):
+        for k in range(4):
+            part = ([], [])
+            for x in range(GX):
+                first = in_ref[2 * x, pl.ds(a * 32 + k * 8, 8), :]
+                second = in_ref[2 * x + 1, pl.ds(a * 32 + k * 8, 8), :]
+                part[0].append(jnp.where(low, first, lanes(second, 32)))
+                part[1].append(jnp.where(low, lanes(first, -32), second))
+            for pp in range(2):
+                for xv, tile in enumerate(regroup(part[pp], 0, 2, row)):
+                    out_ref[a, k + 4 * pp, xv] = tile
+
+
+def to_slab(received):
+    return pl.pallas_call(
+        slab_kernel,
+        out_shape=jax.ShapeDtypeStruct((3, 8, 4) + TILE, jnp.float32),
+        in_specs=[pl.BlockSpec(memory_space=pltpu.VMEM)],
+        out_specs=pl.BlockSpec(memory_space=pltpu.VMEM),
+        name="to_slab",
+    )(received)
+
+
+class Planes:
+    def __init__(self, upper, cut, lower=None, base=0):
+        self.upper, self.cut, self.lower, self.base = upper, cut, lower, base
+
+    def __getitem__(self, p):
+        return self.upper[p - self.cut] if p >= self.cut else self.lower[p - self.base]
+
+    def __setitem__(self, p, value):
+        if p >= self.cut:
+            self.upper[p - self.cut] = value
+        else:
+            self.lower[p - self.base] = value
+
+
+def x_up(value):
+    return jnp.concatenate([value[1:], rows(value[:1], -1)], axis=0)
+
+
+def x_down(value):
+    return jnp.concatenate([rows(value[-1:], 1), value[:-1]], axis=0)
+
+
+def couple(v, p, cx, cy, cz, dup):
+    here, by_x, by_y = v[p], cx[p], cy[p]
+    total = by_x * x_up(here) + x_down(by_x * here)
+    total = total + (by_y * lanes(here, -dup) + lanes(by_y * here, dup))
+    return total + (cz[p] * v[p - 1] + cz[p + 1] * v[p + 1])
+
+
+def chebyshev_factors(count, lower):
+    center = (UPPER_EIG + lower) / 2.0
+    half_width = (UPPER_EIG - lower) / 2.0
+    ratio = center / half_width
+    old = 1.0 / ratio
+    out = [(0.0, 1.0 / center)]
+    for _ in range(count - 1):
+        new = 1.0 / (2.0 * ratio - old)
+        out.append((new * old, 2.0 * new / half_width))
+        old = new
+    return out
+
+
+def smooth(v_pair, d, b, dinv, coeffs, factors, first, last, dup):
+    old, new = v_pair
+    for number, (carry, gain) in enumerate(factors):
+        for p in range(first + number, last):
+            t = (b[p] + couple(old, p, *coeffs, dup)) * dinv[p] - old[p]
+            step = gain * t if carry == 0.0 else carry * d[p] + gain * t
+            if number + 1 < len(factors):
+                d[p] = step
+            new[p] = old[p] + step
+        new[last] = lanes(new[last - 1], 64)
+        old, new = new, old
+    return old
+
+
+def level_coefficients(beta, alpha, first, last, shift, dup, cx, cy, cz, dinv, diag, ends, seam):
+    lane, row = lane_ids(), row_ids()
+    groups = beta[first].shape[0]
+    y_last = (lane % 64) // dup == 64 // dup - 1
+    y_first = (lane % 64) // dup == 0
+    y_rim = jnp.where(y_last | y_first, 0.5, 0.0)
+    rim = [y_rim] * groups
+    rim[0] = rim[0] + jnp.where(row == 0, 0.5, 0.0)
+    rim[-1] = rim[-1] + jnp.where(row == 7, 0.5, 0.0)
+    rim = jnp.stack(rim)
+    face = 0.5 * (beta[first - 1] + beta[first])
+    for p in range(first, last):
+        here = beta[p]
+        by_x = 0.5 * (here + x_up(here))
+        by_x = jnp.concatenate([by_x[:-1], jnp.where(row == 7, 0.0, by_x[-1:])], axis=0)
+        by_y = jnp.where(y_last, 0.0, 0.5 * (here + lanes(here, -dup)))
+        after = beta[p + 1] if p + 1 < last else lanes(here, 64)
+        next_face = 0.5 * (here + after)
+        total = shift * alpha[p] + by_x + x_down(by_x)
+        total = total + (by_y + lanes(by_y, dup)) + here * rim + (face + next_face)
+        cx[p], cy[p] = by_x, by_y
+        cz[p] = face * ends if p == seam else face
+        if diag is not None and p >= seam:
+            diag[p] = total
+        dinv[p] = 1.0 / jnp.where(total > 0.0, total, 1.0)
+        face = next_face
+    cz[last] = face
+
+
+def restrict_pair(first, second, dup):
+    lane = lane_ids()
+    total = first + second
+    groups = total.shape[0]
+    total = jnp.concatenate([total[i : i + 1] + total[i + 1 : i + 2] for i in range(0, groups, 2)], axis=0)
+    return total + jnp.where((lane // dup) % 2 == 0, lanes(total, -dup), lanes(total, dup))
+
+
+def halo_masks():
+    x, y, z = position()
+    chunk = chunk_of(x, y, z)
+    half = lane_ids() // 64
+    return chunk, (half + chunk % 2) == 1
+
+
+def ends_factor():
+    x, y, z = position()
+    slab = 8 * z + chunk_of(x, y, z)
+    half = lane_ids() // 64
+    end = ((half == 0) & (slab == 0)) | ((half == 1) & (slab == 8 * GZ - 1))
+    return jnp.where(end, 0.0, 1.0)
+
+
+def down_kernel(
+    own, even, odd,
+    gather, rim, u0, b0, dinv0, diag0, cx0, cy0, cz0, u1, b1, dinv1, cx1, cy1, cz1,
+    beta_s, alpha_s, b_s, dinv_s, cx_s, cy_s, cz_s, v_a, v_b, d_s,
+    beta1_s, alpha1_s, b1_s, w_a, w_b, e_s,
+):
+    lane = lane_ids()
+    _, from_even = halo_masks()
+    ends = ends_factor()
+
+    def field(a, p):
+        if p >= 16:
+            return own[a, p - 16]
+        if p >= 8:
+            return lanes(jnp.where(from_even, odd[a, 15 - p], even[a, 15 - p]), 64)
+        return jnp.where(from_even, even[a, p], odd[a, p])
+
+    for p in range(PLANES):
+        beta_s[p] = field(2, p)
+        alpha_s[p] = field(1, p)
+    b = Planes(b0, 12, b_s)
+    for p in range(4, PLANES):
+        b[p] = field(0, p)
+    cx, cy, cz = Planes(cx0, 12, cx_s), Planes(cy0, 12, cy_s), Planes(cz0, 12, cz_s)
+    dinv = Planes(dinv0, 12, dinv_s)
+    diag = Planes(diag0, 16)
+    level_coefficients(beta_s, alpha_s, 4, PLANES, SHIFT_BASE, 1, cx, cy, cz, dinv, diag, ends, 16)
+    diag_all = lambda p: diag[p]
+
+    factors = chebyshev_factors(SWEEPS, SMOOTH_LOWER)
+    for p in range(4, PLANES):
+        start = factors[0][1] * (b[p] * dinv[p])
+        v_a[p] = start
+        d_s[p] = start
+    v_a[PLANES] = lanes(v_a[PLANES - 1], 64)
+    v = smooth((v_a, v_b), d_s, b, dinv, (cx, cy, cz), factors[1:], 5, PLANES, 1)
+    for p in range(8):
+        u0[p] = v[16 + p]
+
+    def residual(v, p, b, dinv, coeffs, dup):
+        return ((b[p] + couple(v, p, *coeffs, dup)) * dinv[p] - v[p]) / dinv[p]
+
+    b_one = Planes(b1, 8, b1_s)
+    for p in range(4, PLANES1):
+        pair = [residual(v, 2 * p + i, b, dinv, (cx, cy, cz), 1) for i in range(2)]
+        b_one[p] = 0.5 * restrict_pair(*pair, 1)
+    for p in range(PLANES1):
+        beta1_s[p] = 0.125 * restrict_pair(beta_s[2 * p], beta_s[2 * p + 1], 1)
+        alpha1_s[p] = 0.125 * restrict_pair(alpha_s[2 * p], alpha_s[2 * p + 1], 1)
+    cx, cy, cz, dinv = Planes(cx1, 2), Planes(cy1, 2), Planes(cz1, 2), Planes(dinv1, 2)
+    level_coefficients(beta1_s, alpha1_s, 2, PLANES1, SHIFT_BASE * 4.0, 2, cx, cy, cz, dinv, None, ends, 8)
+    for p in range(4, PLANES1):
+        start = factors[0][1] * (b_one[p] * dinv[p])
+        w_a[p] = start
+        e_s[p] = start
+    w_a[PLANES1] = lanes(w_a[PLANES1 - 1], 64)
+    w = smooth((w_a, w_b), e_s, b_one, dinv, (cx, cy, cz), factors[1:], 5, PLANES1, 2)
+    for p in range(4):
+        u1[p] = w[8 + p]
+        rim[20 + 2 * p : 22 + 2 * p] = jnp.where(lane % 2 == 0, w[8 + p], b_one[8 + p])
+    for p in range(5):
+        rim[4 * p : 4 * p + 4] = u0[p]
+    for p in range(2):
+        pair = [residual(w, 8 + 2 * p + i, b_one, dinv, (cx, cy, cz), 2) for i in range(2)]
+        b_two = 0.5 * restrict_pair(*pair, 2)
+        beta_two = 0.125 * restrict_pair(beta1_s[8 + 2 * p], beta1_s[9 + 2 * p], 2)
+        alpha_two = 0.125 * restrict_pair(alpha1_s[8 + 2 * p], alpha1_s[9 + 2 * p], 2)
+        tile = jnp.where(lane % 4 == 0, b_two, jnp.where(lane % 4 == 1, beta_two, alpha_two))
+        for block in range(GX * GZ):
+            gather[block, p] = tile[0]
+
+
+def shape_of(*dims):
+    return jax.ShapeDtypeStruct(dims + TILE, jnp.float32)
+
+
+def scratch(*dims):
+    return pltpu.VMEM(dims + TILE, jnp.float32)
+
+
+def down(own, even, odd):
+    out_shape = [
+        shape_of(GX * GZ, 2), shape_of(28), shape_of(8, 4),
+        shape_of(12, 4), shape_of(12, 4), shape_of(8, 4), shape_of(12, 4), shape_of(12, 4), shape_of(13, 4),
+        shape_of(4, 2), shape_of(4, 2), shape_of(10, 2), shape_of(10, 2), shape_of(10, 2), shape_of(11, 2),
+    ]
+    vmem = pl.BlockSpec(memory_space=pltpu.VMEM)
+    return pl.pallas_call(
+        down_kernel,
+        out_shape=out_shape,
+        in_specs=[vmem] * 3,
+        out_specs=[vmem] * len(out_shape),
+        scratch_shapes=[
+            scratch(24, 4), scratch(24, 4), scratch(12, 4), scratch(12, 4), scratch(12, 4), scratch(12, 4), scratch(12, 4),
+            scratch(25, 4), scratch(25, 4), scratch(24, 4),
+            scratch(12, 2), scratch(12, 2), scratch(8, 2), scratch(13, 2), scratch(13, 2), scratch(12, 2),
+        ],
+        compiler_params=pltpu.CompilerParams(vmem_limit_bytes=32 * 2**20),
+        name="down_strokes",
+    )(own, even, odd)
+
+
+def outer(value, half):
+    before = jnp.concatenate([lanes(value[-1:], 1), value[:-1]], axis=0)
+    after = jnp.concatenate([value[1:], lanes(value[:1], -1)], axis=0)
+    return jnp.where(half == 0, before, after)
+
+
+def coarse_kernel(
+    mine, other, rim_even, rim_odd, u0, b0, dinv0, diag0, cx0, cy0, cz0, u1, b1, dinv1, cx1, cy1, cz1,
+    out, cores, e2_s, v_a, v_b, d_s, w_a, w_b, e_s, bx_s, uz_s, got,
+):
+    lane, row = lane_ids(), row_ids()
+    half = lane // 64
+    x, y, z = position()
+    cores[y] = mine[...]
+    cores[1 - y] = other[...]
+
+    def collect(f):
+        planes = []
+        for p in range(2):
+            tiles = []
+            for group in range(8):
+                tile = None
+                for q in range(GZ):
+                    natural = 7 - group if q % 2 else group
+                    rank, core = natural // 2, natural % 2
+                    piece = lanes(cores[core, (rank ^ (rank >> 1)) * GZ + q, p], q - f)
+                    tile = piece if tile is None else jnp.where(lane % 4 == q, piece, tile)
+                tiles.append(tile)
+            planes.append(jnp.stack(tiles))
+        return planes
+
+    b_two, beta_two, alpha_two = collect(0), collect(1), collect(2)
+    slab = lax.broadcasted_iota(jnp.int32, (8,) + TILE, 0)
+    end = ((slab == 0) & (lane % 4 == 0) & (half == 0)) | ((slab == 7) & (lane % 4 == 3) & (half == 1))
+
+    def sides(beta, dx, dy):
+        x_last, x_first = row >= 8 - dx, row < dx
+        place = (lane % 64) // dy
+        y_last, y_first = place == 64 // dy - 1, place == 0
+        by_x = jnp.where(x_last, 0.0, 0.5 * (beta + rows(beta, -dx)))
+        by_y = jnp.where(y_last, 0.0, 0.5 * (beta + lanes(beta, -dy)))
+        rim = jnp.where(x_last | x_first, 0.5, 0.0) + jnp.where(y_last | y_first, 0.5, 0.0)
+        return by_x, by_y, (by_x + rows(by_x, dx)) + (by_y + lanes(by_y, dy)) + beta * rim
+
+    def flat(v, by_x, by_y, dx, dy):
+        total = by_x * rows(v, -dx) + rows(by_x * v, dx)
+        return total + (by_y * lanes(v, -dy) + lanes(by_y * v, dy))
+
+    x0, y0, s0 = sides(beta_two[0], 1, 4)
+    x1, y1, s1 = sides(beta_two[1], 1, 4)
+    middle = 0.5 * (beta_two[0] + beta_two[1])
+    inner = 0.5 * (beta_two[1] + lanes(beta_two[1], 64))
+    edge = 0.5 * (beta_two[0] + jnp.where(end, 0.0, outer(lanes(beta_two[0], 64), half)))
+    rim2 = jnp.where(end, 0.0, edge)
+    shift = SHIFT_BASE * 16.0
+    diag_a = shift * alpha_two[0] + s0 + (middle + edge)
+    diag_b = shift * alpha_two[1] + s1 + (middle + inner)
+    inv_a, inv_b = 1.0 / diag_a, 1.0 / diag_b
+
+    def apply_two(va, vb):
+        ta = flat(va, x0, y0, 1, 4) + (middle * vb + rim2 * outer(lanes(va, 64), half))
+        tb = flat(vb, x1, y1, 1, 4) + (middle * va + inner * lanes(vb, 64))
+        return ta, tb
+
+    def sweeps_two(va, vb, da, db, factors):
+        for carry, gain in factors:
+            ta, tb = apply_two(va, vb)
+            ta = (b_two[0] + ta) * inv_a - va
+            tb = (b_two[1] + tb) * inv_b - vb
+            if carry == 0.0:
+                da, db = gain * ta, gain * tb
+            else:
+                da, db = carry * da + gain * ta, carry * db + gain * tb
+            va, vb = va + da, vb + db
+        return va, vb
+
+    factors = chebyshev_factors(SWEEPS, SMOOTH_LOWER)
+    da, db = factors[0][1] * (b_two[0] * inv_a), factors[0][1] * (b_two[1] * inv_b)
+    ua, ub = sweeps_two(da, db, da, db, factors[1:])
+    ta, tb = apply_two(ua, ub)
+
+    def restrict_whole(first, second):
+        total = first + second
+        total = total + jnp.where(row % 2 == 0, rows(total, -1), rows(total, 1))
+        return total + jnp.where((lane // 4) % 2 == 0, lanes(total, -4), lanes(total, 4))
+
+    b_low = 0.5 * restrict_whole(b_two[0] + ta - diag_a * ua, b_two[1] + tb - diag_b * ub)
+    beta_low = 0.125 * restrict_whole(beta_two[0], beta_two[1])
+    alpha_low = 0.125 * restrict_whole(alpha_two[0], alpha_two[1])
+
+    x_low, y_low, s_low = sides(beta_low, 2, 8)
+    turned = lanes(beta_low, 64)
+    inner_low = 0.5 * (beta_low + turned)
+    edge_low = 0.5 * (beta_low + jnp.where(end, 0.0, outer(turned, half)))
+    rim_low = jnp.where(end, 0.0, edge_low)
+    diag_low = SHIFT_BASE * 64.0 * alpha_low + s_low + (inner_low + edge_low)
+    inv_low = 1.0 / diag_low
+    step = None
+    v = None
+    for carry, gain in chebyshev_factors(BOTTOM, BOTTOM_LOWER):
+        if v is None:
+            step = gain * (b_low * inv_low)
+            v = step
+            continue
+        turned = lanes(v, 64)
+        total = flat(v, x_low, y_low, 2, 8) + (inner_low * turned + rim_low * outer(turned, half))
+        step = carry * step + gain * ((b_low + total) * inv_low - v)
+        v = v + step
+    va, vb = sweeps_two(ua + v, ub + v, None, None, factors)
+    for group in range(8):
+        e2_s[group, 0] = va[group]
+        e2_s[group, 1] = vb[group]
+
+    chunk = chunk_of(x, y, z)
+    place = 8 * z + chunk
+
+    def fetch(offset):
+        index = jnp.clip(place + offset, 0, 8 * GZ - 1)
+        out = []
+        for p in range(2):
+            tile = pltpu.roll(e2_s[index % 8, p], (128 - index // 8) % 128, 1)
+            tile = jnp.where(lane % 4 == 0, tile, 0.0)
+            tile = tile + lanes(tile, 1)
+            out.append(tile + lanes(tile, 2))
+        return out
+
+    below, here, above = fetch(-1), fetch(0), fetch(1)
+    first = half == 0
+    e_two = [
+        jnp.where(first, below[0], above[0]),
+        jnp.where(first, below[1], above[1]),
+        lanes(jnp.where(first, above[1], below[1]), 64),
+        lanes(jnp.where(first, above[0], below[0]), 64),
+        here[0],
+        here[1],
+    ]
+    _, from_even = halo_masks()
+
+    for p in range(1, 8):
+        if p >= 4:
+            k = 7 - p
+            both = lanes(jnp.where(from_even, rim_odd[20 + 2 * k : 22 + 2 * k], rim_even[20 + 2 * k : 22 + 2 * k]), 64)
+        else:
+            both = jnp.where(from_even, rim_even[20 + 2 * p : 22 + 2 * p], rim_odd[20 + 2 * p : 22 + 2 * p])
+        w_a[p] = jnp.where(lane % 2 == 0, both, lanes(both, 1)) + e_two[p // 2]
+        if p >= 2:
+            bx_s[p] = jnp.where(lane % 2 == 0, lanes(both, -1), both)
+    for p in range(8, PLANES1):
+        w_a[p] = u1[p - 8] + e_two[p // 2]
+    w_a[PLANES1] = lanes(w_a[PLANES1 - 1], 64)
+    b_one = Planes(b1, 8, bx_s)
+    coeffs = (Planes(cx1, 2), Planes(cy1, 2), Planes(cz1, 2))
+    w = smooth((w_a, w_b), e_s, b_one, Planes(dinv1, 2), coeffs, factors, 2, PLANES1, 2)
+
+    for p in range(11, PLANES):
+        if p >= 16:
+            start = u0[p - 16]
+        else:
+            k = 4 * (15 - p)
+            start = lanes(jnp.where(from_even, rim_odd[k : k + 4], rim_even[k : k + 4]), 64)
+        e_one = w[p // 2]
+        e_one = jnp.concatenate([e_one[:1], e_one[:1], e_one[1:], e_one[1:]], axis=0)
+        v_a[p] = start + e_one
+    v_a[PLANES] = lanes(v_a[PLANES - 1], 64)
+    b = Planes(b0, 12)
+    coeffs = (Planes(cx0, 12), Planes(cy0, 12), Planes(cz0, 12))
+    v = smooth((v_a, v_b), d_s, b, Planes(dinv0, 12), coeffs, factors, 12, PLANES, 1)
+    low = (lane // 32) % 2 == 0
+    for k in range(4):
+        for o in range(2):
+            parts = []
+            for pp in range(2):
+                p = 16 + k + 4 * pp
+                value = v[p] if o == 0 else (b[p] + couple(v, p, *coeffs, 1)) - diag0[p - 16] * v[p]
+                parts.append(regroup([value[i] for i in range(4)], 0, 2, row))
+            for i in range(GX):
+                one, two = parts[0][i], parts[1][i]
+                out[2 * i, pl.ds(o * 32 + k * 8, 8), :] = jnp.where(low, one, lanes(two, 32))
+                out[2 * i + 1, pl.ds(o * 32 + k * 8, 8), :] = jnp.where(low, lanes(one, -32), two)
+
+
+def coarse_and_up(mine, other, rim_even, rim_odd, kept):
+    vmem = pl.BlockSpec(memory_space=pltpu.VMEM)
+    operands = (mine, other, rim_even, rim_odd, *kept)
+    return pl.pallas_call(
+        coarse_kernel,
+        out_shape=jax.ShapeDtypeStruct((8, 64, 128), jnp.float32),
+        in_specs=[vmem] * len(operands),
+        out_specs=vmem,
+        scratch_shapes=[
+            scratch(2, GX * GZ, 2), scratch(8, 2), scratch(25, 4), scratch(25, 4), scratch(24, 4),
+            scratch(13, 2), scratch(13, 2), scratch(12, 2), scratch(8, 2), scratch(1), scratch(1),
+        ],
+        compiler_params=pltpu.CompilerParams(vmem_limit_bytes=32 * 2**20),
+        name="coarse_and_up",
+    )(*operands)
+
+
+def unpack_kernel(in_ref, v_ref, r_ref, turned, staged):
+    z = lax.axis_index("gz")
+    lane = lane_ids()
+    for x in range(GX):
+        for y in range(GY):
+            start = pl.multiple_of(chunk_of(x, y, z) * 64, 64)
+            staged[pl.ds(start, 64), :] = in_ref[x * GY + y]
+    for o, ref in enumerate((v_ref, r_ref)):
+        for xg in range(2):
+            slot = turned.at[2 * o + xg]
+            for k in range(4):
+                tiles = [staged[pl.ds(o * 32 + k * 8 + 2 * x4 + xg, 8, stride=64), :] for x4 in range(4)]
+                for g, tile in enumerate(regroup(tiles, 1, 32, lane)):
+                    slot[pl.ds(depth_of(k, g), 8, stride=16), :] = tile
+            ref[4 * xg : 4 * xg + 4] = slot[...].T.reshape(4, 32, 128)
+
+
+def unpack(received):
+    vmem = pl.BlockSpec(memory_space=pltpu.VMEM)
+    return pl.pallas_call(
+        unpack_kernel,
+        out_shape=[jax.ShapeDtypeStruct(BLOCK, jnp.float32)] * 2,
+        in_specs=[vmem],
+        out_specs=[vmem] * 2,
+        scratch_shapes=[pltpu.VMEM((4, 128, 128), jnp.float32), pltpu.VMEM((512, 128), jnp.float32)],
+        name="unpack",
+    )(received)
+
+
+def slab_shards(right_side, alpha_coef, beta_coef):
+    even_pairs, odd_pairs = swap_pairs(False), swap_pairs(True)
+    packed = pack(right_side, alpha_coef, beta_coef)
+    own = to_slab(lax.all_to_all(packed, RING, 0, 0))
+    even = lax.ppermute(own, ALL, even_pairs)
+    odd = lax.ppermute(own, ALL, odd_pairs)
+    gather, rim, *kept = down(own, even, odd)
+    rim_even = lax.ppermute(rim, ALL, even_pairs)
+    rim_odd = lax.ppermute(rim, ALL, odd_pairs)
+    mine = lax.all_to_all(gather, ("gx", "gz"), 0, 0)
+    other = lax.ppermute(mine, "gy", [(0, 1), (1, 0)])
+    result = coarse_and_up(mine, other, rim_even, rim_odd, kept)
+    return tuple(unpack(lax.all_to_all(result, RING, 0, 0)))
+
+
 def solution(mesh):
-    in_specs = (P("gx", "gy", "gz"), P("gx", "gy", "gz"), P("gx", "gy", "gz"))
-    out_specs = (P("gx", "gy", "gz"), P("gx", "gy", "gz"))
-    return jax.shard_map(shards, mesh=mesh, in_specs=in_specs, out_specs=out_specs, check_vma=False)
+    spec = P("gx", "gy", "gz")
+    plain = jax.shard_map(shards, mesh=mesh, in_specs=(spec,) * 3, out_specs=(spec,) * 2, check_vma=False)
+    slabs = jax.shard_map(slab_shards, mesh=mesh, in_specs=(spec,) * 3, out_specs=(spec,) * 2, check_vma=False)
+    sizes = tuple(mesh.shape[axis] for axis in ALL)
+
+    def run(right_side, alpha_coef, beta_coef):
+        block = tuple(n // size for n, size in zip(right_side.shape, sizes))
+        fits = sizes == (GX, GY, GZ) and block == BLOCK
+        return (slabs if fits else plain)(right_side, alpha_coef, beta_coef)
+
+    return run

time: 692 us -> 68.4 us (0.10); the launches traced: 684 us -> 68 us
  starting transfers between devices: 489 us -> 5.12 us
  waiting for transfers between devices: 131 us -> 2.53 us
  blocking collectives: 0 us -> 43.3 us
  local copies, waits for them, and re-layouts: 37.7 us -> 1 us
  other arithmetic: 23.3 us -> 0 us
  Pallas kernels: 0 us -> 15.3 us
    ppermute x173 -> x5, starting transfers between devices: 489 us -> 5.12 us  [the longest x1 1.97 us: slab_shards(): even = lax.ppermute(own, ALL, even_pairs)]
    ppermute x173 -> x5, waiting for transfers between devices: 131 us -> 2.53 us  [the longest x1 1.56 us: slab_shards(): even = lax.ppermute(own, ALL, even_pairs)]
    all_to_all x0 -> x3, blocking collectives: none -> 43.3 us  [the longest x1 18.3 us: slab_shards(): mine = lax.all_to_all(gather, ('gx', 'gz'), 0, 0)]
    reshape x8 -> x0, local copies, waits for them, and re-layouts: 30.7 us -> none  [the longest x4 30.2 us: restrict_mean(): blocks = field.reshape(first // 2, 2, second // 2, 2, third // 2, 2)]
    pallas_call x0 -> x5, Pallas kernels: none -> 15.3 us  [the longest x1 4.96 us: coarse_and_up(): pl.pallas_call(coarse_kernel, out_shape=jax.ShapeDtypeStruct((8, 64, 128)...]
    reduce_sum x12 -> x0, other arithmetic: 12.9 us -> none  [restrict_mean(): return jnp.sum(blocks, axis=(1, 3, 5)) * 0.125]
  transfers between devices with their start and end apart: 173 -> 5, of which waited for: 92 -> 2; matrix products, arithmetic and copies ran while one was open for 7% -> 0% of each run, Pallas kernels for 0% -> 0%
where the time goes in v1:
time: 68.4 us; the launch traced here: 68 us
  blocking collectives  43.3 us (63%)
  Pallas kernels  15.3 us (22%)
  starting transfers between devices  5.12 us (7%)
  waiting for transfers between devices  2.53 us (4%)
  local copies, waits for them, and re-layouts  1 us (1%)
    all_to_all x1, blocking collectives, slab_shards(): mine = lax.all_to_all(gather, ('gx', 'gz'), 0, 0)  18.3 us
    all_to_all x1, blocking collectives, slab_shards(): own = to_slab(lax.all_to_all(packed, RING, 0, 0))  13.6 us
    all_to_all x1, blocking collectives, slab_shards(): return tuple(unpack(lax.all_to_all(result, RING, 0, 0)))  11.4 us
    pallas_call x1, Pallas kernels, coarse_and_up(): pl.pallas_call(coarse_kernel, out_shape=jax.ShapeDtypeStruct((8, 64, 128)...  4.96 us
    pallas_call x1, Pallas kernels, down(): pl.pallas_call(down_kernel, out_shape=out_shape, in_specs=[vmem] * 3, out...  3.44 us
    pallas_call x1, Pallas kernels, pack(): pl.pallas_call(pack_kernel, out_shape=jax.ShapeDtypeStruct((8, 96, 128),...  2.9 us
    pallas_call x1, Pallas kernels, unpack(): pl.pallas_call(unpack_kernel, out_shape=[jax.ShapeDtypeStruct(BLOCK, jnp....  2.08 us
    ppermute x1, starting transfers between devices, slab_shards(): even = lax.ppermute(own, ALL, even_pairs)  1.97 us
  transfers between devices with their start and end apart: 5, of which 2 were waited for; matrix products, arithmetic and copies ran while one was open for 0% of the time, Pallas kernels for 0%

profile of v1, /device:TPU:0, one launch (start us, length us, event | category | flops | bytes accessed | tf_op | source)
XLA Modules:
  0.0 68.0 jit_solution(10525915796321684082)
XLA Ops:
  0.6 2.9 %pack.1 = f32[8,96,128]{2,1,0:T(8,128)} custom-call(f32[8,32,128]{2,1,0:T(8,128)} %b_ref.1, f32[8,32,128]{2,1,0:T(8,128)} %alpha_ref.1, f32[8,32,128]{2,1,0:T(8,128)} %beta_ref.1), custom_call_target="tpu_custom_call" | custom-call | tf_op jit(solution)/shard_map/pack/pallas_call | solution.py:266
  3.5 13.6 %all_to_all.15.in_ref = f32[8,96,128]{2,1,0:T(8,128)} all-to-all(f32[8,96,128]{2,1,0:T(8,128)} %pack.1), channel_id=1, replica_groups=mesh['gx'=4,'gy'=2,'gz'=4] {'gx','gy'}, dimensions={0} | all-to-all | bytes 786432 | tf_op jit(solution)/shard_map/all_to_all | solution.py:742
  17.1 1.9 %to_slab.1.own = f32[3,8,4,8,128]{4,3,2,1,0:T(8,128)} custom-call(f32[8,96,128]{2,1,0:T(8,128)} %all_to_all.15.in_ref), custom_call_target="tpu_custom_call" | custom-call | tf_op jit(solution)/shard_map/to_slab/pallas_call | solution.py:293
  19.1 0.7 collective-permute-start.1
  19.7 2.0 %collective-permute-start = (f32[3,8,4,8,128]{4,3,2,1,0:T(8,128)}, f32[3,8,4,8,128]{4,3,2,1,0:T(8,128)S(1)}, u32[]{:S(2)}, u32[]{:S(2)}) collective-permute-start(f32[3,8,4,8,128]{4,3,2,1,0:T(8,128)} %to_slab.1.own), channel_id=1, source_target_pairs={{0,4},{8,12},{24,28},{16,20},{21,17},{29,25},{13,9},{5,1},{2,6},{1... | collective-permute-start | bytes 1179656 | tf_op jit(solution)/shard_map/ppermute | solution.py:743
  21.7 0.0 collective-permute-done.1.odd
  21.7 1.6 %collective-permute-done.even = f32[3,8,4,8,128]{4,3,2,1,0:T(8,128)S(1)} collective-permute-done((f32[3,8,4,8,128]{4,3,2,1,0:T(8,128)}, f32[3,8,4,8,128]{4,3,2,1,0:T(8,128)S(1)}, u32[]{:S(2)}, u32[]{:S(2)}) %collective-permute-start) | collective-permute-done | bytes 393248 | tf_op jit(solution)/shard_map/ppermute | solution.py:743
  23.3 0.0 copy-start
  23.3 1.0 %copy-done = f32[3,8,4,8,128]{4,3,2,1,0:T(8,128)S(1)} copy-done((f32[3,8,4,8,128]{4,3,2,1,0:T(8,128)S(1)}, f32[3,8,4,8,128]{4,3,2,1,0:T(8,128)}, u32[]{:S(2)}) %copy-start) | copy-done | bytes 393240
  24.3 3.4 %down_strokes.1 = (f32[16,2,8,128]{3,2,1,0:T(8,128)S(1)}, f32[28,8,128]{2,1,0:T(8,128)S(1)}, f32[8,4,8,128]{3,2,1,0:T(8,128)S(1)}, f32[12,4,8,128]{3,2,1,0:T(8,1...) custom-call(f32[3,8,4,8,128]{4,3,2,1,0:T(8,128)S(1)} %copy-done, ...), custom_call_target="tpu_custom_call" | custom-call | tf_op jit(solution)/shard_map/down_strokes/pallas_call | solution.py:497
  27.7 18.3 %all_to_all.16.mine = f32[16,2,8,128]{3,2,1,0:T(8,128)S(1)} all-to-all(f32[16,2,8,128]{3,2,1,0:T(8,128)S(1)} %get-tuple-element.17), channel_id=1, replica_groups=mesh['gx'=4,'gy'=2,'gz'=4] {'gx','gz'}, dimensions={0} | all-to-all | bytes 262144 | tf_op jit(solution)/shard_map/all_to_all | solution.py:748
  46.0 0.0 collective-permute-start.2
  46.0 0.7 collective-permute-start.4
  46.7 1.8 %collective-permute-start.3 = (f32[28,8,128]{2,1,0:T(8,128)S(1)}, f32[28,8,128]{2,1,0:T(8,128)S(1)}, u32[]{:S(2)}, u32[]{:S(2)}) collective-permute-start(f32[28,8,128]{2,1,0:T(8,128)S(1)} %get-tuple-element.18), channel_id=1, source_target_pairs={{0,4},{8,12},{24,28},{16,20},{21,17},{29,25},{13,9},{5,1},{2,6},{1... | collective-permute-start | bytes 344072 | tf_op jit(solution)/shard_map/ppermute | solution.py:746
  48.5 0.0 collective-permute-done.4.rim_odd
  48.5 1.0 %collective-permute-done.3.rim_even = f32[28,8,128]{2,1,0:T(8,128)S(1)} collective-permute-done((f32[28,8,128]{2,1,0:T(8,128)S(1)}, f32[28,8,128]{2,1,0:T(8,128)S(1)}, u32[]{:S(2)}, u32[]{:S(2)}) %collective-permute-start.3) | collective-permute-done | bytes 114720 | tf_op jit(solution)/shard_map/ppermute | solution.py:746
  49.5 0.0 collective-permute-done.2.other
  49.5 5.0 %coarse_and_up.1 = f32[8,64,128]{2,1,0:T(8,128)S(1)} custom-call(f32[16,2,8,128]{3,2,1,0:T(8,128)S(1)} %all_to_all.16.mine, f32[16,2,8,128]{3,2,1,0:T(8,128)S(1)} %collective-permute-done.2.other, f32[28,8,128]{2,1,0:T(8,128)S(1)} %collective-permute-done.3.rim_even, f32[28,8,128]{2,1,0:T(8,128)S(1)} %collective-permute-done.4.rim_odd, ...), custom_call_target="tpu_custom_call" | custom-call | tf_op jit(solution)/shard_map/coarse_and_up/pallas_call | solution.py:696
  54.4 11.4 %all_to_all.17.in_ref = f32[8,64,128]{2,1,0:T(8,128)} all-to-all(f32[8,64,128]{2,1,0:T(8,128)S(1)} %coarse_and_up.1), channel_id=1, replica_groups=mesh['gx'=4,'gy'=2,'gz'=4] {'gx','gy'}, dimensions={0} | all-to-all | bytes 524288 | tf_op jit(solution)/shard_map/all_to_all | solution.py:751
  65.9 2.1 %unpack.1 = (f32[8,32,128]{2,1,0:T(8,128)}, f32[8,32,128]{2,1,0:T(8,128)}) custom-call(f32[8,64,128]{2,1,0:T(8,128)} %all_to_all.17.in_ref), custom_call_target="tpu_custom_call" | custom-call | tf_op jit(solution)/shard_map/unpack/pallas_call | solution.py:729
Async XLA Ops:
  19.1 2.6 %collective-permute-start.1 = (f32[3,8,4,8,128]{4,3,2,1,0:T(8,128)}, f32[3,8,4,8,128]{4,3,2,1,0:T(8,128)S(1)}, u32[]{:S(2)}, u32[]{:S(2)}) collective-permute-start(f32[3,8,4,8,128]{4,3,2,1,0:T(8,128)} %to_slab.1.own), channel_id=1, source_target_pairs={{4,8},{12,24},{28,16},{20,21},{17,29},{25,13},{9,5},{1,2},{6,10},{... | collective-permute-start | bytes 1179656 | tf_op jit(solution)/shard_map/ppermute | solution.py:744
  19.7 3.5 %collective-permute-start = (f32[3,8,4,8,128]{4,3,2,1,0:T(8,128)}, f32[3,8,4,8,128]{4,3,2,1,0:T(8,128)S(1)}, u32[]{:S(2)}, u32[]{:S(2)}) collective-permute-start(f32[3,8,4,8,128]{4,3,2,1,0:T(8,128)} %to_slab.1.own), channel_id=1, source_target_pairs={{0,4},{8,12},{24,28},{16,20},{21,17},{29,25},{13,9},{5,1},{2,6},{1... | collective-permute-start | bytes 1179656 | tf_op jit(solution)/shard_map/ppermute | solution.py:743
  23.3 1.0 %copy-start = (f32[3,8,4,8,128]{4,3,2,1,0:T(8,128)S(1)}, f32[3,8,4,8,128]{4,3,2,1,0:T(8,128)}, u32[]{:S(2)}) copy-start(f32[3,8,4,8,128]{4,3,2,1,0:T(8,128)} %to_slab.1.own) | copy-start | bytes 1179652
  46.0 3.5 %collective-permute-start.2 = (f32[16,2,8,128]{3,2,1,0:T(8,128)S(1)}, f32[16,2,8,128]{3,2,1,0:T(8,128)S(1)}, u32[]{:S(2)}, u32[]{:S(2)}) collective-permute-start(f32[16,2,8,128]{3,2,1,0:T(8,128)S(1)} %all_to_all.16.mine), channel_id=1, source_target_pairs={{0,4},{4,0},{1,5},{5,1},{2,6},{6,2},{3,7},{7,3},{8,12},{12,8},{9,1... | collective-permute-start | bytes 393224 | tf_op jit(solution)/shard_map/ppermute | solution.py:749
  46.0 2.5 %collective-permute-start.4 = (f32[28,8,128]{2,1,0:T(8,128)S(1)}, f32[28,8,128]{2,1,0:T(8,128)S(1)}, u32[]{:S(2)}, u32[]{:S(2)}) collective-permute-start(f32[28,8,128]{2,1,0:T(8,128)S(1)} %get-tuple-element.18), channel_id=1, source_target_pairs={{4,8},{12,24},{28,16},{20,21},{17,29},{25,13},{9,5},{1,2},{6,10},{... | collective-permute-start | bytes 344072 | tf_op jit(solution)/shard_map/ppermute | solution.py:747
  46.7 2.8 %collective-permute-start.3 = (f32[28,8,128]{2,1,0:T(8,128)S(1)}, f32[28,8,128]{2,1,0:T(8,128)S(1)}, u32[]{:S(2)}, u32[]{:S(2)}) collective-permute-start(f32[28,8,128]{2,1,0:T(8,128)S(1)} %get-tuple-element.18), channel_id=1, source_target_pairs={{0,4},{8,12},{24,28},{16,20},{21,17},{29,25},{13,9},{5,1},{2,6},{1... | collective-permute-start | bytes 344072 | tf_op jit(solution)/shard_map/ppermute | solution.py:746

commit v2 on v1

--- a/solution.py
+++ b/solution.py
@@ -245,13 +245,13 @@
     return 15 - plane if half else plane
 
 
-def pack_kernel(b_ref, alpha_ref, beta_ref, out_ref, turned, staged):
+def pack_kernel(fields, out_ref, turned, staged):
     z = lax.axis_index("gz")
     lane = lane_ids()
-    for a, ref in enumerate((b_ref, alpha_ref, beta_ref)):
+    for a in range(3):
         for xg in range(2):
             slot = turned.at[2 * a + xg]
-            slot[...] = ref[4 * xg : 4 * xg + 4].reshape(128, 128).T
+            slot[...] = fields[a, 4 * xg : 4 * xg + 4].reshape(128, 128).T
             for k in range(4):
                 tiles = [slot[pl.ds(depth_of(k, g), 8, stride=16), :] for g in range(4)]
                 for x4, tile in enumerate(regroup(tiles, 1, 32, lane)):
@@ -262,15 +262,16 @@
             out_ref[x * GY + y] = staged[pl.ds(start, 96), :]
 
 
-def pack(b, alpha, beta):
+def pack(fields):
     return pl.pallas_call(
         pack_kernel,
         out_shape=jax.ShapeDtypeStruct((8, 96, 128), jnp.float32),
-        in_specs=[pl.BlockSpec(memory_space=pltpu.VMEM)] * 3,
+        in_specs=[pl.BlockSpec(memory_space=pltpu.VMEM)],
         out_specs=pl.BlockSpec(memory_space=pltpu.VMEM),
         scratch_shapes=[pltpu.VMEM((6, 128, 128), jnp.float32), pltpu.VMEM((768, 128), jnp.float32)],
+        compiler_params=pltpu.CompilerParams(vmem_limit_bytes=4 * 2**20),
         name="pack",
-    )(b, alpha, beta)
+    )(fields)
 
 
 def slab_kernel(in_ref, out_ref):
@@ -295,6 +296,7 @@
         out_shape=jax.ShapeDtypeStruct((3, 8, 4) + TILE, jnp.float32),
         in_specs=[pl.BlockSpec(memory_space=pltpu.VMEM)],
         out_specs=pl.BlockSpec(memory_space=pltpu.VMEM),
+        compiler_params=pltpu.CompilerParams(vmem_limit_bytes=4 * 2**20),
         name="to_slab",
     )(received)
 
@@ -489,7 +491,7 @@
 
 def down(own, even, odd):
     out_shape = [
-        shape_of(GX * GZ, 2), shape_of(28), shape_of(8, 4),
+        shape_of(GX * GZ, 2), shape_of(36), shape_of(8, 4),
         shape_of(12, 4), shape_of(12, 4), shape_of(8, 4), shape_of(12, 4), shape_of(12, 4), shape_of(13, 4),
         shape_of(4, 2), shape_of(4, 2), shape_of(10, 2), shape_of(10, 2), shape_of(10, 2), shape_of(11, 2),
     ]
@@ -504,7 +506,7 @@
             scratch(25, 4), scratch(25, 4), scratch(24, 4),
             scratch(12, 2), scratch(12, 2), scratch(8, 2), scratch(13, 2), scratch(13, 2), scratch(12, 2),
         ],
-        compiler_params=pltpu.CompilerParams(vmem_limit_bytes=32 * 2**20),
+        compiler_params=pltpu.CompilerParams(vmem_limit_bytes=16 * 2**20),
         name="down_strokes",
     )(own, even, odd)
 
@@ -702,26 +704,30 @@
             scratch(2, GX * GZ, 2), scratch(8, 2), scratch(25, 4), scratch(25, 4), scratch(24, 4),
             scratch(13, 2), scratch(13, 2), scratch(12, 2), scratch(8, 2), scratch(1), scratch(1),
         ],
-        compiler_params=pltpu.CompilerParams(vmem_limit_bytes=32 * 2**20),
+        compiler_params=pltpu.CompilerParams(vmem_limit_bytes=16 * 2**20),
         name="coarse_and_up",
     )(*operands)
 
 
-def unpack_kernel(in_ref, v_ref, r_ref, turned, staged):
+def unpack_kernel(in_ref, v_ref, r_ref, fields, turned, staged, left):
     z = lax.axis_index("gz")
     lane = lane_ids()
     for x in range(GX):
         for y in range(GY):
             start = pl.multiple_of(chunk_of(x, y, z) * 64, 64)
             staged[pl.ds(start, 64), :] = in_ref[x * GY + y]
-    for o, ref in enumerate((v_ref, r_ref)):
+    copies = [pltpu.make_async_copy(fields.at[o], ref, left.at[o]) for o, ref in enumerate((v_ref, r_ref))]
+    for o, copy in enumerate(copies):
         for xg in range(2):
             slot = turned.at[2 * o + xg]
             for k in range(4):
                 tiles = [staged[pl.ds(o * 32 + k * 8 + 2 * x4 + xg, 8, stride=64), :] for x4 in range(4)]
                 for g, tile in enumerate(regroup(tiles, 1, 32, lane)):
                     slot[pl.ds(depth_of(k, g), 8, stride=16), :] = tile
-            ref[4 * xg : 4 * xg + 4] = slot[...].T.reshape(4, 32, 128)
+            fields[o, 4 * xg : 4 * xg + 4] = slot[...].T.reshape(4, 32, 128)
+        copy.start()
+    for copy in copies:
+        copy.wait()
 
 
 def unpack(received):
@@ -730,15 +736,21 @@
         unpack_kernel,
         out_shape=[jax.ShapeDtypeStruct(BLOCK, jnp.float32)] * 2,
         in_specs=[vmem],
-        out_specs=[vmem] * 2,
-        scratch_shapes=[pltpu.VMEM((4, 128, 128), jnp.float32), pltpu.VMEM((512, 128), jnp.float32)],
+        out_specs=[pl.BlockSpec(memory_space=pltpu.HBM)] * 2,
+        scratch_shapes=[
+            pltpu.VMEM((2,) + BLOCK, jnp.float32),
+            pltpu.VMEM((4, 128, 128), jnp.float32),
+            pltpu.VMEM((512, 128), jnp.float32),
+            pltpu.SemaphoreType.DMA((2,)),
+        ],
+        compiler_params=pltpu.CompilerParams(vmem_limit_bytes=4 * 2**20),
         name="unpack",
     )(received)
 
 
 def slab_shards(right_side, alpha_coef, beta_coef):
     even_pairs, odd_pairs = swap_pairs(False), swap_pairs(True)
-    packed = pack(right_side, alpha_coef, beta_coef)
+    packed = pack(jnp.stack([right_side, alpha_coef, beta_coef]))
     own = to_slab(lax.all_to_all(packed, RING, 0, 0))
     even = lax.ppermute(own, ALL, even_pairs)
     odd = lax.ppermute(own, ALL, odd_pairs)

time: 68.4 us -> 59.8 us (0.87)
  blocking collectives: 43.3 us -> 22.7 us
  starting transfers between devices: 5.12 us -> 16.8 us
  waiting for transfers between devices: 2.53 us -> 6.83 us
  Pallas kernels: 15.3 us -> 11.5 us
  other arithmetic: 0 us -> 1.06 us
  local copies, waits for them, and re-layouts: 1 us -> 0 us
    all_to_all x1 -> x0, blocking collectives: 18.3 us -> none  [slab_shards(): mine = lax.all_to_all(gather, ('gx', 'gz'), 0, 0)]
    all_to_all x0 -> x1, starting transfers between devices: none -> 10.1 us  [slab_shards(): mine = lax.all_to_all(gather, ('gx', 'gz'), 0, 0)]
    all_to_all x0 -> x1, waiting for transfers between devices: none -> 4.14 us  [slab_shards(): mine = lax.all_to_all(gather, ('gx', 'gz'), 0, 0)]
    all_to_all x1, blocking collectives: 11.4 us -> 9.35 us  [slab_shards(): return tuple(unpack(lax.all_to_all(result, RING, 0, 0)))]
    pallas_call x1, Pallas kernels: 2.9 us -> 1.1 us  [pack(): pl.pallas_call(pack_kernel, out_shape=jax.ShapeDtypeStruct((8, 96, 128),...]
    pallas_call x1, Pallas kernels: 1.93 us -> 0.17 us  [to_slab(): pl.pallas_call(slab_kernel, out_shape=jax.ShapeDtypeStruct((3, 8, 4) + TI...]
    ppermute x1, starting transfers between devices: 1.82 us -> 3.33 us  [slab_shards(): rim_even = lax.ppermute(rim, ALL, even_pairs)]
    ppermute x1, waiting for transfers between devices: 0.01 us -> 1.34 us  [slab_shards(): other = lax.ppermute(mine, 'gy', [(0, 1), (1, 0)])]
  transfers between devices with their start and end apart: 5 -> 6, of which waited for: 2 -> 3; matrix products, arithmetic and copies ran while one was open for 0% -> 0% of each run, Pallas kernels for 0% -> 0%
where the time goes in v2:
time: 59.8 us; the launch traced here: 59.4 us
  blocking collectives  22.7 us (38%)
  starting transfers between devices  16.8 us (28%)
  Pallas kernels  11.5 us (19%)
  waiting for transfers between devices  6.83 us (11%)
  other arithmetic  1.06 us (2%)
  between operations  0.69 us (1%)
    all_to_all x1, blocking collectives, slab_shards(): own = to_slab(lax.all_to_all(packed, RING, 0, 0))  13.3 us
    all_to_all x1, starting transfers between devices, slab_shards(): mine = lax.all_to_all(gather, ('gx', 'gz'), 0, 0)  10.1 us
    all_to_all x1, blocking collectives, slab_shards(): return tuple(unpack(lax.all_to_all(result, RING, 0, 0)))  9.35 us
    pallas_call x1, Pallas kernels, coarse_and_up(): pl.pallas_call(coarse_kernel, out_shape=jax.ShapeDtypeStruct((8, 64, 128)...  4.97 us
    all_to_all x1, waiting for transfers between devices, slab_shards(): mine = lax.all_to_all(gather, ('gx', 'gz'), 0, 0)  4.14 us
    pallas_call x1, Pallas kernels, down(): pl.pallas_call(down_kernel, out_shape=out_shape, in_specs=[vmem] * 3, out...  4.08 us
    ppermute x1, starting transfers between devices, slab_shards(): rim_even = lax.ppermute(rim, ALL, even_pairs)  3.33 us
    ppermute x1, starting transfers between devices, slab_shards(): even = lax.ppermute(own, ALL, even_pairs)  1.97 us
  transfers between devices with their start and end apart: 6, of which 3 were waited for; matrix products, arithmetic and copies ran while one was open for 0% of the time, Pallas kernels for 0%

profile of v2, /device:TPU:0, one launch (start us, length us, event | category | flops | bytes accessed | tf_op | source)
XLA Modules:
  0.0 59.4 jit_solution(10157070190377360316)
XLA Ops:
  0.6 1.1 %pad_maximum_fusion.fields = f32[3,8,32,128]{3,2,1,0:T(8,128)S(1)} fusion(f32[1,8,32,128]{3,2,1,0:T(8,128)} %bitcast.3, f32[1,8,32,128]{3,2,1,0:T(8,128)} %bitcast.4, f32[1,8,32,128]{3,2,1,0:T(8,128)} %bitcast.5), kind=kLoop, calls=%fused_computation | loop fusion | flops 196608 | bytes 786432 | tf_op jit(solution)/shard_map/stack | solution.py:753
  1.7 1.1 %pack.1 = f32[8,96,128]{2,1,0:T(8,128)S(1)} custom-call(f32[3,8,32,128]{3,2,1,0:T(8,128)S(1)} %pad_maximum_fusion.fields), custom_call_target="tpu_custom_call" | custom-call | tf_op jit(solution)/shard_map/pack/pallas_call | solution.py:266
  2.8 13.3 %all_to_all.15.in_ref = f32[8,96,128]{2,1,0:T(8,128)S(1)} all-to-all(f32[8,96,128]{2,1,0:T(8,128)S(1)} %pack.1), channel_id=1, replica_groups=mesh['gx'=4,'gy'=2,'gz'=4] {'gx','gy'}, dimensions={0} | all-to-all | bytes 786432 | tf_op jit(solution)/shard_map/all_to_all | solution.py:754
  16.1 0.2 to_slab.1.own
  16.3 0.7 %collective-permute-start.1 = (f32[3,8,4,8,128]{4,3,2,1,0:T(8,128)S(1)}, f32[3,8,4,8,128]{4,3,2,1,0:T(8,128)S(1)}, u32[]{:S(2)}, u32[]{:S(2)}) collective-permute-start(f32[3,8,4,8,128]{4,3,2,1,0:T(8,128)S(1)} %to_slab.1.own), channel_id=1, source_target_pairs={{4,8},{12,24},{28,16},{20,21},{17,29},{25,13},{9,5},{1,2},{6,10},{... | collective-permute-start | bytes 1179656 | tf_op jit(solution)/shard_map/ppermute | solution.py:756
  17.0 2.0 %collective-permute-start = (f32[3,8,4,8,128]{4,3,2,1,0:T(8,128)S(1)}, f32[3,8,4,8,128]{4,3,2,1,0:T(8,128)S(1)}, u32[]{:S(2)}, u32[]{:S(2)}) collective-permute-start(f32[3,8,4,8,128]{4,3,2,1,0:T(8,128)S(1)} %to_slab.1.own), channel_id=1, source_target_pairs={{0,4},{8,12},{24,28},{16,20},{21,17},{29,25},{13,9},{5,1},{2,6},{1... | collective-permute-start | bytes 1179656 | tf_op jit(solution)/shard_map/ppermute | solution.py:755
  18.9 0.0 collective-permute-done.1.odd
  18.9 1.3 %collective-permute-done.even = f32[3,8,4,8,128]{4,3,2,1,0:T(8,128)S(1)} collective-permute-done((f32[3,8,4,8,128]{4,3,2,1,0:T(8,128)S(1)}, f32[3,8,4,8,128]{4,3,2,1,0:T(8,128)S(1)}, u32[]{:S(2)}, u32[]{:S(2)}) %collective-permute-start) | collective-permute-done | bytes 393248 | tf_op jit(solution)/shard_map/ppermute | solution.py:755
  20.3 4.1 %down_strokes.1 = (f32[16,2,8,128]{3,2,1,0:T(8,128)}, f32[36,8,128]{2,1,0:T(8,128)S(1)}, f32[8,4,8,128]{3,2,1,0:T(8,128)S(1)}, f32[12,4,8,128]{3,2,1,0:T(8,128)S...) custom-call(f32[3,8,4,8,128]{4,3,2,1,0:T(8,128)S(1)} %to_slab.1.own,, ...), custom_call_target="tpu_custom_call" | custom-call | tf_op jit(solution)/shard_map/down_strokes/pallas_call | solution.py:499
  24.4 10.1 %all-to-all-start.1 = ((f32[16,2,8,128]{3,2,1,0:T(8,128)}), f32[16,2,8,128]{3,2,1,0:T(8,128)S(1)}, u32[]{:S(2)}, u32[]{:S(2)}) async-start(f32[16,2,8,128]{3,2,1,0:T(8,128)} %get-tuple-element.17), calls=%async_computation.1 | async-start | bytes 262144 | tf_op jit(solution)/shard_map/all_to_all | solution.py:760
  34.5 0.7 %collective-permute-start.4 = (f32[36,8,128]{2,1,0:T(8,128)S(1)}, f32[36,8,128]{2,1,0:T(8,128)S(1)}, u32[]{:S(2)}, u32[]{:S(2)}) collective-permute-start(f32[36,8,128]{2,1,0:T(8,128)S(1)} %get-tuple-element.18), channel_id=1, source_target_pairs={{4,8},{12,24},{28,16},{20,21},{17,29},{25,13},{9,5},{1,2},{6,10},{... | collective-permute-start | bytes 442376 | tf_op jit(solution)/shard_map/ppermute | solution.py:759
  35.2 3.3 %collective-permute-start.3 = (f32[36,8,128]{2,1,0:T(8,128)S(1)}, f32[36,8,128]{2,1,0:T(8,128)S(1)}, u32[]{:S(2)}, u32[]{:S(2)}) collective-permute-start(f32[36,8,128]{2,1,0:T(8,128)S(1)} %get-tuple-element.18), channel_id=1, source_target_pairs={{0,4},{8,12},{24,28},{16,20},{21,17},{29,25},{13,9},{5,1},{2,6},{1... | collective-permute-start | bytes 442376 | tf_op jit(solution)/shard_map/ppermute | solution.py:758
  38.5 4.1 %all-to-all-done.1.mine = f32[16,2,8,128]{3,2,1,0:T(8,128)S(1)} async-done(((f32[16,2,8,128]{3,2,1,0:T(8,128)}), f32[16,2,8,128]{3,2,1,0:T(8,128)S(1)}, u32[]{:S(2)}, u32[]{:S(2)}) %all-to-all-start.1) | async-done | bytes 131104 | tf_op jit(solution)/shard_map/all_to_all | solution.py:760
  42.6 0.0 collective-permute-start.2
  42.6 0.0 collective-permute-done.4.rim_odd
  42.6 0.0 collective-permute-done.3.rim_even
  42.6 1.3 %collective-permute-done.2.other = f32[16,2,8,128]{3,2,1,0:T(8,128)S(1)} collective-permute-done((f32[16,2,8,128]{3,2,1,0:T(8,128)S(1)}, f32[16,2,8,128]{3,2,1,0:T(8,128)S(1)}, u32[]{:S(2)}, u32[]{:S(2)}) %collective-permute-start.2) | collective-permute-done | bytes 131104 | tf_op jit(solution)/shard_map/ppermute | solution.py:761
  44.0 5.0 %coarse_and_up.1 = f32[8,64,128]{2,1,0:T(8,128)S(1)} custom-call(f32[16,2,8,128]{3,2,1,0:T(8,128)S(1)} %all-to-all-done.1.mine, f32[16,2,8,128]{3,2,1,0:T(8,128)S(1)} %collective-permute-done.2.other, f32[36,8,128]{2,1,0:T(8,128)S(1)} %collective-permute-done.3.rim_even, f32[36,8,128]{2,1,0:T(8,128)S(1)} %collective-permute-done.4.rim_odd, ...), custom_call_target="tpu_custom_call" | custom-call | tf_op jit(solution)/shard_map/coarse_and_up/pallas_call | solution.py:698
  49.0 9.3 %all_to_all.16.in_ref = f32[8,64,128]{2,1,0:T(8,128)S(1)} all-to-all(f32[8,64,128]{2,1,0:T(8,128)S(1)} %coarse_and_up.1), channel_id=1, replica_groups=mesh['gx'=4,'gy'=2,'gz'=4] {'gx','gy'}, dimensions={0} | all-to-all | bytes 524288 | tf_op jit(solution)/shard_map/all_to_all | solution.py:763
  58.3 1.1 %unpack.1 = (f32[8,32,128]{2,1,0:T(8,128)}, f32[8,32,128]{2,1,0:T(8,128)}) custom-call(f32[8,64,128]{2,1,0:T(8,128)S(1)} %all_to_all.16.in_ref), custom_call_target="tpu_custom_call" | custom-call | tf_op jit(solution)/shard_map/unpack/pallas_call | solution.py:735
Async XLA Ops:
  16.3 2.7 %collective-permute-start.1 = (f32[3,8,4,8,128]{4,3,2,1,0:T(8,128)S(1)}, f32[3,8,4,8,128]{4,3,2,1,0:T(8,128)S(1)}, u32[]{:S(2)}, u32[]{:S(2)}) collective-permute-start(f32[3,8,4,8,128]{4,3,2,1,0:T(8,128)S(1)} %to_slab.1.own), channel_id=1, source_target_pairs={{4,8},{12,24},{28,16},{20,21},{17,29},{25,13},{9,5},{1,2},{6,10},{... | collective-permute-start | bytes 1179656 | tf_op jit(solution)/shard_map/ppermute | solution.py:756
  17.0 3.3 %collective-permute-start = (f32[3,8,4,8,128]{4,3,2,1,0:T(8,128)S(1)}, f32[3,8,4,8,128]{4,3,2,1,0:T(8,128)S(1)}, u32[]{:S(2)}, u32[]{:S(2)}) collective-permute-start(f32[3,8,4,8,128]{4,3,2,1,0:T(8,128)S(1)} %to_slab.1.own), channel_id=1, source_target_pairs={{0,4},{8,12},{24,28},{16,20},{21,17},{29,25},{13,9},{5,1},{2,6},{1... | collective-permute-start | bytes 1179656 | tf_op jit(solution)/shard_map/ppermute | solution.py:755
  24.4 18.3 %all-to-all-start.1 = ((f32[16,2,8,128]{3,2,1,0:T(8,128)}), f32[16,2,8,128]{3,2,1,0:T(8,128)S(1)}, u32[]{:S(2)}, u32[]{:S(2)}) async-start(f32[16,2,8,128]{3,2,1,0:T(8,128)} %get-tuple-element.17), calls=%async_computation.1 | async-start | bytes 262144 | tf_op jit(solution)/shard_map/all_to_all | solution.py:760
  34.5 8.2 %collective-permute-start.4 = (f32[36,8,128]{2,1,0:T(8,128)S(1)}, f32[36,8,128]{2,1,0:T(8,128)S(1)}, u32[]{:S(2)}, u32[]{:S(2)}) collective-permute-start(f32[36,8,128]{2,1,0:T(8,128)S(1)} %get-tuple-element.18), channel_id=1, source_target_pairs={{4,8},{12,24},{28,16},{20,21},{17,29},{25,13},{9,5},{1,2},{6,10},{... | collective-permute-start | bytes 442376 | tf_op jit(solution)/shard_map/ppermute | solution.py:759
  35.2 7.5 %collective-permute-start.3 = (f32[36,8,128]{2,1,0:T(8,128)S(1)}, f32[36,8,128]{2,1,0:T(8,128)S(1)}, u32[]{:S(2)}, u32[]{:S(2)}) collective-permute-start(f32[36,8,128]{2,1,0:T(8,128)S(1)} %get-tuple-element.18), channel_id=1, source_target_pairs={{0,4},{8,12},{24,28},{16,20},{21,17},{29,25},{13,9},{5,1},{2,6},{1... | collective-permute-start | bytes 442376 | tf_op jit(solution)/shard_map/ppermute | solution.py:758
  42.6 1.3 %collective-permute-start.2 = (f32[16,2,8,128]{3,2,1,0:T(8,128)S(1)}, f32[16,2,8,128]{3,2,1,0:T(8,128)S(1)}, u32[]{:S(2)}, u32[]{:S(2)}) collective-permute-start(f32[16,2,8,128]{3,2,1,0:T(8,128)S(1)} %all-to-all-done.1.mine), channel_id=1, source_target_pairs={{0,4},{4,0},{1,5},{5,1},{2,6},{6,2},{3,7},{7,3},{8,12},{12,8},{9,1... | collective-permute-start | bytes 393224 | tf_op jit(solution)/shard_map/ppermute | solution.py:761

commit v3 on v2

--- a/solution.py
+++ b/solution.py
@@ -186,6 +186,7 @@
 TILE = (8, 128)
 PLANES = 24
 PLANES1 = 12
+SPAN, SPAN1, COEF_SPAN, COEF_SPAN1 = 2, 4, 2, 4
 
 
 def chunk_of(x, y, z):
@@ -293,7 +294,7 @@
 def to_slab(received):
     return pl.pallas_call(
         slab_kernel,
-        out_shape=jax.ShapeDtypeStruct((3, 8, 4) + TILE, jnp.float32),
+        out_shape=shape_of(3, 8, 4),
         in_specs=[pl.BlockSpec(memory_space=pltpu.VMEM)],
         out_specs=pl.BlockSpec(memory_space=pltpu.VMEM),
         compiler_params=pltpu.CompilerParams(vmem_limit_bytes=4 * 2**20),
@@ -302,32 +303,41 @@
 
 
 class Planes:
-    def __init__(self, upper, cut, lower=None, base=0):
-        self.upper, self.cut, self.lower, self.base = upper, cut, lower, base
-
-    def __getitem__(self, p):
-        return self.upper[p - self.cut] if p >= self.cut else self.lower[p - self.base]
-
-    def __setitem__(self, p, value):
-        if p >= self.cut:
-            self.upper[p - self.cut] = value
-        else:
-            self.lower[p - self.base] = value
+    def __init__(self, *segments):
+        self.segments = [(first, first + ref.shape[0], ref) for first, ref in segments]
+
+    def find(self, p, q):
+        for first, last, ref in self.segments:
+            low, high = max(p, first), min(q, last)
+            if low < high:
+                yield low, high, ref, slice(low - first, high - first)
+
+    def get(self, p, q):
+        pieces = [ref[place] for _, _, ref, place in self.find(p, q)]
+        return pieces[0] if len(pieces) == 1 else jnp.concatenate(pieces, axis=0)
+
+    def put(self, p, value):
+        for low, high, ref, place in self.find(p, p + value.shape[0]):
+            ref[place] = value[low - p : high - p]
+
+
+def spans(first, last, size):
+    return [(p, min(p + size, last)) for p in range(first, last, size)]
 
 
 def x_up(value):
-    return jnp.concatenate([value[1:], rows(value[:1], -1)], axis=0)
+    return jnp.concatenate([value[:, 1:], rows(value[:, :1], -1)], axis=1)
 
 
 def x_down(value):
-    return jnp.concatenate([rows(value[-1:], 1), value[:-1]], axis=0)
-
-
-def couple(v, p, cx, cy, cz, dup):
-    here, by_x, by_y = v[p], cx[p], cy[p]
+    return jnp.concatenate([rows(value[:, -1:], 1), value[:, :-1]], axis=1)
+
+
+def couple(v, p, q, cx, cy, cz, dup):
+    here, by_x, by_y = v.get(p, q), cx.get(p, q), cy.get(p, q)
     total = by_x * x_up(here) + x_down(by_x * here)
     total = total + (by_y * lanes(here, -dup) + lanes(by_y * here, dup))
-    return total + (cz[p] * v[p - 1] + cz[p + 1] * v[p + 1])
+    return total + (cz.get(p, q) * v.get(p - 1, q - 1) + cz.get(p + 1, q + 1) * v.get(p + 1, q + 1))
 
 
 def chebyshev_factors(count, lower):
@@ -343,55 +353,75 @@
     return out
 
 
-def smooth(v_pair, d, b, dinv, coeffs, factors, first, last, dup):
-    old, new = v_pair
-    for number, (carry, gain) in enumerate(factors):
-        for p in range(first + number, last):
-            t = (b[p] + couple(old, p, *coeffs, dup)) * dinv[p] - old[p]
-            step = gain * t if carry == 0.0 else carry * d[p] + gain * t
-            if number + 1 < len(factors):
-                d[p] = step
-            new[p] = old[p] + step
-        new[last] = lanes(new[last - 1], 64)
-        old, new = new, old
-    return old
-
-
-def level_coefficients(beta, alpha, first, last, shift, dup, cx, cy, cz, dinv, diag, ends, seam):
+def sweep(new, now, before, factor, b, dinv, coeffs, p, q, dup, size):
+    carry, gain = factor
+    for p, q in spans(p, q, size):
+        base = (1.0 + carry - gain) * now.get(p, q)
+        if carry != 0.0 and before is not None:
+            base = base - carry * before.get(p, q)
+        new.put(p, (b.get(p, q) + couple(now, p, q, *coeffs, dup)) * (gain * dinv.get(p, q)) + base)
+
+
+def close(v, last):
+    v.put(last, lanes(v.get(last - 1, last), 64))
+
+
+def smooth(pair, b, dinv, coeffs, factors, first, last, dup, size):
+    before, now, spare = pair
+    for number, factor in enumerate(factors):
+        new = spare if before is None else before
+        sweep(new, now, before, factor, b, dinv, coeffs, first + number, last, dup, size)
+        close(new, last)
+        before, now = now, new
+    return now
+
+
+def inverse(value):
+    guess = pl.reciprocal(value, approx=True)
+    return guess * (2.0 - value * guess)
+
+
+def level_coefficients(beta, alpha, first, last, shift, dup, cx, cy, cz, dinv, diag, ends, seam, size):
     lane, row = lane_ids(), row_ids()
-    groups = beta[first].shape[0]
     y_last = (lane % 64) // dup == 64 // dup - 1
     y_first = (lane % 64) // dup == 0
-    y_rim = jnp.where(y_last | y_first, 0.5, 0.0)
-    rim = [y_rim] * groups
-    rim[0] = rim[0] + jnp.where(row == 0, 0.5, 0.0)
-    rim[-1] = rim[-1] + jnp.where(row == 7, 0.5, 0.0)
-    rim = jnp.stack(rim)
-    face = 0.5 * (beta[first - 1] + beta[first])
-    for p in range(first, last):
-        here = beta[p]
+    x_rim = jnp.where(row == 0, 0.5, 0.0), jnp.where(row == 7, 0.5, 0.0)
+    for p, q in spans(first, last, size):
+        here = beta.get(p, q)
         by_x = 0.5 * (here + x_up(here))
-        by_x = jnp.concatenate([by_x[:-1], jnp.where(row == 7, 0.0, by_x[-1:])], axis=0)
-        by_y = jnp.where(y_last, 0.0, 0.5 * (here + lanes(here, -dup)))
-        after = beta[p + 1] if p + 1 < last else lanes(here, 64)
-        next_face = 0.5 * (here + after)
-        total = shift * alpha[p] + by_x + x_down(by_x)
-        total = total + (by_y + lanes(by_y, dup)) + here * rim + (face + next_face)
-        cx[p], cy[p] = by_x, by_y
-        cz[p] = face * ends if p == seam else face
-        if diag is not None and p >= seam:
-            diag[p] = total
-        dinv[p] = 1.0 / jnp.where(total > 0.0, total, 1.0)
-        face = next_face
-    cz[last] = face
+        by_x = jnp.concatenate([by_x[:, :-1], jnp.where(row == 7, 0.0, by_x[:, -1:])], axis=1)
+        above = jnp.where(y_last, 0.0, lanes(here, -dup))
+        below = jnp.where(y_first, 0.0, lanes(here, dup))
+        by_y = jnp.where(y_last, 0.0, 0.5 * (here + above))
+        face = 0.5 * (beta.get(p - 1, q - 1) + here)
+        total = shift * alpha.get(p, q) + (by_x + x_down(by_x)) + (here + 0.5 * (above + below))
+        total = total + (face + 0.5 * (here + beta.get(p + 1, q + 1)))
+        groups = [total[:, i : i + 1] for i in range(total.shape[1])]
+        groups[0] = groups[0] + here[:, :1] * x_rim[0]
+        groups[-1] = groups[-1] + here[:, -1:] * x_rim[1]
+        total = jnp.concatenate(groups, axis=1)
+        cx.put(p, by_x)
+        cy.put(p, by_y)
+        cz.put(p, face)
+        diag.put(p, total)
+        dinv.put(p, inverse(jnp.where(total > 0.0, total, 1.0)))
+    if first <= seam < last:
+        cz.put(seam, cz.get(seam, seam + 1) * ends)
+    else:
+        cz.put(last, 0.5 * (beta.get(last - 1, last) + beta.get(last, last + 1)))
 
 
 def restrict_pair(first, second, dup):
     lane = lane_ids()
     total = first + second
-    groups = total.shape[0]
-    total = jnp.concatenate([total[i : i + 1] + total[i + 1 : i + 2] for i in range(0, groups, 2)], axis=0)
+    total = jnp.concatenate([total[:, i : i + 1] + total[:, i + 1 : i + 2] for i in range(0, total.shape[1], 2)], axis=1)
     return total + jnp.where((lane // dup) % 2 == 0, lanes(total, -dup), lanes(total, dup))
+
+
+def restrict(take, p, q, dup):
+    fine = take(2 * p, 2 * q)
+    fine = fine.reshape((q - p, 2) + fine.shape[1:])
+    return restrict_pair(fine[:, 0], fine[:, 1], dup)
 
 
 def halo_masks():
@@ -409,118 +439,168 @@
     return jnp.where(end, 0.0, 1.0)
 
 
-def down_kernel(
-    own, even, odd,
-    gather, rim, u0, b0, dinv0, diag0, cx0, cy0, cz0, u1, b1, dinv1, cx1, cy1, cz1,
-    beta_s, alpha_s, b_s, dinv_s, cx_s, cy_s, cz_s, v_a, v_b, d_s,
-    beta1_s, alpha1_s, b1_s, w_a, w_b, e_s,
-):
+def shape_of(*dims):
+    return jax.ShapeDtypeStruct(dims + TILE, jnp.float32)
+
+
+def scratch(*dims):
+    return pltpu.VMEM(dims + TILE, jnp.float32)
+
+
+def call(kernel, name, operands, out_shape, scratch_shapes, hbm_outputs=0):
+    vmem = pl.BlockSpec(memory_space=pltpu.VMEM)
+    return pl.pallas_call(
+        kernel,
+        out_shape=out_shape,
+        in_specs=[vmem] * len(operands),
+        out_specs=[pl.BlockSpec(memory_space=pl.ANY)] * hbm_outputs + [vmem] * (len(out_shape) - hbm_outputs),
+        scratch_shapes=scratch_shapes,
+        compiler_params=pltpu.CompilerParams(vmem_limit_bytes=16 * 2**20),
+        name=name,
+    )(*operands)
+
+
+PRE_SHAPES = [(7, 4), (7, 4), (8, 4), (7, 4), (7, 4), (3, 2), (3, 2), (4, 2), (3, 2), (3, 2)]
+MID_SHAPES = [(13, 4)] * 5 + [(7, 2)] * 5
+
+
+def coefficient_planes(pre, mid):
+    zero = [Planes(*([(4, mid[i])] if mid else []), *([(17, pre[i])] if pre else [])) for i in range(5)]
+    one = [Planes(*([(2, mid[i])] if mid else []), *([(9, pre[i])] if pre else [])) for i in range(5, 10)]
+    return zero, one
+
+
+def pre_kernel(own, *refs):
+    pre, (alpha1, beta1, v1, v2, v3, v4), (ghost, ghost1) = refs[:10], refs[10:16], refs[16:]
+    zero, one = coefficient_planes(pre, None)
+    alpha, beta = Planes((16, own.at[0])), Planes((16, own.at[1]), (24, ghost))
+    alpha_one, beta_one = Planes((8, alpha1)), Planes((8, beta1), (12, ghost1))
+    close(beta, PLANES)
+    level_coefficients(beta, alpha, 17, PLANES, SHIFT_BASE, 1, *zero, None, 16, COEF_SPAN)
+    beta_one.put(8, 0.125 * restrict(beta.get, 8, PLANES1, 1))
+    alpha_one.put(8, 0.125 * restrict(alpha.get, 8, PLANES1, 1))
+    close(beta_one, PLANES1)
+    level_coefficients(beta_one, alpha_one, 9, PLANES1, SHIFT_BASE * 4.0, 2, *one, None, 8, COEF_SPAN1)
+    b, coeffs, dinv = Planes((16, own.at[2])), zero[:3], zero[3]
+    factors = chebyshev_factors(SWEEPS, SMOOTH_LOWER)
+    iterates = [None, Planes((17, v1)), Planes((18, v2)), Planes((19, v3)), Planes((20, v4))]
+    for p, q in spans(17, PLANES, 4):
+        iterates[1].put(p, factors[0][1] * (b.get(p, q) * dinv.get(p, q)))
+    close(iterates[1], PLANES)
+    for i in range(2, 5):
+        sweep(iterates[i], iterates[i - 1], iterates[i - 2], factors[i - 1], b, dinv, coeffs, 16 + i, PLANES, 1, SPAN)
+        close(iterates[i], PLANES)
+
+
+def mid_kernel(own, even, odd, *refs):
+    beta1_own, alpha1_own, mid, (beta_s, alpha_s, beta1_s, alpha1_s) = refs[0], refs[1], refs[2:12], refs[12:]
+    _, from_even = halo_masks()
+    zero, one = coefficient_planes(None, mid)
+    for p in range(16):
+        alpha_s[p], beta_s[p] = (halo_plane(even.at[a], odd.at[a], p, 16, from_even) for a in range(2))
+    beta, alpha = Planes((0, beta_s), (16, own.at[1])), Planes((0, alpha_s), (16, own.at[0]))
+    ends = ends_factor()
+    level_coefficients(beta, alpha, 4, 17, SHIFT_BASE, 1, *zero, ends, 16, COEF_SPAN)
+    beta_one, alpha_one = Planes((0, beta1_s), (8, beta1_own)), Planes((0, alpha1_s), (8, alpha1_own))
+    for p, q in spans(0, 8, 2):
+        beta_one.put(p, 0.125 * restrict(beta.get, p, q, 1))
+        alpha_one.put(p, 0.125 * restrict(alpha.get, p, q, 1))
+    level_coefficients(beta_one, alpha_one, 2, 9, SHIFT_BASE * 4.0, 2, *one, ends, 8, COEF_SPAN1)
+
+
+def halo_plane(even, odd, p, count, from_even):
+    if p < count // 2:
+        return jnp.where(from_even, even[p], odd[p])
+    k = count - 1 - p
+    return lanes(jnp.where(from_even, odd[k], even[k]), 64)
+
+
+def post_kernel(own, even, odd, *refs):
+    pre, (alpha1, beta1, v1, v2, v3, v4), mid = refs[:10], refs[10:16], refs[16:26]
+    gather, rim, halo_b, late, u1, b1 = refs[26:32]
+    f1, f2, f3, b1_s, w_a, w_b, tile_s, rim_s, sent = refs[32:]
     lane = lane_ids()
     _, from_even = halo_masks()
-    ends = ends_factor()
-
-    def field(a, p):
-        if p >= 16:
-            return own[a, p - 16]
-        if p >= 8:
-            return lanes(jnp.where(from_even, odd[a, 15 - p], even[a, 15 - p]), 64)
-        return jnp.where(from_even, even[a, p], odd[a, p])
-
-    for p in range(PLANES):
-        beta_s[p] = field(2, p)
-        alpha_s[p] = field(1, p)
-    b = Planes(b0, 12, b_s)
-    for p in range(4, PLANES):
-        b[p] = field(0, p)
-    cx, cy, cz = Planes(cx0, 12, cx_s), Planes(cy0, 12, cy_s), Planes(cz0, 12, cz_s)
-    dinv = Planes(dinv0, 12, dinv_s)
-    diag = Planes(diag0, 16)
-    level_coefficients(beta_s, alpha_s, 4, PLANES, SHIFT_BASE, 1, cx, cy, cz, dinv, diag, ends, 16)
-    diag_all = lambda p: diag[p]
-
+    zero, one = coefficient_planes(pre, mid)
+    coeffs, dinv, diag = zero[:3], zero[3], zero[4]
+    b = Planes((4, halo_b), (16, own.at[2]))
+    for p in range(4, 16):
+        b.put(p, halo_plane(even.at[2], odd.at[2], p, 16, from_even)[None])
     factors = chebyshev_factors(SWEEPS, SMOOTH_LOWER)
-    for p in range(4, PLANES):
-        start = factors[0][1] * (b[p] * dinv[p])
-        v_a[p] = start
-        d_s[p] = start
-    v_a[PLANES] = lanes(v_a[PLANES - 1], 64)
-    v = smooth((v_a, v_b), d_s, b, dinv, (cx, cy, cz), factors[1:], 5, PLANES, 1)
-    for p in range(8):
-        u0[p] = v[16 + p]
-
-    def residual(v, p, b, dinv, coeffs, dup):
-        return ((b[p] + couple(v, p, *coeffs, dup)) * dinv[p] - v[p]) / dinv[p]
-
-    b_one = Planes(b1, 8, b1_s)
+    iterates = [
+        None,
+        Planes((4, f1), (17, v1)),
+        Planes((5, f2), (18, v2)),
+        Planes((6, f3), (19, v3)),
+        Planes((7, late), (20, v4)),
+    ]
+    for p, q in spans(4, 17, 4):
+        iterates[1].put(p, factors[0][1] * (b.get(p, q) * dinv.get(p, q)))
+    for i in range(2, 5):
+        sweep(iterates[i], iterates[i - 1], iterates[i - 2], factors[i - 1], b, dinv, coeffs, 3 + i, 16 + i, 1, SPAN)
+    v = iterates[4]
+    rim_s[0:20] = v.get(16, 21).reshape((20,) + TILE)
+    copies = [pltpu.make_async_copy(rim_s.at[0:20], rim.at[0:20], sent.at[0])]
+    copies[0].start()
+
+    def residual(v, b, diag, coeffs, dup):
+        return lambda p, q: (b.get(p, q) + couple(v, p, q, *coeffs, dup)) - diag.get(p, q) * v.get(p, q)
+
+    b_one = Planes((4, b1_s), (8, b1))
     for p in range(4, PLANES1):
-        pair = [residual(v, 2 * p + i, b, dinv, (cx, cy, cz), 1) for i in range(2)]
-        b_one[p] = 0.5 * restrict_pair(*pair, 1)
-    for p in range(PLANES1):
-        beta1_s[p] = 0.125 * restrict_pair(beta_s[2 * p], beta_s[2 * p + 1], 1)
-        alpha1_s[p] = 0.125 * restrict_pair(alpha_s[2 * p], alpha_s[2 * p + 1], 1)
-    cx, cy, cz, dinv = Planes(cx1, 2), Planes(cy1, 2), Planes(cz1, 2), Planes(dinv1, 2)
-    level_coefficients(beta1_s, alpha1_s, 2, PLANES1, SHIFT_BASE * 4.0, 2, cx, cy, cz, dinv, None, ends, 8)
-    for p in range(4, PLANES1):
-        start = factors[0][1] * (b_one[p] * dinv[p])
-        w_a[p] = start
-        e_s[p] = start
-    w_a[PLANES1] = lanes(w_a[PLANES1 - 1], 64)
-    w = smooth((w_a, w_b), e_s, b_one, dinv, (cx, cy, cz), factors[1:], 5, PLANES1, 2)
-    for p in range(4):
-        u1[p] = w[8 + p]
-        rim[20 + 2 * p : 22 + 2 * p] = jnp.where(lane % 2 == 0, w[8 + p], b_one[8 + p])
-    for p in range(5):
-        rim[4 * p : 4 * p + 4] = u0[p]
-    for p in range(2):
-        pair = [residual(w, 8 + 2 * p + i, b_one, dinv, (cx, cy, cz), 2) for i in range(2)]
-        b_two = 0.5 * restrict_pair(*pair, 2)
-        beta_two = 0.125 * restrict_pair(beta1_s[8 + 2 * p], beta1_s[9 + 2 * p], 2)
-        alpha_two = 0.125 * restrict_pair(alpha1_s[8 + 2 * p], alpha1_s[9 + 2 * p], 2)
-        tile = jnp.where(lane % 4 == 0, b_two, jnp.where(lane % 4 == 1, beta_two, alpha_two))
-        for block in range(GX * GZ):
-            gather[block, p] = tile[0]
-
-
-def shape_of(*dims):
-    return jax.ShapeDtypeStruct(dims + TILE, jnp.float32)
-
-
-def scratch(*dims):
-    return pltpu.VMEM(dims + TILE, jnp.float32)
-
-
-def down(own, even, odd):
-    out_shape = [
-        shape_of(GX * GZ, 2), shape_of(36), shape_of(8, 4),
-        shape_of(12, 4), shape_of(12, 4), shape_of(8, 4), shape_of(12, 4), shape_of(12, 4), shape_of(13, 4),
-        shape_of(4, 2), shape_of(4, 2), shape_of(10, 2), shape_of(10, 2), shape_of(10, 2), shape_of(11, 2),
-    ]
-    vmem = pl.BlockSpec(memory_space=pltpu.VMEM)
-    return pl.pallas_call(
-        down_kernel,
-        out_shape=out_shape,
-        in_specs=[vmem] * 3,
-        out_specs=[vmem] * len(out_shape),
-        scratch_shapes=[
-            scratch(24, 4), scratch(24, 4), scratch(12, 4), scratch(12, 4), scratch(12, 4), scratch(12, 4), scratch(12, 4),
-            scratch(25, 4), scratch(25, 4), scratch(24, 4),
-            scratch(12, 2), scratch(12, 2), scratch(8, 2), scratch(13, 2), scratch(13, 2), scratch(12, 2),
+        b_one.put(p, 0.5 * restrict(residual(v, b, diag, coeffs, 1), p, p + 1, 1))
+    coeffs, dinv, diag = one[:3], one[3], one[4]
+    w, spare = Planes((0, w_a)), Planes((0, w_b))
+    w.put(4, factors[0][1] * (b_one.get(4, PLANES1) * dinv.get(4, PLANES1)))
+    close(w, PLANES1)
+    w = smooth((None, w, spare), b_one, dinv, coeffs, factors[1:], 5, PLANES1, 2, SPAN1)
+    b_two = 0.5 * restrict(residual(w, b_one, diag, coeffs, 2), 4, 6, 2)
+    beta_two = 0.125 * restrict(Planes((8, beta1)).get, 4, 6, 2)
+    alpha_two = 0.125 * restrict(Planes((8, alpha1)).get, 4, 6, 2)
+    tile_s[...] = jnp.where(lane % 4 == 0, b_two, jnp.where(lane % 4 == 1, beta_two, alpha_two))[:, 0]
+    copies += [pltpu.make_async_copy(tile_s, gather.at[n], sent.at[n + 1]) for n in range(GX * GZ)]
+    for copy in copies[1:]:
+        copy.start()
+    u1[...] = w.get(8, PLANES1)
+    rim_s[20:28] = jnp.where(lane % 2 == 0, w.get(8, PLANES1), b_one.get(8, PLANES1)).reshape((8,) + TILE)
+    copies.append(pltpu.make_async_copy(rim_s.at[20:28], rim.at[20:28], sent.at[GX * GZ + 1]))
+    copies[-1].start()
+    for copy in copies:
+        copy.wait()
+
+
+def down_pre(own):
+    shapes = PRE_SHAPES + [(4, 2), (4, 2), (8, 4), (7, 4), (6, 4), (5, 4)]
+    return call(pre_kernel, "down_pre", (own,), [shape_of(*n) for n in shapes], [scratch(1, 4), scratch(1, 2)])
+
+
+def down_mid(own, even, odd, beta1, alpha1):
+    return call(
+        mid_kernel, "down_mid", (own, even, odd, beta1, alpha1), [shape_of(*n) for n in MID_SHAPES],
+        [scratch(16, 4), scratch(16, 4), scratch(8, 2), scratch(8, 2)],
+    )
+
+
+def down_post(own, even, odd, pre, mid):
+    shapes = [(GX * GZ, 2), (36,), (12, 4), (13, 4), (4, 2), (4, 2)]
+    return call(
+        post_kernel, "down_post", (own, even, odd, *pre, *mid), [shape_of(*n) for n in shapes],
+        [
+            scratch(13, 4), scratch(13, 4), scratch(13, 4), scratch(4, 2), scratch(13, 2), scratch(13, 2),
+            scratch(2), scratch(28), pltpu.SemaphoreType.DMA((GX * GZ + 2,)),
         ],
-        compiler_params=pltpu.CompilerParams(vmem_limit_bytes=16 * 2**20),
-        name="down_strokes",
-    )(own, even, odd)
+        hbm_outputs=2,
+    )
 
 
 def outer(value, half):
-    before = jnp.concatenate([lanes(value[-1:], 1), value[:-1]], axis=0)
-    after = jnp.concatenate([value[1:], lanes(value[:1], -1)], axis=0)
-    return jnp.where(half == 0, before, after)
-
-
-def coarse_kernel(
-    mine, other, rim_even, rim_odd, u0, b0, dinv0, diag0, cx0, cy0, cz0, u1, b1, dinv1, cx1, cy1, cz1,
-    out, cores, e2_s, v_a, v_b, d_s, w_a, w_b, e_s, bx_s, uz_s, got,
-):
+    turned = lanes(value, 64)
+    before = jnp.concatenate([lanes(value[-1:], 65), turned[:-1]], axis=0)
+    after = jnp.concatenate([turned[1:], lanes(value[:1], 63)], axis=0)
+    return jnp.where(half == 0, before, after), turned
+
+
+def coarse_kernel(mine, other, out, cores, e2_s):
     lane, row = lane_ids(), row_ids()
     half = lane // 64
     x, y, z = position()
@@ -555,41 +635,47 @@
         rim = jnp.where(x_last | x_first, 0.5, 0.0) + jnp.where(y_last | y_first, 0.5, 0.0)
         return by_x, by_y, (by_x + rows(by_x, dx)) + (by_y + lanes(by_y, dy)) + beta * rim
 
-    def flat(v, by_x, by_y, dx, dy):
-        total = by_x * rows(v, -dx) + rows(by_x * v, dx)
-        return total + (by_y * lanes(v, -dy) + lanes(by_y * v, dy))
+    def scaled(by_x, by_y, inv, dx, dy):
+        return by_x * inv, rows(by_x, dx) * inv, by_y * inv, lanes(by_y, dy) * inv
+
+    def flat(v, coeffs, dx, dy):
+        x_above, x_below, y_above, y_below = coeffs
+        total = x_above * rows(v, -dx) + x_below * rows(v, dx)
+        return total + (y_above * lanes(v, -dy) + y_below * lanes(v, dy))
 
     x0, y0, s0 = sides(beta_two[0], 1, 4)
     x1, y1, s1 = sides(beta_two[1], 1, 4)
     middle = 0.5 * (beta_two[0] + beta_two[1])
     inner = 0.5 * (beta_two[1] + lanes(beta_two[1], 64))
-    edge = 0.5 * (beta_two[0] + jnp.where(end, 0.0, outer(lanes(beta_two[0], 64), half)))
-    rim2 = jnp.where(end, 0.0, edge)
+    edge = 0.5 * (beta_two[0] + jnp.where(end, 0.0, outer(beta_two[0], half)[0]))
     shift = SHIFT_BASE * 16.0
     diag_a = shift * alpha_two[0] + s0 + (middle + edge)
     diag_b = shift * alpha_two[1] + s1 + (middle + inner)
-    inv_a, inv_b = 1.0 / diag_a, 1.0 / diag_b
+    inv_a, inv_b = inverse(diag_a), inverse(diag_b)
+    flat_a, flat_b = scaled(x0, y0, inv_a, 1, 4), scaled(x1, y1, inv_b, 1, 4)
+    middle_a, middle_b = middle * inv_a, middle * inv_b
+    rim_a, inner_b = jnp.where(end, 0.0, edge) * inv_a, inner * inv_b
+    rhs_a, rhs_b = b_two[0] * inv_a, b_two[1] * inv_b
 
     def apply_two(va, vb):
-        ta = flat(va, x0, y0, 1, 4) + (middle * vb + rim2 * outer(lanes(va, 64), half))
-        tb = flat(vb, x1, y1, 1, 4) + (middle * va + inner * lanes(vb, 64))
+        ta = flat(va, flat_a, 1, 4) + (middle_a * vb + rim_a * outer(va, half)[0])
+        tb = flat(vb, flat_b, 1, 4) + (middle_b * va + inner_b * lanes(vb, 64))
         return ta, tb
 
-    def sweeps_two(va, vb, da, db, factors):
+    def sweeps_two(before, now, factors):
         for carry, gain in factors:
-            ta, tb = apply_two(va, vb)
-            ta = (b_two[0] + ta) * inv_a - va
-            tb = (b_two[1] + tb) * inv_b - vb
-            if carry == 0.0:
-                da, db = gain * ta, gain * tb
-            else:
-                da, db = carry * da + gain * ta, carry * db + gain * tb
-            va, vb = va + da, vb + db
-        return va, vb
+            totals = apply_two(*now)
+            new = []
+            for v, old, rhs, total in zip(now, before or (None, None), (rhs_a, rhs_b), totals):
+                base = (1.0 + carry - gain) * v + gain * rhs
+                if carry != 0.0 and old is not None:
+                    base = base - carry * old
+                new.append(base + gain * total)
+            before, now = now, new
+        return now
 
     factors = chebyshev_factors(SWEEPS, SMOOTH_LOWER)
-    da, db = factors[0][1] * (b_two[0] * inv_a), factors[0][1] * (b_two[1] * inv_b)
-    ua, ub = sweeps_two(da, db, da, db, factors[1:])
+    ua, ub = sweeps_two(None, (factors[0][1] * rhs_a, factors[0][1] * rhs_b), factors[1:])
     ta, tb = apply_two(ua, ub)
 
     def restrict_whole(first, second):
@@ -597,29 +683,31 @@
         total = total + jnp.where(row % 2 == 0, rows(total, -1), rows(total, 1))
         return total + jnp.where((lane // 4) % 2 == 0, lanes(total, -4), lanes(total, 4))
 
-    b_low = 0.5 * restrict_whole(b_two[0] + ta - diag_a * ua, b_two[1] + tb - diag_b * ub)
+    b_low = 0.5 * restrict_whole(diag_a * (rhs_a + ta - ua), diag_b * (rhs_b + tb - ub))
     beta_low = 0.125 * restrict_whole(beta_two[0], beta_two[1])
     alpha_low = 0.125 * restrict_whole(alpha_two[0], alpha_two[1])
 
     x_low, y_low, s_low = sides(beta_low, 2, 8)
-    turned = lanes(beta_low, 64)
+    beyond, turned = outer(beta_low, half)
     inner_low = 0.5 * (beta_low + turned)
-    edge_low = 0.5 * (beta_low + jnp.where(end, 0.0, outer(turned, half)))
-    rim_low = jnp.where(end, 0.0, edge_low)
-    diag_low = SHIFT_BASE * 64.0 * alpha_low + s_low + (inner_low + edge_low)
-    inv_low = 1.0 / diag_low
-    step = None
-    v = None
+    edge_low = 0.5 * (beta_low + jnp.where(end, 0.0, beyond))
+    inv_low = inverse(SHIFT_BASE * 64.0 * alpha_low + s_low + (inner_low + edge_low))
+    flat_low = scaled(x_low, y_low, inv_low, 2, 8)
+    rim_low = jnp.where(end, 0.0, edge_low) * inv_low
+    inner_low = inner_low * inv_low
+    rhs_low = b_low * inv_low
+    before = v = None
     for carry, gain in chebyshev_factors(BOTTOM, BOTTOM_LOWER):
         if v is None:
-            step = gain * (b_low * inv_low)
-            v = step
+            v = gain * rhs_low
             continue
-        turned = lanes(v, 64)
-        total = flat(v, x_low, y_low, 2, 8) + (inner_low * turned + rim_low * outer(turned, half))
-        step = carry * step + gain * ((b_low + total) * inv_low - v)
-        v = v + step
-    va, vb = sweeps_two(ua + v, ub + v, None, None, factors)
+        beyond, turned = outer(v, half)
+        base = (1.0 + carry - gain) * v + gain * rhs_low
+        if before is not None:
+            base = base - carry * before
+        total = flat(v, flat_low, 2, 8) + (inner_low * turned + rim_low * beyond)
+        before, v = v, base + gain * total
+    va, vb = sweeps_two(None, (ua + v, ub + v), factors)
     for group in range(8):
         e2_s[group, 0] = va[group]
         e2_s[group, 1] = vb[group]
@@ -639,15 +727,33 @@
 
     below, here, above = fetch(-1), fetch(0), fetch(1)
     first = half == 0
-    e_two = [
-        jnp.where(first, below[0], above[0]),
-        jnp.where(first, below[1], above[1]),
-        lanes(jnp.where(first, above[1], below[1]), 64),
-        lanes(jnp.where(first, above[0], below[0]), 64),
-        here[0],
-        here[1],
-    ]
+    out[0] = jnp.where(first, below[0], above[0])
+    out[1] = jnp.where(first, below[1], above[1])
+    out[2] = lanes(jnp.where(first, above[1], below[1]), 64)
+    out[3] = lanes(jnp.where(first, above[0], below[0]), 64)
+    out[4] = here[0]
+    out[5] = here[1]
+
+
+def coarse(mine, other):
+    vmem = pl.BlockSpec(memory_space=pltpu.VMEM)
+    return pl.pallas_call(
+        coarse_kernel,
+        out_shape=shape_of(6),
+        in_specs=[vmem] * 2,
+        out_specs=vmem,
+        scratch_shapes=[scratch(2, GX * GZ, 2), scratch(8, 2)],
+        compiler_params=pltpu.CompilerParams(vmem_limit_bytes=8 * 2**20),
+        name="coarse",
+    )(mine, other)
+
+
+def up_kernel(e_two, rim_even, rim_odd, own, halo_b, late, u1, b1, v4, *refs):
+    pre, mid, (out, v_a, v_b, w_a, w_b, bx_s) = refs[:10], refs[10:20], refs[20:]
+    zero, one = coefficient_planes(pre, mid)
+    lane, row = lane_ids(), row_ids()
     _, from_even = halo_masks()
+    factors = chebyshev_factors(SWEEPS, SMOOTH_LOWER)
 
     for p in range(1, 8):
         if p >= 4:
@@ -661,52 +767,42 @@
     for p in range(8, PLANES1):
         w_a[p] = u1[p - 8] + e_two[p // 2]
     w_a[PLANES1] = lanes(w_a[PLANES1 - 1], 64)
-    b_one = Planes(b1, 8, bx_s)
-    coeffs = (Planes(cx1, 2), Planes(cy1, 2), Planes(cz1, 2))
-    w = smooth((w_a, w_b), e_s, b_one, Planes(dinv1, 2), coeffs, factors, 2, PLANES1, 2)
+    pair = (Planes((0, w_b)), Planes((0, w_a)), None)
+    w = smooth(pair, Planes((0, bx_s), (8, b1)), one[3], one[:3], factors, 2, PLANES1, 2, SPAN1)
 
     for p in range(11, PLANES):
         if p >= 16:
-            start = u0[p - 16]
+            start = Planes((7, late), (20, v4)).get(p, p + 1)[0]
         else:
             k = 4 * (15 - p)
             start = lanes(jnp.where(from_even, rim_odd[k : k + 4], rim_even[k : k + 4]), 64)
-        e_one = w[p // 2]
+        e_one = w.get(p // 2, p // 2 + 1)[0]
         e_one = jnp.concatenate([e_one[:1], e_one[:1], e_one[1:], e_one[1:]], axis=0)
         v_a[p] = start + e_one
     v_a[PLANES] = lanes(v_a[PLANES - 1], 64)
-    b = Planes(b0, 12)
-    coeffs = (Planes(cx0, 12), Planes(cy0, 12), Planes(cz0, 12))
-    v = smooth((v_a, v_b), d_s, b, Planes(dinv0, 12), coeffs, factors, 12, PLANES, 1)
+    b, diag, coeffs = Planes((4, halo_b), (16, own.at[2])), zero[4], zero[:3]
+    v = smooth((Planes((0, v_b)), Planes((0, v_a)), None), b, zero[3], coeffs, factors, 12, PLANES, 1, SPAN)
     low = (lane // 32) % 2 == 0
     for k in range(4):
         for o in range(2):
             parts = []
             for pp in range(2):
                 p = 16 + k + 4 * pp
-                value = v[p] if o == 0 else (b[p] + couple(v, p, *coeffs, 1)) - diag0[p - 16] * v[p]
-                parts.append(regroup([value[i] for i in range(4)], 0, 2, row))
+                value = v.get(p, p + 1)
+                if o == 1:
+                    value = (b.get(p, p + 1) + couple(v, p, p + 1, *coeffs, 1)) - diag.get(p, p + 1) * value
+                parts.append(regroup([value[0, i] for i in range(4)], 0, 2, row))
             for i in range(GX):
                 one, two = parts[0][i], parts[1][i]
                 out[2 * i, pl.ds(o * 32 + k * 8, 8), :] = jnp.where(low, one, lanes(two, 32))
                 out[2 * i + 1, pl.ds(o * 32 + k * 8, 8), :] = jnp.where(low, lanes(one, -32), two)
 
 
-def coarse_and_up(mine, other, rim_even, rim_odd, kept):
-    vmem = pl.BlockSpec(memory_space=pltpu.VMEM)
-    operands = (mine, other, rim_even, rim_odd, *kept)
-    return pl.pallas_call(
-        coarse_kernel,
-        out_shape=jax.ShapeDtypeStruct((8, 64, 128), jnp.float32),
-        in_specs=[vmem] * len(operands),
-        out_specs=vmem,
-        scratch_shapes=[
-            scratch(2, GX * GZ, 2), scratch(8, 2), scratch(25, 4), scratch(25, 4), scratch(24, 4),
-            scratch(13, 2), scratch(13, 2), scratch(12, 2), scratch(8, 2), scratch(1), scratch(1),
-        ],
-        compiler_params=pltpu.CompilerParams(vmem_limit_bytes=16 * 2**20),
-        name="coarse_and_up",
-    )(*operands)
+def up(*operands):
+    return call(
+        up_kernel, "up_strokes", operands, [jax.ShapeDtypeStruct((8, 64, 128), jnp.float32)],
+        [scratch(25, 4), scratch(25, 4), scratch(13, 2), scratch(13, 2), scratch(8, 2)],
+    )[0]
 
 
 def unpack_kernel(in_ref, v_ref, r_ref, fields, turned, staged, left):
@@ -750,16 +846,20 @@
 
 def slab_shards(right_side, alpha_coef, beta_coef):
     even_pairs, odd_pairs = swap_pairs(False), swap_pairs(True)
-    packed = pack(jnp.stack([right_side, alpha_coef, beta_coef]))
+    packed = pack(jnp.stack([alpha_coef, beta_coef, right_side]))
     own = to_slab(lax.all_to_all(packed, RING, 0, 0))
     even = lax.ppermute(own, ALL, even_pairs)
     odd = lax.ppermute(own, ALL, odd_pairs)
-    gather, rim, *kept = down(own, even, odd)
+    found = down_pre(own)
+    pre, alpha1, beta1, v4 = found[:10], found[10], found[11], found[15]
+    mid = down_mid(own, even, odd, beta1, alpha1)
+    gather, rim, halo_b, late, u1, b1 = down_post(own, even, odd, found, mid)
     rim_even = lax.ppermute(rim, ALL, even_pairs)
     rim_odd = lax.ppermute(rim, ALL, odd_pairs)
     mine = lax.all_to_all(gather, ("gx", "gz"), 0, 0)
     other = lax.ppermute(mine, "gy", [(0, 1), (1, 0)])
-    result = coarse_and_up(mine, other, rim_even, rim_odd, kept)
+    kept = (own, halo_b, late, u1, b1, v4, *pre, *mid)
+    result = up(coarse(mine, other), rim_even, rim_odd, *kept)
     return tuple(unpack(lax.all_to_all(result, RING, 0, 0)))
 
 

time: 59.8 us -> 57.2 us (0.957)
  Pallas kernels: 11.5 us -> 9.32 us
    pallas_call x3 -> x6, Pallas kernels: 9.22 us -> 7.08 us  [the longest x4 4.14 us: call(): pl.pallas_call(kernel, out_shape=out_shape, in_specs=[vmem] * len(operand...]
  transfers between devices with their start and end apart: 6 -> 6, of which waited for: 3 -> 3; matrix products, arithmetic and copies ran while one was open for 0% -> 0% of each run, Pallas kernels for 0% -> 6%
where the time goes in v3:
time: 57.2 us; the launch traced here: 56.9 us
  blocking collectives  22.7 us (40%)
  starting transfers between devices  16.8 us (29%)
  Pallas kernels  9.32 us (16%)
  waiting for transfers between devices  6.38 us (11%)
  other arithmetic  1.06 us (2%)
  between operations  0.71 us (1%)
    all_to_all x1, blocking collectives, slab_shards(): own = to_slab(lax.all_to_all(packed, RING, 0, 0))  13.3 us
    all_to_all x1, starting transfers between devices, slab_shards(): mine = lax.all_to_all(gather, ('gx', 'gz'), 0, 0)  10.1 us
    all_to_all x1, blocking collectives, slab_shards(): return tuple(unpack(lax.all_to_all(result, RING, 0, 0)))  9.35 us
    pallas_call x4, Pallas kernels, call(): pl.pallas_call(kernel, out_shape=out_shape, in_specs=[vmem] * len(operand...  4.14 us
    all_to_all x1, waiting for transfers between devices, slab_shards(): mine = lax.all_to_all(gather, ('gx', 'gz'), 0, 0)  4.14 us
    ppermute x1, starting transfers between devices, slab_shards(): rim_even = lax.ppermute(rim, ALL, even_pairs)  3.33 us
    pallas_call x1, Pallas kernels, coarse(): pl.pallas_call(coarse_kernel, out_shape=shape_of(6), in_specs=[vmem] * 2,...  2.77 us
    ppermute x1, starting transfers between devices, slab_shards(): even = lax.ppermute(own, ALL, even_pairs)  1.97 us
  transfers between devices with their start and end apart: 6, of which 3 were waited for; matrix products, arithmetic and copies ran while one was open for 0% of the time, Pallas kernels for 6%

profile of v3, /device:TPU:0, one launch (start us, length us, event | category | flops | bytes accessed | tf_op | source)
XLA Modules:
  0.0 56.9 jit_solution(18425025210131213484)
XLA Ops:
  0.6 1.1 %pad_maximum_fusion.fields = f32[3,8,32,128]{3,2,1,0:T(8,128)S(1)} fusion(f32[1,8,32,128]{3,2,1,0:T(8,128)} %bitcast.3, f32[1,8,32,128]{3,2,1,0:T(8,128)} %bitcast.4, f32[1,8,32,128]{3,2,1,0:T(8,128)} %bitcast.5), kind=kLoop, calls=%fused_computation | loop fusion | flops 196608 | bytes 786432 | tf_op jit(solution)/shard_map/stack | solution.py:849
  1.7 1.1 %pack.1 = f32[8,96,128]{2,1,0:T(8,128)S(1)} custom-call(f32[3,8,32,128]{3,2,1,0:T(8,128)S(1)} %pad_maximum_fusion.fields), custom_call_target="tpu_custom_call" | custom-call | tf_op jit(solution)/shard_map/pack/pallas_call | solution.py:267
  2.8 13.3 %all_to_all.15.in_ref = f32[8,96,128]{2,1,0:T(8,128)S(1)} all-to-all(f32[8,96,128]{2,1,0:T(8,128)S(1)} %pack.1), channel_id=1, replica_groups=mesh['gx'=4,'gy'=2,'gz'=4] {'gx','gy'}, dimensions={0} | all-to-all | bytes 786432 | tf_op jit(solution)/shard_map/all_to_all | solution.py:850
  16.1 0.2 to_slab.1.own
  16.3 0.7 %collective-permute-start.1 = (f32[3,8,4,8,128]{4,3,2,1,0:T(8,128)S(1)}, f32[3,8,4,8,128]{4,3,2,1,0:T(8,128)S(1)}, u32[]{:S(2)}, u32[]{:S(2)}) collective-permute-start(f32[3,8,4,8,128]{4,3,2,1,0:T(8,128)S(1)} %to_slab.1.own), channel_id=1, source_target_pairs={{4,8},{12,24},{28,16},{20,21},{17,29},{25,13},{9,5},{1,2},{6,10},{... | collective-permute-start | bytes 1179656 | tf_op jit(solution)/shard_map/ppermute | solution.py:852
  17.0 2.0 %collective-permute-start = (f32[3,8,4,8,128]{4,3,2,1,0:T(8,128)S(1)}, f32[3,8,4,8,128]{4,3,2,1,0:T(8,128)S(1)}, u32[]{:S(2)}, u32[]{:S(2)}) collective-permute-start(f32[3,8,4,8,128]{4,3,2,1,0:T(8,128)S(1)} %to_slab.1.own), channel_id=1, source_target_pairs={{0,4},{8,12},{24,28},{16,20},{21,17},{29,25},{13,9},{5,1},{2,6},{1... | collective-permute-start | bytes 1179656 | tf_op jit(solution)/shard_map/ppermute | solution.py:851
  18.9 0.5 down_pre.1
  19.4 0.0 collective-permute-done.1.odd
  19.4 0.9 %collective-permute-done.even = f32[3,8,4,8,128]{4,3,2,1,0:T(8,128)S(1)} collective-permute-done((f32[3,8,4,8,128]{4,3,2,1,0:T(8,128)S(1)}, f32[3,8,4,8,128]{4,3,2,1,0:T(8,128)S(1)}, u32[]{:S(2)}, u32[]{:S(2)}) %collective-permute-start) | collective-permute-done | bytes 393248 | tf_op jit(solution)/shard_map/ppermute | solution.py:851
  20.3 0.4 down_mid.1
  20.7 2.1 %down_post.1 = (f32[16,2,8,128]{3,2,1,0:T(8,128)}, f32[36,8,128]{2,1,0:T(8,128)}, f32[12,4,8,128]{3,2,1,0:T(8,128)S(1)}, f32[13,4,8,128]{3,2,1,0:T(8,128)S(1)}, ...) custom-call(f32[3,8,4,8,128]{4,3,2,1,0:T(8,128)S(1)} %to_slab.1.own, ...), custom_call_target="tpu_custom_call" | custom-call | tf_op jit(solution)/shard_map/down_post/pallas_call | solution.py:452
  22.8 10.1 %all-to-all-start.1 = ((f32[16,2,8,128]{3,2,1,0:T(8,128)}), f32[16,2,8,128]{3,2,1,0:T(8,128)S(1)}, u32[]{:S(2)}, u32[]{:S(2)}) async-start(f32[16,2,8,128]{3,2,1,0:T(8,128)} %get-tuple-element.60), calls=%async_computation.1 | async-start | bytes 262144 | tf_op jit(solution)/shard_map/all_to_all | solution.py:859
  32.9 0.7 %collective-permute-start.4 = (f32[36,8,128]{2,1,0:T(8,128)}, f32[36,8,128]{2,1,0:T(8,128)S(1)}, u32[]{:S(2)}, u32[]{:S(2)}) collective-permute-start(f32[36,8,128]{2,1,0:T(8,128)} %get-tuple-element.61), channel_id=1, source_target_pairs={{4,8},{12,24},{28,16},{20,21},{17,29},{25,13},{9,5},{1,2},{6,10},{... | collective-permute-start | bytes 442376 | tf_op jit(solution)/shard_map/ppermute | solution.py:858
  33.6 3.3 %collective-permute-start.3 = (f32[36,8,128]{2,1,0:T(8,128)}, f32[36,8,128]{2,1,0:T(8,128)S(1)}, u32[]{:S(2)}, u32[]{:S(2)}) collective-permute-start(f32[36,8,128]{2,1,0:T(8,128)} %get-tuple-element.61), channel_id=1, source_target_pairs={{0,4},{8,12},{24,28},{16,20},{21,17},{29,25},{13,9},{5,1},{2,6},{1... | collective-permute-start | bytes 442376 | tf_op jit(solution)/shard_map/ppermute | solution.py:857
  36.9 4.1 %all-to-all-done.1.mine = f32[16,2,8,128]{3,2,1,0:T(8,128)S(1)} async-done(((f32[16,2,8,128]{3,2,1,0:T(8,128)}), f32[16,2,8,128]{3,2,1,0:T(8,128)S(1)}, u32[]{:S(2)}, u32[]{:S(2)}) %all-to-all-start.1) | async-done | bytes 131104 | tf_op jit(solution)/shard_map/all_to_all | solution.py:859
  41.1 0.0 collective-permute-start.2
  41.1 1.3 %collective-permute-done.2.other = f32[16,2,8,128]{3,2,1,0:T(8,128)S(1)} collective-permute-done((f32[16,2,8,128]{3,2,1,0:T(8,128)S(1)}, f32[16,2,8,128]{3,2,1,0:T(8,128)S(1)}, u32[]{:S(2)}, u32[]{:S(2)}) %collective-permute-start.2) | collective-permute-done | bytes 131104 | tf_op jit(solution)/shard_map/ppermute | solution.py:860
  42.4 2.8 %coarse.1.e_two = f32[6,8,128]{2,1,0:T(8,128)S(1)} custom-call(f32[16,2,8,128]{3,2,1,0:T(8,128)S(1)} %all-to-all-done.1.mine, f32[16,2,8,128]{3,2,1,0:T(8,128)S(1)} %collective-permute-done.2.other), custom_call_target="tpu_custom_call" | custom-call | tf_op jit(solution)/shard_map/coarse/pallas_call | solution.py:740
  45.2 0.0 collective-permute-done.4.rim_odd
  45.2 0.0 collective-permute-done.3.rim_even
  45.2 1.2 %up_strokes.1 = f32[8,64,128]{2,1,0:T(8,128)S(1)} custom-call(f32[6,8,128]{2,1,0:T(8,128)S(1)} %coarse.1.e_two, f32[36,8,128]{2,1,0:T(8,128)S(1)} %collective-permute-done.3.rim_even, f32[36,8,128]{2,1,0:T(8,128)S(1)} %collective-permute-done.4.rim_odd, f32[3,8,4,8,128]{4,3,2,1,0:T(8,128)S(1)} %to_slab.1.own, ...), custom_call_target="tpu_custom_call" | custom-call | tf_op jit(solution)/shard_map/up_strokes/pallas_call | solution.py:452
  46.4 9.3 %all_to_all.16.in_ref = f32[8,64,128]{2,1,0:T(8,128)S(1)} all-to-all(f32[8,64,128]{2,1,0:T(8,128)S(1)} %up_strokes.1), channel_id=1, replica_groups=mesh['gx'=4,'gy'=2,'gz'=4] {'gx','gy'}, dimensions={0} | all-to-all | bytes 524288 | tf_op jit(solution)/shard_map/all_to_all | solution.py:863
  55.7 1.1 %unpack.1 = (f32[8,32,128]{2,1,0:T(8,128)}, f32[8,32,128]{2,1,0:T(8,128)}) custom-call(f32[8,64,128]{2,1,0:T(8,128)S(1)} %all_to_all.16.in_ref), custom_call_target="tpu_custom_call" | custom-call | tf_op jit(solution)/shard_map/unpack/pallas_call | solution.py:831
Async XLA Ops:
  16.3 3.1 %collective-permute-start.1 = (f32[3,8,4,8,128]{4,3,2,1,0:T(8,128)S(1)}, f32[3,8,4,8,128]{4,3,2,1,0:T(8,128)S(1)}, u32[]{:S(2)}, u32[]{:S(2)}) collective-permute-start(f32[3,8,4,8,128]{4,3,2,1,0:T(8,128)S(1)} %to_slab.1.own), channel_id=1, source_target_pairs={{4,8},{12,24},{28,16},{20,21},{17,29},{25,13},{9,5},{1,2},{6,10},{... | collective-permute-start | bytes 1179656 | tf_op jit(solution)/shard_map/ppermute | solution.py:852
  17.0 3.3 %collective-permute-start = (f32[3,8,4,8,128]{4,3,2,1,0:T(8,128)S(1)}, f32[3,8,4,8,128]{4,3,2,1,0:T(8,128)S(1)}, u32[]{:S(2)}, u32[]{:S(2)}) collective-permute-start(f32[3,8,4,8,128]{4,3,2,1,0:T(8,128)S(1)} %to_slab.1.own), channel_id=1, source_target_pairs={{0,4},{8,12},{24,28},{16,20},{21,17},{29,25},{13,9},{5,1},{2,6},{1... | collective-permute-start | bytes 1179656 | tf_op jit(solution)/shard_map/ppermute | solution.py:851
  22.8 18.3 %all-to-all-start.1 = ((f32[16,2,8,128]{3,2,1,0:T(8,128)}), f32[16,2,8,128]{3,2,1,0:T(8,128)S(1)}, u32[]{:S(2)}, u32[]{:S(2)}) async-start(f32[16,2,8,128]{3,2,1,0:T(8,128)} %get-tuple-element.60), calls=%async_computation.1 | async-start | bytes 262144 | tf_op jit(solution)/shard_map/all_to_all | solution.py:859
  32.9 12.3 %collective-permute-start.4 = (f32[36,8,128]{2,1,0:T(8,128)}, f32[36,8,128]{2,1,0:T(8,128)S(1)}, u32[]{:S(2)}, u32[]{:S(2)}) collective-permute-start(f32[36,8,128]{2,1,0:T(8,128)} %get-tuple-element.61), channel_id=1, source_target_pairs={{4,8},{12,24},{28,16},{20,21},{17,29},{25,13},{9,5},{1,2},{6,10},{... | collective-permute-start | bytes 442376 | tf_op jit(solution)/shard_map/ppermute | solution.py:858
  33.6 11.6 %collective-permute-start.3 = (f32[36,8,128]{2,1,0:T(8,128)}, f32[36,8,128]{2,1,0:T(8,128)S(1)}, u32[]{:S(2)}, u32[]{:S(2)}) collective-permute-start(f32[36,8,128]{2,1,0:T(8,128)} %get-tuple-element.61), channel_id=1, source_target_pairs={{0,4},{8,12},{24,28},{16,20},{21,17},{29,25},{13,9},{5,1},{2,6},{1... | collective-permute-start | bytes 442376 | tf_op jit(solution)/shard_map/ppermute | solution.py:857
  41.1 1.3 %collective-permute-start.2 = (f32[16,2,8,128]{3,2,1,0:T(8,128)S(1)}, f32[16,2,8,128]{3,2,1,0:T(8,128)S(1)}, u32[]{:S(2)}, u32[]{:S(2)}) collective-permute-start(f32[16,2,8,128]{3,2,1,0:T(8,128)S(1)} %all-to-all-done.1.mine), channel_id=1, source_target_pairs={{0,4},{4,0},{1,5},{5,1},{2,6},{6,2},{3,7},{7,3},{8,12},{12,8},{9,1... | collective-permute-start | bytes 393224 | tf_op jit(solution)/shard_map/ppermute | solution.py:860

commit v4 on v3

--- a/solution.py
+++ b/solution.py
@@ -180,6 +180,8 @@
 
 
 GX, GY, GZ = 4, 2, 4
+COUNT = GX * GY * GZ
+RIM = 28
 BLOCK = (8, 32, 128)
 RING = ("gx", "gy")
 ALL = ("gx", "gy", "gz")
@@ -230,14 +232,19 @@
 
 def regroup(tiles, axis, width, ids):
     move = lanes if axis == 1 else rows
-    low = (ids // width) % 2 == 0
-    high = (ids // (2 * width)) % 2 == 0
+    group = ids // width % 4
+    odd, upper = group % 2 == 1, group >= 2
     a, b, c, d = tiles
-    a, b = jnp.where(low, a, move(b, width)), jnp.where(low, move(a, -width), b)
-    c, d = jnp.where(low, c, move(d, width)), jnp.where(low, move(c, -width), d)
-    a, c = jnp.where(high, a, move(c, 2 * width)), jnp.where(high, move(a, -2 * width), c)
-    b, d = jnp.where(high, b, move(d, 2 * width)), jnp.where(high, move(b, -2 * width), d)
-    return [a, b, c, d]
+    turned = move(jnp.where(odd, a, b), width)
+    a, b = jnp.where(odd, turned, a), jnp.where(odd, b, turned)
+    turned = move(jnp.where(odd, c, d), width)
+    c, d = jnp.where(odd, turned, c), jnp.where(odd, d, turned)
+    turned = move(jnp.where(upper, a, c), 2 * width)
+    a, c = jnp.where(upper, turned, a), jnp.where(upper, c, turned)
+    turned = move(jnp.where(upper, b, d), 2 * width)
+    own = jnp.where(upper, d, b)
+    inner = odd != upper
+    return [a, jnp.where(inner, own, turned), c, jnp.where(inner, turned, own)]
 
 
 def depth_of(k, group):
@@ -275,10 +282,49 @@
     )(fields)
 
 
-def slab_kernel(in_ref, out_ref):
+def shape_of(*dims):
+    return jax.ShapeDtypeStruct(dims + TILE, jnp.float32)
+
+
+def scratch(*dims):
+    return pltpu.VMEM(dims + TILE, jnp.float32)
+
+
+def halo_masks():
+    x, y, z = position()
+    chunk = chunk_of(x, y, z)
+    half = lane_ids() // 64
+    return chunk, (half + chunk % 2) == 1
+
+
+PLACE = [(r, True) for r in range(6)] + [(4, False), (5, False), (3, False), (2, False), (1, False), (0, False)]
+PLACE += [(6, False), (6, True)]
+FIRST_TILE = (0, 6, 13)
+MESSAGE = 19
+
+
+def message(planes, near, count):
+    tiles = [jnp.where(near, planes[t], planes[t + 4]) for t in range(4)]
+    tiles += [jnp.where(near, planes[t], lanes(planes[t + 2], 64)) for t in (4, 5)]
+    if count == 7:
+        tiles.append(jnp.where(near, lanes(planes[2], 64), planes[3]))
+    return tiles
+
+
+def halo_plane(even, odd, a, r, from_even):
+    tile, moved = PLACE[r]
+    tile = FIRST_TILE[a] + tile
+    if moved:
+        return lanes(jnp.where(from_even, odd[tile], even[tile]), 64)
+    return jnp.where(from_even, even[tile], odd[tile])
+
+
+def slab_kernel(in_ref, out_ref, even_ref, odd_ref):
     lane, row = lane_ids(), row_ids()
     low = (lane // 32) % 2 == 0
+    _, from_even = halo_masks()
     for a in range(3):
+        planes = [None] * 8
         for k in range(4):
             part = ([], [])
             for x in range(GX):
@@ -287,16 +333,21 @@
                 part[0].append(jnp.where(low, first, lanes(second, 32)))
                 part[1].append(jnp.where(low, lanes(first, -32), second))
             for pp in range(2):
-                for xv, tile in enumerate(regroup(part[pp], 0, 2, row)):
-                    out_ref[a, k + 4 * pp, xv] = tile
+                planes[k + 4 * pp] = jnp.stack(regroup(part[pp], 0, 2, row))
+                out_ref[a, k + 4 * pp] = planes[k + 4 * pp]
+        count = 7 if a == 1 else 6
+        for near, ref in ((from_even, even_ref), (~from_even, odd_ref)):
+            for t, tile in enumerate(message(planes, near, count)):
+                ref[FIRST_TILE[a] + t] = tile
 
 
 def to_slab(received):
+    vmem = pl.BlockSpec(memory_space=pltpu.VMEM)
     return pl.pallas_call(
         slab_kernel,
-        out_shape=shape_of(3, 8, 4),
-        in_specs=[pl.BlockSpec(memory_space=pltpu.VMEM)],
-        out_specs=pl.BlockSpec(memory_space=pltpu.VMEM),
+        out_shape=[shape_of(3, 8, 4), shape_of(MESSAGE, 4), shape_of(MESSAGE, 4)],
+        in_specs=[vmem],
+        out_specs=[vmem] * 3,
         compiler_params=pltpu.CompilerParams(vmem_limit_bytes=4 * 2**20),
         name="to_slab",
     )(received)
@@ -424,27 +475,12 @@
     return restrict_pair(fine[:, 0], fine[:, 1], dup)
 
 
-def halo_masks():
-    x, y, z = position()
-    chunk = chunk_of(x, y, z)
-    half = lane_ids() // 64
-    return chunk, (half + chunk % 2) == 1
-
-
 def ends_factor():
     x, y, z = position()
     slab = 8 * z + chunk_of(x, y, z)
     half = lane_ids() // 64
     end = ((half == 0) & (slab == 0)) | ((half == 1) & (slab == 8 * GZ - 1))
     return jnp.where(end, 0.0, 1.0)
-
-
-def shape_of(*dims):
-    return jax.ShapeDtypeStruct(dims + TILE, jnp.float32)
-
-
-def scratch(*dims):
-    return pltpu.VMEM(dims + TILE, jnp.float32)
 
 
 def call(kernel, name, operands, out_shape, scratch_shapes, hbm_outputs=0):
@@ -496,23 +532,19 @@
     beta1_own, alpha1_own, mid, (beta_s, alpha_s, beta1_s, alpha1_s) = refs[0], refs[1], refs[2:12], refs[12:]
     _, from_even = halo_masks()
     zero, one = coefficient_planes(None, mid)
-    for p in range(16):
-        alpha_s[p], beta_s[p] = (halo_plane(even.at[a], odd.at[a], p, 16, from_even) for a in range(2))
+    for p in range(2, 16):
+        beta_s[p] = halo_plane(even, odd, 1, 15 - p, from_even)
+        if p >= 4:
+            alpha_s[p] = halo_plane(even, odd, 0, 15 - p, from_even)
     beta, alpha = Planes((0, beta_s), (16, own.at[1])), Planes((0, alpha_s), (16, own.at[0]))
     ends = ends_factor()
     level_coefficients(beta, alpha, 4, 17, SHIFT_BASE, 1, *zero, ends, 16, COEF_SPAN)
     beta_one, alpha_one = Planes((0, beta1_s), (8, beta1_own)), Planes((0, alpha1_s), (8, alpha1_own))
-    for p, q in spans(0, 8, 2):
-        beta_one.put(p, 0.125 * restrict(beta.get, p, q, 1))
-        alpha_one.put(p, 0.125 * restrict(alpha.get, p, q, 1))
+    for p in range(1, 8):
+        beta_one.put(p, 0.125 * restrict(beta.get, p, p + 1, 1))
+        if p >= 2:
+            alpha_one.put(p, 0.125 * restrict(alpha.get, p, p + 1, 1))
     level_coefficients(beta_one, alpha_one, 2, 9, SHIFT_BASE * 4.0, 2, *one, ends, 8, COEF_SPAN1)
-
-
-def halo_plane(even, odd, p, count, from_even):
-    if p < count // 2:
-        return jnp.where(from_even, even[p], odd[p])
-    k = count - 1 - p
-    return lanes(jnp.where(from_even, odd[k], even[k]), 64)
 
 
 def post_kernel(own, even, odd, *refs):
@@ -525,7 +557,7 @@
     coeffs, dinv, diag = zero[:3], zero[3], zero[4]
     b = Planes((4, halo_b), (16, own.at[2]))
     for p in range(4, 16):
-        b.put(p, halo_plane(even.at[2], odd.at[2], p, 16, from_even)[None])
+        b.put(p, halo_plane(even, odd, 2, 15 - p, from_even)[None])
     factors = chebyshev_factors(SWEEPS, SMOOTH_LOWER)
     iterates = [
         None,
@@ -557,13 +589,19 @@
     b_two = 0.5 * restrict(residual(w, b_one, diag, coeffs, 2), 4, 6, 2)
     beta_two = 0.125 * restrict(Planes((8, beta1)).get, 4, 6, 2)
     alpha_two = 0.125 * restrict(Planes((8, alpha1)).get, 4, 6, 2)
-    tile_s[...] = jnp.where(lane % 4 == 0, b_two, jnp.where(lane % 4 == 1, beta_two, alpha_two))[:, 0]
-    copies += [pltpu.make_async_copy(tile_s, gather.at[n], sent.at[n + 1]) for n in range(GX * GZ)]
+    slot = lane % 4
+    both = jnp.where(slot < 2, *(jnp.where(slot % 2 == 0, field[0, 0], field[1, 0]) for field in (b_two, beta_two)))
+    last = jnp.where(slot % 2 == 0, alpha_two[0, 0], alpha_two[1, 0])
+    last = jnp.where(slot[:4] < 2, last[:4], last[4:])
+    for n in range(2):
+        for i, part in enumerate((both[:4], both[4:], last)):
+            tile_s[n, i] = part
+    copies += [pltpu.make_async_copy(tile_s, gather.at[n : n + 2], sent.at[n + 1]) for n in range(0, COUNT, 2)]
     for copy in copies[1:]:
         copy.start()
     u1[...] = w.get(8, PLANES1)
     rim_s[20:28] = jnp.where(lane % 2 == 0, w.get(8, PLANES1), b_one.get(8, PLANES1)).reshape((8,) + TILE)
-    copies.append(pltpu.make_async_copy(rim_s.at[20:28], rim.at[20:28], sent.at[GX * GZ + 1]))
+    copies.append(pltpu.make_async_copy(rim_s.at[20:28], rim.at[20:28], sent.at[COUNT + 1]))
     copies[-1].start()
     for copy in copies:
         copy.wait()
@@ -582,12 +620,13 @@
 
 
 def down_post(own, even, odd, pre, mid):
-    shapes = [(GX * GZ, 2), (36,), (12, 4), (13, 4), (4, 2), (4, 2)]
+    shapes = [shape_of(*n) for n in ((RIM,), (12, 4), (13, 4), (4, 2), (4, 2))]
     return call(
-        post_kernel, "down_post", (own, even, odd, *pre, *mid), [shape_of(*n) for n in shapes],
+        post_kernel, "down_post", (own, even, odd, *pre, *mid),
+        [jax.ShapeDtypeStruct((COUNT, 3, 4, 128), jnp.float32), *shapes],
         [
             scratch(13, 4), scratch(13, 4), scratch(13, 4), scratch(4, 2), scratch(13, 2), scratch(13, 2),
-            scratch(2), scratch(28), pltpu.SemaphoreType.DMA((GX * GZ + 2,)),
+            pltpu.VMEM((2, 3, 4, 128), jnp.float32), scratch(28), pltpu.SemaphoreType.DMA((COUNT + 2,)),
         ],
         hbm_outputs=2,
     )
@@ -600,29 +639,28 @@
     return jnp.where(half == 0, before, after), turned
 
 
-def coarse_kernel(mine, other, out, cores, e2_s):
+def coarse_kernel(gathered, out, tiles_s, e2_s):
     lane, row = lane_ids(), row_ids()
     half = lane // 64
     x, y, z = position()
-    cores[y] = mine[...]
-    cores[1 - y] = other[...]
-
-    def collect(f):
-        planes = []
-        for p in range(2):
-            tiles = []
-            for group in range(8):
-                tile = None
-                for q in range(GZ):
-                    natural = 7 - group if q % 2 else group
-                    rank, core = natural // 2, natural % 2
-                    piece = lanes(cores[core, (rank ^ (rank >> 1)) * GZ + q, p], q - f)
-                    tile = piece if tile is None else jnp.where(lane % 4 == q, piece, tile)
-                tiles.append(tile)
-            planes.append(jnp.stack(tiles))
-        return planes
-
-    b_two, beta_two, alpha_two = collect(0), collect(1), collect(2)
+    for n in range(COUNT):
+        tiles_s[n, 0] = jnp.concatenate([gathered[n, 0], gathered[n, 1]], axis=0)
+        tiles_s[n, 1] = jnp.concatenate([gathered[n, 2], lanes(gathered[n, 2], -2)], axis=0)
+
+    def collect(tile, slot):
+        out = []
+        for group in range(8):
+            joined = None
+            for q in range(GZ):
+                natural = 7 - group if q % 2 else group
+                rank, core = natural // 2, natural % 2
+                n = ((rank ^ (rank >> 1)) * GY + core) * GZ + q
+                piece = tiles_s[n, tile] if q == slot else lanes(tiles_s[n, tile], q - slot)
+                joined = piece if joined is None else jnp.where(lane % 4 == q, piece, joined)
+            out.append(joined)
+        return jnp.stack(out)
+
+    b_two, beta_two, alpha_two = ([collect(tile, slot + p) for p in range(2)] for tile, slot in ((0, 0), (0, 2), (1, 0)))
     slab = lax.broadcasted_iota(jnp.int32, (8,) + TILE, 0)
     end = ((slab == 0) & (lane % 4 == 0) & (half == 0)) | ((slab == 7) & (lane % 4 == 3) & (half == 1))
 
@@ -735,17 +773,17 @@
     out[5] = here[1]
 
 
-def coarse(mine, other):
+def coarse(gathered):
     vmem = pl.BlockSpec(memory_space=pltpu.VMEM)
     return pl.pallas_call(
         coarse_kernel,
         out_shape=shape_of(6),
-        in_specs=[vmem] * 2,
+        in_specs=[vmem],
         out_specs=vmem,
-        scratch_shapes=[scratch(2, GX * GZ, 2), scratch(8, 2)],
+        scratch_shapes=[scratch(COUNT, 2), scratch(8, 2)],
         compiler_params=pltpu.CompilerParams(vmem_limit_bytes=8 * 2**20),
         name="coarse",
-    )(mine, other)
+    )(gathered)
 
 
 def up_kernel(e_two, rim_even, rim_odd, own, halo_b, late, u1, b1, v4, *refs):
@@ -847,19 +885,17 @@
 def slab_shards(right_side, alpha_coef, beta_coef):
     even_pairs, odd_pairs = swap_pairs(False), swap_pairs(True)
     packed = pack(jnp.stack([alpha_coef, beta_coef, right_side]))
-    own = to_slab(lax.all_to_all(packed, RING, 0, 0))
-    even = lax.ppermute(own, ALL, even_pairs)
-    odd = lax.ppermute(own, ALL, odd_pairs)
+    own, to_even, to_odd = to_slab(lax.all_to_all(packed, RING, 0, 0))
+    even = lax.ppermute(to_even, ALL, even_pairs)
+    odd = lax.ppermute(to_odd, ALL, odd_pairs)
     found = down_pre(own)
     pre, alpha1, beta1, v4 = found[:10], found[10], found[11], found[15]
     mid = down_mid(own, even, odd, beta1, alpha1)
     gather, rim, halo_b, late, u1, b1 = down_post(own, even, odd, found, mid)
     rim_even = lax.ppermute(rim, ALL, even_pairs)
     rim_odd = lax.ppermute(rim, ALL, odd_pairs)
-    mine = lax.all_to_all(gather, ("gx", "gz"), 0, 0)
-    other = lax.ppermute(mine, "gy", [(0, 1), (1, 0)])
     kept = (own, halo_b, late, u1, b1, v4, *pre, *mid)
-    result = up(coarse(mine, other), rim_even, rim_odd, *kept)
+    result = up(coarse(lax.all_to_all(gather, ALL, 0, 0)), rim_even, rim_odd, *kept)
     return tuple(unpack(lax.all_to_all(result, RING, 0, 0)))
 
 

time: 57.2 us -> 55.1 us (0.963)
  starting transfers between devices: 16.8 us -> 15.3 us
    ppermute x3 -> x2, starting transfers between devices: 2.65 us -> 0.75 us  [the longest x1 0.68 us: slab_shards(): odd = lax.ppermute(to_odd, ALL, odd_pairs)]
    ppermute x3 -> x2, waiting for transfers between devices: 2.23 us -> 0.45 us  [the longest x1 0.45 us: slab_shards(): even = lax.ppermute(to_even, ALL, even_pairs)]
    all_to_all x1, waiting for transfers between devices: 4.14 us -> 5.47 us  [slab_shards(): lax.all_to_all(gather, ALL, 0, 0)]
    all_to_all x1, starting transfers between devices: 10.1 us -> 10.7 us  [slab_shards(): lax.all_to_all(gather, ALL, 0, 0)]
  transfers between devices with their start and end apart: 6 -> 5, of which waited for: 3 -> 2; matrix products, arithmetic and copies ran while one was open for 0% -> 0% of each run, Pallas kernels for 6% -> 6%
where the time goes in v4:
time: 55.1 us; the launch traced here: 54.8 us
  blocking collectives  22.7 us (41%)
  starting transfers between devices  15.3 us (28%)
  Pallas kernels  9.19 us (17%)
  waiting for transfers between devices  5.92 us (11%)
  other arithmetic  1.06 us (2%)
  between operations  0.7 us (1%)
    all_to_all x1, blocking collectives, slab_shards(): own, to_even, to_odd = to_slab(lax.all_to_all(packed, RING, 0, 0))  13.3 us
    all_to_all x1, starting transfers between devices, slab_shards(): lax.all_to_all(gather, ALL, 0, 0)  10.7 us
    all_to_all x1, blocking collectives, slab_shards(): return tuple(unpack(lax.all_to_all(result, RING, 0, 0)))  9.35 us
    all_to_all x1, waiting for transfers between devices, slab_shards(): lax.all_to_all(gather, ALL, 0, 0)  5.47 us
    pallas_call x4, Pallas kernels, call(): pl.pallas_call(kernel, out_shape=out_shape, in_specs=[vmem] * len(operand...  4.26 us
    ppermute x1, starting transfers between devices, slab_shards(): rim_even = lax.ppermute(rim, ALL, even_pairs)  3.19 us
    pallas_call x1, Pallas kernels, coarse(): pl.pallas_call(coarse_kernel, out_shape=shape_of(6), in_specs=[vmem], out...  2.84 us
    pallas_call x1, Pallas kernels, unpack(): pl.pallas_call(unpack_kernel, out_shape=[jax.ShapeDtypeStruct(BLOCK, jnp....  1.12 us
  transfers between devices with their start and end apart: 5, of which 2 were waited for; matrix products, arithmetic and copies ran while one was open for 0% of the time, Pallas kernels for 6%

profile of v4, /device:TPU:0, one launch (start us, length us, event | category | flops | bytes accessed | tf_op | source)
XLA Modules:
  0.0 54.8 jit_solution(15596595879375367725)
XLA Ops:
  0.6 1.1 %pad_maximum_fusion.fields = f32[3,8,32,128]{3,2,1,0:T(8,128)S(1)} fusion(f32[1,8,32,128]{3,2,1,0:T(8,128)} %bitcast.3, f32[1,8,32,128]{3,2,1,0:T(8,128)} %bitcast.4, f32[1,8,32,128]{3,2,1,0:T(8,128)} %bitcast.5), kind=kLoop, calls=%fused_computation | loop fusion | flops 196608 | bytes 786432 | tf_op jit(solution)/shard_map/stack | solution.py:887
  1.7 0.7 %pack.1 = f32[8,96,128]{2,1,0:T(8,128)S(1)} custom-call(f32[3,8,32,128]{3,2,1,0:T(8,128)S(1)} %pad_maximum_fusion.fields), custom_call_target="tpu_custom_call" | custom-call | tf_op jit(solution)/shard_map/pack/pallas_call | solution.py:274
  2.4 13.3 %all_to_all.15.in_ref = f32[8,96,128]{2,1,0:T(8,128)S(1)} all-to-all(f32[8,96,128]{2,1,0:T(8,128)S(1)} %pack.1), channel_id=1, replica_groups=mesh['gx'=4,'gy'=2,'gz'=4] {'gx','gy'}, dimensions={0} | all-to-all | bytes 786432 | tf_op jit(solution)/shard_map/all_to_all | solution.py:888
  15.7 0.3 to_slab.1
  16.0 0.1 collective-permute-start
  16.1 0.7 %collective-permute-start.1 = (f32[19,4,8,128]{3,2,1,0:T(8,128)S(1)}, f32[19,4,8,128]{3,2,1,0:T(8,128)S(1)}, u32[]{:S(2)}, u32[]{:S(2)}) collective-permute-start(f32[19,4,8,128]{3,2,1,0:T(8,128)S(1)} %get-tuple-element.39), channel_id=1, source_target_pairs={{4,8},{12,24},{28,16},{20,21},{17,29},{25,13},{9,5},{1,2},{6,10},{... | collective-permute-start | bytes 933896 | tf_op jit(solution)/shard_map/ppermute | solution.py:890
  16.7 0.5 down_pre.1
  17.2 0.4 collective-permute-done.even
  17.6 0.0 collective-permute-done.1.odd
  17.6 0.4 down_mid.1
  18.0 2.2 %down_post.1 = (f32[32,3,4,128]{3,2,1,0:T(4,128)}, f32[28,8,128]{2,1,0:T(8,128)}, f32[12,4,8,128]{3,2,1,0:T(8,128)S(1)}, f32[13,4,8,128]{3,2,1,0:T(8,128)S(1)}, ...) custom-call(f32[3,8,4,8,128]{4,3,2,1,0:T(8,128)S(1)} %get-tuple-element.37.own, ...), custom_call_target="tpu_custom_call" | custom-call | tf_op jit(solution)/shard_map/down_post/pallas_call | solution.py:488
  20.3 10.7 %all-to-all-start.1 = ((f32[32,3,4,128]{3,2,1,0:T(4,128)}), f32[32,3,4,128]{3,2,1,0:T(4,128)S(1)}, u32[]{:S(2)}, u32[]{:S(2)}) async-start(f32[32,3,4,128]{3,2,1,0:T(4,128)} %get-tuple-element.66), calls=%async_computation.1 | async-start | bytes 393216 | tf_op jit(solution)/shard_map/all_to_all | solution.py:898
  31.0 0.7 %collective-permute-start.3 = (f32[28,8,128]{2,1,0:T(8,128)}, f32[28,8,128]{2,1,0:T(8,128)S(1)}, u32[]{:S(2)}, u32[]{:S(2)}) collective-permute-start(f32[28,8,128]{2,1,0:T(8,128)} %get-tuple-element.67), channel_id=1, source_target_pairs={{4,8},{12,24},{28,16},{20,21},{17,29},{25,13},{9,5},{1,2},{6,10},{... | collective-permute-start | bytes 344072 | tf_op jit(solution)/shard_map/ppermute | solution.py:896
  31.6 3.2 %collective-permute-start.2 = (f32[28,8,128]{2,1,0:T(8,128)}, f32[28,8,128]{2,1,0:T(8,128)S(1)}, u32[]{:S(2)}, u32[]{:S(2)}) collective-permute-start(f32[28,8,128]{2,1,0:T(8,128)} %get-tuple-element.67), channel_id=1, source_target_pairs={{0,4},{8,12},{24,28},{16,20},{21,17},{29,25},{13,9},{5,1},{2,6},{1... | collective-permute-start | bytes 344072 | tf_op jit(solution)/shard_map/ppermute | solution.py:895
  34.8 5.5 %all-to-all-done.1.gathered = f32[32,3,4,128]{3,2,1,0:T(4,128)S(1)} async-done(((f32[32,3,4,128]{3,2,1,0:T(4,128)}), f32[32,3,4,128]{3,2,1,0:T(4,128)S(1)}, u32[]{:S(2)}, u32[]{:S(2)}) %all-to-all-start.1) | async-done | bytes 196640 | tf_op jit(solution)/shard_map/all_to_all | solution.py:898
  40.3 2.8 %coarse.1.e_two = f32[6,8,128]{2,1,0:T(8,128)S(1)} custom-call(f32[32,3,4,128]{3,2,1,0:T(4,128)S(1)} %all-to-all-done.1.gathered), custom_call_target="tpu_custom_call" | custom-call | tf_op jit(solution)/shard_map/coarse/pallas_call | solution.py:778
  43.1 0.0 collective-permute-done.3.rim_odd
  43.1 0.0 collective-permute-done.2.rim_even
  43.1 1.2 %up_strokes.1 = f32[8,64,128]{2,1,0:T(8,128)S(1)} custom-call(f32[6,8,128]{2,1,0:T(8,128)S(1)} %coarse.1.e_two, f32[28,8,128]{2,1,0:T(8,128)S(1)} %collective-permute-done.2.rim_even, f32[28,8,128]{2,1,0:T(8,128)S(1)} %collective-permute-done.3.rim_odd, f32[3,8,4,8,128]{4,3,2,1,0:T(8,128)S(1)} %get-tuple-element.37.own, ...), custom_call_target="tpu_custom_call" | custom-call | tf_op jit(solution)/shard_map/up_strokes/pallas_call | solution.py:488
  44.3 9.3 %all_to_all.16.in_ref = f32[8,64,128]{2,1,0:T(8,128)S(1)} all-to-all(f32[8,64,128]{2,1,0:T(8,128)S(1)} %up_strokes.1), channel_id=1, replica_groups=mesh['gx'=4,'gy'=2,'gz'=4] {'gx','gy'}, dimensions={0} | all-to-all | bytes 524288 | tf_op jit(solution)/shard_map/all_to_all | solution.py:899
  53.7 1.1 %unpack.1 = (f32[8,32,128]{2,1,0:T(8,128)}, f32[8,32,128]{2,1,0:T(8,128)}) custom-call(f32[8,64,128]{2,1,0:T(8,128)S(1)} %all_to_all.16.in_ref), custom_call_target="tpu_custom_call" | custom-call | tf_op jit(solution)/shard_map/unpack/pallas_call | solution.py:869
Async XLA Ops:
  16.0 1.7 %collective-permute-start = (f32[19,4,8,128]{3,2,1,0:T(8,128)S(1)}, f32[19,4,8,128]{3,2,1,0:T(8,128)S(1)}, u32[]{:S(2)}, u32[]{:S(2)}) collective-permute-start(f32[19,4,8,128]{3,2,1,0:T(8,128)S(1)} %get-tuple-element.38), channel_id=1, source_target_pairs={{0,4},{8,12},{24,28},{16,20},{21,17},{29,25},{13,9},{5,1},{2,6},{1... | collective-permute-start | bytes 933896 | tf_op jit(solution)/shard_map/ppermute | solution.py:889
  16.1 1.6 %collective-permute-start.1 = (f32[19,4,8,128]{3,2,1,0:T(8,128)S(1)}, f32[19,4,8,128]{3,2,1,0:T(8,128)S(1)}, u32[]{:S(2)}, u32[]{:S(2)}) collective-permute-start(f32[19,4,8,128]{3,2,1,0:T(8,128)S(1)} %get-tuple-element.39), channel_id=1, source_target_pairs={{4,8},{12,24},{28,16},{20,21},{17,29},{25,13},{9,5},{1,2},{6,10},{... | collective-permute-start | bytes 933896 | tf_op jit(solution)/shard_map/ppermute | solution.py:890
  20.3 20.0 %all-to-all-start.1 = ((f32[32,3,4,128]{3,2,1,0:T(4,128)}), f32[32,3,4,128]{3,2,1,0:T(4,128)S(1)}, u32[]{:S(2)}, u32[]{:S(2)}) async-start(f32[32,3,4,128]{3,2,1,0:T(4,128)} %get-tuple-element.66), calls=%async_computation.1 | async-start | bytes 393216 | tf_op jit(solution)/shard_map/all_to_all | solution.py:898
  31.0 12.2 %collective-permute-start.3 = (f32[28,8,128]{2,1,0:T(8,128)}, f32[28,8,128]{2,1,0:T(8,128)S(1)}, u32[]{:S(2)}, u32[]{:S(2)}) collective-permute-start(f32[28,8,128]{2,1,0:T(8,128)} %get-tuple-element.67), channel_id=1, source_target_pairs={{4,8},{12,24},{28,16},{20,21},{17,29},{25,13},{9,5},{1,2},{6,10},{... | collective-permute-start | bytes 344072 | tf_op jit(solution)/shard_map/ppermute | solution.py:896
  31.6 11.5 %collective-permute-start.2 = (f32[28,8,128]{2,1,0:T(8,128)}, f32[28,8,128]{2,1,0:T(8,128)S(1)}, u32[]{:S(2)}, u32[]{:S(2)}) collective-permute-start(f32[28,8,128]{2,1,0:T(8,128)} %get-tuple-element.67), channel_id=1, source_target_pairs={{0,4},{8,12},{24,28},{16,20},{21,17},{29,25},{13,9},{5,1},{2,6},{1... | collective-permute-start | bytes 344072 | tf_op jit(solution)/shard_map/ppermute | solution.py:895

commit v5 on v4

--- a/solution.py
+++ b/solution.py
@@ -528,8 +528,7 @@
         close(iterates[i], PLANES)
 
 
-def mid_kernel(own, even, odd, *refs):
-    beta1_own, alpha1_own, mid, (beta_s, alpha_s, beta1_s, alpha1_s) = refs[0], refs[1], refs[2:12], refs[12:]
+def mid_part(own, even, odd, beta1_own, alpha1_own, mid, beta_s, alpha_s, beta1_s, alpha1_s):
     _, from_even = halo_masks()
     zero, one = coefficient_planes(None, mid)
     for p in range(2, 16):
@@ -548,9 +547,9 @@
 
 
 def post_kernel(own, even, odd, *refs):
-    pre, (alpha1, beta1, v1, v2, v3, v4), mid = refs[:10], refs[10:16], refs[16:26]
-    gather, rim, halo_b, late, u1, b1 = refs[26:32]
-    f1, f2, f3, b1_s, w_a, w_b, tile_s, rim_s, sent = refs[32:]
+    pre, (alpha1, beta1, v1, v2, v3, v4), (gather, rim, halo_b, late, u1, b1) = refs[:10], refs[10:16], refs[16:22]
+    mid, (f1, f2, f3, b1_s, w_a, w_b, tile_s, rim_s, sent), scratch_mid = refs[22:32], refs[32:41], refs[41:]
+    mid_part(own, even, odd, beta1, alpha1, mid, *scratch_mid)
     lane = lane_ids()
     _, from_even = halo_masks()
     zero, one = coefficient_planes(pre, mid)
@@ -612,21 +611,14 @@
     return call(pre_kernel, "down_pre", (own,), [shape_of(*n) for n in shapes], [scratch(1, 4), scratch(1, 2)])
 
 
-def down_mid(own, even, odd, beta1, alpha1):
+def down_post(own, even, odd, pre):
+    shapes = [shape_of(*n) for n in [(RIM,), (12, 4), (13, 4), (4, 2), (4, 2), *MID_SHAPES]]
     return call(
-        mid_kernel, "down_mid", (own, even, odd, beta1, alpha1), [shape_of(*n) for n in MID_SHAPES],
-        [scratch(16, 4), scratch(16, 4), scratch(8, 2), scratch(8, 2)],
-    )
-
-
-def down_post(own, even, odd, pre, mid):
-    shapes = [shape_of(*n) for n in ((RIM,), (12, 4), (13, 4), (4, 2), (4, 2))]
-    return call(
-        post_kernel, "down_post", (own, even, odd, *pre, *mid),
-        [jax.ShapeDtypeStruct((COUNT, 3, 4, 128), jnp.float32), *shapes],
+        post_kernel, "down_post", (own, even, odd, *pre), [jax.ShapeDtypeStruct((COUNT, 3, 4, 128), jnp.float32), *shapes],
         [
             scratch(13, 4), scratch(13, 4), scratch(13, 4), scratch(4, 2), scratch(13, 2), scratch(13, 2),
             pltpu.VMEM((2, 3, 4, 128), jnp.float32), scratch(28), pltpu.SemaphoreType.DMA((COUNT + 2,)),
+            scratch(16, 4), scratch(16, 4), scratch(8, 2), scratch(8, 2),
         ],
         hbm_outputs=2,
     )
@@ -665,32 +657,31 @@
     end = ((slab == 0) & (lane % 4 == 0) & (half == 0)) | ((slab == 7) & (lane % 4 == 3) & (half == 1))
 
     def sides(beta, dx, dy):
-        x_last, x_first = row >= 8 - dx, row < dx
         place = (lane % 64) // dy
-        y_last, y_first = place == 64 // dy - 1, place == 0
-        by_x = jnp.where(x_last, 0.0, 0.5 * (beta + rows(beta, -dx)))
-        by_y = jnp.where(y_last, 0.0, 0.5 * (beta + lanes(beta, -dy)))
-        rim = jnp.where(x_last | x_first, 0.5, 0.0) + jnp.where(y_last | y_first, 0.5, 0.0)
-        return by_x, by_y, (by_x + rows(by_x, dx)) + (by_y + lanes(by_y, dy)) + beta * rim
-
-    def scaled(by_x, by_y, inv, dx, dy):
-        return by_x * inv, rows(by_x, dx) * inv, by_y * inv, lanes(by_y, dy) * inv
+        rims = row >= 8 - dx, row < dx, place == 64 // dy - 1, place == 0
+        others = rows(beta, -dx), rows(beta, dx), lanes(beta, -dy), lanes(beta, dy)
+        faces = [jnp.where(rim, 0.0, 0.5 * (beta + other)) for rim, other in zip(rims, others)]
+        edge = jnp.where(rims[0] | rims[1], 0.5, 0.0) + jnp.where(rims[2] | rims[3], 0.5, 0.0)
+        return faces, (faces[0] + faces[1]) + (faces[2] + faces[3]) + beta * edge
+
+    def scaled(faces, inv):
+        return [face * inv for face in faces]
 
     def flat(v, coeffs, dx, dy):
         x_above, x_below, y_above, y_below = coeffs
         total = x_above * rows(v, -dx) + x_below * rows(v, dx)
         return total + (y_above * lanes(v, -dy) + y_below * lanes(v, dy))
 
-    x0, y0, s0 = sides(beta_two[0], 1, 4)
-    x1, y1, s1 = sides(beta_two[1], 1, 4)
+    faces_a, sum_a = sides(beta_two[0], 1, 4)
+    faces_b, sum_b = sides(beta_two[1], 1, 4)
     middle = 0.5 * (beta_two[0] + beta_two[1])
     inner = 0.5 * (beta_two[1] + lanes(beta_two[1], 64))
     edge = 0.5 * (beta_two[0] + jnp.where(end, 0.0, outer(beta_two[0], half)[0]))
     shift = SHIFT_BASE * 16.0
-    diag_a = shift * alpha_two[0] + s0 + (middle + edge)
-    diag_b = shift * alpha_two[1] + s1 + (middle + inner)
+    diag_a = shift * alpha_two[0] + sum_a + (middle + edge)
+    diag_b = shift * alpha_two[1] + sum_b + (middle + inner)
     inv_a, inv_b = inverse(diag_a), inverse(diag_b)
-    flat_a, flat_b = scaled(x0, y0, inv_a, 1, 4), scaled(x1, y1, inv_b, 1, 4)
+    flat_a, flat_b = scaled(faces_a, inv_a), scaled(faces_b, inv_b)
     middle_a, middle_b = middle * inv_a, middle * inv_b
     rim_a, inner_b = jnp.where(end, 0.0, edge) * inv_a, inner * inv_b
     rhs_a, rhs_b = b_two[0] * inv_a, b_two[1] * inv_b
@@ -721,17 +712,32 @@
         total = total + jnp.where(row % 2 == 0, rows(total, -1), rows(total, 1))
         return total + jnp.where((lane // 4) % 2 == 0, lanes(total, -4), lanes(total, 4))
 
-    b_low = 0.5 * restrict_whole(diag_a * (rhs_a + ta - ua), diag_b * (rhs_b + tb - ub))
-    beta_low = 0.125 * restrict_whole(beta_two[0], beta_two[1])
-    alpha_low = 0.125 * restrict_whole(alpha_two[0], alpha_two[1])
-
-    x_low, y_low, s_low = sides(beta_low, 2, 8)
-    beyond, turned = outer(beta_low, half)
+    second = (lane // 4) % 2 == 1
+
+    def pack_low(value):
+        return jnp.where(second, value[4:], value[:4])
+
+    def outer_low(value):
+        turned = lanes(value, 64)
+        first_one, last_one = value[:1], value[-1:]
+        before = jnp.where(second, lanes(last_one, 68), lanes(last_one, 61))
+        after = jnp.where(second, lanes(first_one, 67), lanes(first_one, 60))
+        before = jnp.concatenate([before, turned[:-1]], axis=0)
+        after = jnp.concatenate([turned[1:], after], axis=0)
+        return jnp.where(half == 0, before, after), turned
+
+    b_low = 0.5 * pack_low(restrict_whole(diag_a * (rhs_a + ta - ua), diag_b * (rhs_b + tb - ub)))
+    beta_low = 0.125 * pack_low(restrict_whole(beta_two[0], beta_two[1]))
+    alpha_low = 0.125 * pack_low(restrict_whole(alpha_two[0], alpha_two[1]))
+    slab = lax.broadcasted_iota(jnp.int32, (4,) + TILE, 0) + jnp.where(second, 4, 0)
+    end_low = ((slab == 0) & (lane % 4 == 0) & (half == 0)) | ((slab == 7) & (lane % 4 == 3) & (half == 1))
+    faces_low, sum_low = sides(beta_low, 2, 8)
+    beyond, turned = outer_low(beta_low)
     inner_low = 0.5 * (beta_low + turned)
-    edge_low = 0.5 * (beta_low + jnp.where(end, 0.0, beyond))
-    inv_low = inverse(SHIFT_BASE * 64.0 * alpha_low + s_low + (inner_low + edge_low))
-    flat_low = scaled(x_low, y_low, inv_low, 2, 8)
-    rim_low = jnp.where(end, 0.0, edge_low) * inv_low
+    edge_low = 0.5 * (beta_low + jnp.where(end_low, 0.0, beyond))
+    inv_low = inverse(SHIFT_BASE * 64.0 * alpha_low + sum_low + (inner_low + edge_low))
+    flat_low = scaled(faces_low, inv_low)
+    rim_low = jnp.where(end_low, 0.0, edge_low) * inv_low
     inner_low = inner_low * inv_low
     rhs_low = b_low * inv_low
     before = v = None
@@ -739,12 +745,13 @@
         if v is None:
             v = gain * rhs_low
             continue
-        beyond, turned = outer(v, half)
+        beyond, turned = outer_low(v)
         base = (1.0 + carry - gain) * v + gain * rhs_low
         if before is not None:
             base = base - carry * before
         total = flat(v, flat_low, 2, 8) + (inner_low * turned + rim_low * beyond)
         before, v = v, base + gain * total
+    v = jnp.concatenate([jnp.where(second, lanes(v, 4), v), jnp.where(second, v, lanes(v, -4))], axis=0)
     va, vb = sweeps_two(None, (ua + v, ub + v), factors)
     for group in range(8):
         e2_s[group, 0] = va[group]
@@ -753,24 +760,21 @@
     chunk = chunk_of(x, y, z)
     place = 8 * z + chunk
 
-    def fetch(offset):
-        index = jnp.clip(place + offset, 0, 8 * GZ - 1)
-        out = []
-        for p in range(2):
-            tile = pltpu.roll(e2_s[index % 8, p], (128 - index // 8) % 128, 1)
-            tile = jnp.where(lane % 4 == 0, tile, 0.0)
-            tile = tile + lanes(tile, 1)
-            out.append(tile + lanes(tile, 2))
+    def fetch(offset, p, turn=0):
+        index = jnp.clip(place + offset, 0, COUNT - 1)
+        tile, out = e2_s[index % 8, p], None
+        for slot in range(4):
+            piece = pltpu.roll(tile, (128 + slot + turn - index // 8) % 128, 1)
+            out = piece if out is None else jnp.where(lane % 4 == slot, piece, out)
         return out
 
-    below, here, above = fetch(-1), fetch(0), fetch(1)
     first = half == 0
-    out[0] = jnp.where(first, below[0], above[0])
-    out[1] = jnp.where(first, below[1], above[1])
-    out[2] = lanes(jnp.where(first, above[1], below[1]), 64)
-    out[3] = lanes(jnp.where(first, above[0], below[0]), 64)
-    out[4] = here[0]
-    out[5] = here[1]
+    out[0] = jnp.where(first, fetch(-1, 0), fetch(1, 0))
+    out[1] = jnp.where(first, fetch(-1, 1), fetch(1, 1))
+    out[2] = jnp.where(first, fetch(-1, 1, 64), fetch(1, 1, 64))
+    out[3] = jnp.where(first, fetch(-1, 0, 64), fetch(1, 0, 64))
+    out[4] = fetch(0, 0)
+    out[5] = fetch(0, 1)
 
 
 def coarse(gathered):
@@ -889,9 +893,8 @@
     even = lax.ppermute(to_even, ALL, even_pairs)
     odd = lax.ppermute(to_odd, ALL, odd_pairs)
     found = down_pre(own)
-    pre, alpha1, beta1, v4 = found[:10], found[10], found[11], found[15]
-    mid = down_mid(own, even, odd, beta1, alpha1)
-    gather, rim, halo_b, late, u1, b1 = down_post(own, even, odd, found, mid)
+    pre, v4 = found[:10], found[15]
+    gather, rim, halo_b, late, u1, b1, *mid = down_post(own, even, odd, found)
     rim_even = lax.ppermute(rim, ALL, even_pairs)
     rim_odd = lax.ppermute(rim, ALL, odd_pairs)
     kept = (own, halo_b, late, u1, b1, v4, *pre, *mid)

time: 55.1 us -> 54.6 us (level)
    pallas_call x4 -> x3, Pallas kernels: 4.26 us -> 4.11 us  [call(): pl.pallas_call(kernel, out_shape=out_shape, in_specs=[vmem] * len(operand...]
  transfers between devices with their start and end apart: 5 -> 5, of which waited for: 2 -> 2; matrix products, arithmetic and copies ran while one was open for 0% -> 0% of each run, Pallas kernels for 6% -> 5%
where the time goes in v5:
time: 54.6 us; the launch traced here: 54.3 us
  blocking collectives  22.7 us (42%)
  starting transfers between devices  15.3 us (28%)
  Pallas kernels  8.67 us (16%)
  waiting for transfers between devices  5.92 us (11%)
  other arithmetic  1.06 us (2%)
  between operations  0.71 us (1%)
    all_to_all x1, blocking collectives, slab_shards(): own, to_even, to_odd = to_slab(lax.all_to_all(packed, RING, 0, 0))  13.3 us
    all_to_all x1, starting transfers between devices, slab_shards(): lax.all_to_all(gather, ALL, 0, 0)  10.7 us
    all_to_all x1, blocking collectives, slab_shards(): return tuple(unpack(lax.all_to_all(result, RING, 0, 0)))  9.35 us
    all_to_all x1, waiting for transfers between devices, slab_shards(): lax.all_to_all(gather, ALL, 0, 0)  5.47 us
    pallas_call x3, Pallas kernels, call(): pl.pallas_call(kernel, out_shape=out_shape, in_specs=[vmem] * len(operand...  4.11 us
    ppermute x1, starting transfers between devices, slab_shards(): rim_even = lax.ppermute(rim, ALL, even_pairs)  3.19 us
    pallas_call x1, Pallas kernels, coarse(): pl.pallas_call(coarse_kernel, out_shape=shape_of(6), in_specs=[vmem], out...  2.46 us
    pallas_call x1, Pallas kernels, unpack(): pl.pallas_call(unpack_kernel, out_shape=[jax.ShapeDtypeStruct(BLOCK, jnp....  1.12 us
  transfers between devices with their start and end apart: 5, of which 2 were waited for; matrix products, arithmetic and copies ran while one was open for 0% of the time, Pallas kernels for 5%

profile of v5, /device:TPU:0, one launch (start us, length us, event | category | flops | bytes accessed | tf_op | source)
XLA Modules:
  0.0 54.3 jit_solution(3757534815956180125)
XLA Ops:
  0.6 1.1 %pad_maximum_fusion.fields = f32[3,8,32,128]{3,2,1,0:T(8,128)S(1)} fusion(f32[1,8,32,128]{3,2,1,0:T(8,128)} %bitcast.3, f32[1,8,32,128]{3,2,1,0:T(8,128)} %bitcast.4, f32[1,8,32,128]{3,2,1,0:T(8,128)} %bitcast.5), kind=kLoop, calls=%fused_computation | loop fusion | flops 196608 | bytes 786432 | tf_op jit(solution)/shard_map/stack | solution.py:891
  1.7 0.7 %pack.1 = f32[8,96,128]{2,1,0:T(8,128)S(1)} custom-call(f32[3,8,32,128]{3,2,1,0:T(8,128)S(1)} %pad_maximum_fusion.fields), custom_call_target="tpu_custom_call" | custom-call | tf_op jit(solution)/shard_map/pack/pallas_call | solution.py:274
  2.4 13.3 %all_to_all.15.in_ref = f32[8,96,128]{2,1,0:T(8,128)S(1)} all-to-all(f32[8,96,128]{2,1,0:T(8,128)S(1)} %pack.1), channel_id=1, replica_groups=mesh['gx'=4,'gy'=2,'gz'=4] {'gx','gy'}, dimensions={0} | all-to-all | bytes 786432 | tf_op jit(solution)/shard_map/all_to_all | solution.py:892
  15.7 0.3 to_slab.1
  16.0 0.1 collective-permute-start
  16.1 0.7 %collective-permute-start.1 = (f32[19,4,8,128]{3,2,1,0:T(8,128)S(1)}, f32[19,4,8,128]{3,2,1,0:T(8,128)S(1)}, u32[]{:S(2)}, u32[]{:S(2)}) collective-permute-start(f32[19,4,8,128]{3,2,1,0:T(8,128)S(1)} %get-tuple-element.39), channel_id=1, source_target_pairs={{4,8},{12,24},{28,16},{20,21},{17,29},{25,13},{9,5},{1,2},{6,10},{... | collective-permute-start | bytes 933896 | tf_op jit(solution)/shard_map/ppermute | solution.py:894
  16.7 0.5 down_pre.1
  17.2 0.4 collective-permute-done.even
  17.6 0.0 collective-permute-done.1.odd
  17.6 2.4 %down_post.1 = (f32[32,3,4,128]{3,2,1,0:T(4,128)}, f32[28,8,128]{2,1,0:T(8,128)}, f32[12,4,8,128]{3,2,1,0:T(8,128)S(1)}, f32[13,4,8,128]{3,2,1,0:T(8,128)S(1)}, ...) custom-call(f32[3,8,4,8,128]{4,3,2,1,0:T(8,128)S(1)} %get-tuple-elem, ...), custom_call_target="tpu_custom_call" | custom-call | tf_op jit(solution)/shard_map/down_post/pallas_call | solution.py:488
  20.1 10.7 %all-to-all-start.1 = ((f32[32,3,4,128]{3,2,1,0:T(4,128)}), f32[32,3,4,128]{3,2,1,0:T(4,128)S(1)}, u32[]{:S(2)}, u32[]{:S(2)}) async-start(f32[32,3,4,128]{3,2,1,0:T(4,128)} %get-tuple-element.56), calls=%async_computation.1 | async-start | bytes 393216 | tf_op jit(solution)/shard_map/all_to_all | solution.py:901
  30.8 0.7 %collective-permute-start.3 = (f32[28,8,128]{2,1,0:T(8,128)}, f32[28,8,128]{2,1,0:T(8,128)S(1)}, u32[]{:S(2)}, u32[]{:S(2)}) collective-permute-start(f32[28,8,128]{2,1,0:T(8,128)} %get-tuple-element.57), channel_id=1, source_target_pairs={{4,8},{12,24},{28,16},{20,21},{17,29},{25,13},{9,5},{1,2},{6,10},{... | collective-permute-start | bytes 344072 | tf_op jit(solution)/shard_map/ppermute | solution.py:899
  31.5 3.2 %collective-permute-start.2 = (f32[28,8,128]{2,1,0:T(8,128)}, f32[28,8,128]{2,1,0:T(8,128)S(1)}, u32[]{:S(2)}, u32[]{:S(2)}) collective-permute-start(f32[28,8,128]{2,1,0:T(8,128)} %get-tuple-element.57), channel_id=1, source_target_pairs={{0,4},{8,12},{24,28},{16,20},{21,17},{29,25},{13,9},{5,1},{2,6},{1... | collective-permute-start | bytes 344072 | tf_op jit(solution)/shard_map/ppermute | solution.py:898
  34.7 5.5 %all-to-all-done.1.gathered = f32[32,3,4,128]{3,2,1,0:T(4,128)S(1)} async-done(((f32[32,3,4,128]{3,2,1,0:T(4,128)}), f32[32,3,4,128]{3,2,1,0:T(4,128)S(1)}, u32[]{:S(2)}, u32[]{:S(2)}) %all-to-all-start.1) | async-done | bytes 196640 | tf_op jit(solution)/shard_map/all_to_all | solution.py:901
  40.1 2.5 %coarse.1.e_two = f32[6,8,128]{2,1,0:T(8,128)S(1)} custom-call(f32[32,3,4,128]{3,2,1,0:T(4,128)S(1)} %all-to-all-done.1.gathered), custom_call_target="tpu_custom_call" | custom-call | tf_op jit(solution)/shard_map/coarse/pallas_call | solution.py:782
  42.6 0.0 collective-permute-done.3.rim_odd
  42.6 0.0 collective-permute-done.2.rim_even
  42.6 1.2 %up_strokes.1 = f32[8,64,128]{2,1,0:T(8,128)S(1)} custom-call(f32[6,8,128]{2,1,0:T(8,128)S(1)} %coarse.1.e_two, f32[28,8,128]{2,1,0:T(8,128)S(1)} %collective-permute-done.2.rim_even, f32[28,8,128]{2,1,0:T(8,128)S(1)} %collective-permute-done.3.rim_odd, f32[3,8,4,8,128]{4,3,2,1,0:T(8,128)S(1)} %get-tuple-element.37.own, ...), custom_call_target="tpu_custom_call" | custom-call | tf_op jit(solution)/shard_map/up_strokes/pallas_call | solution.py:488
  43.8 9.3 %all_to_all.16.in_ref = f32[8,64,128]{2,1,0:T(8,128)S(1)} all-to-all(f32[8,64,128]{2,1,0:T(8,128)S(1)} %up_strokes.1), channel_id=1, replica_groups=mesh['gx'=4,'gy'=2,'gz'=4] {'gx','gy'}, dimensions={0} | all-to-all | bytes 524288 | tf_op jit(solution)/shard_map/all_to_all | solution.py:902
  53.2 1.1 %unpack.1 = (f32[8,32,128]{2,1,0:T(8,128)}, f32[8,32,128]{2,1,0:T(8,128)}) custom-call(f32[8,64,128]{2,1,0:T(8,128)S(1)} %all_to_all.16.in_ref), custom_call_target="tpu_custom_call" | custom-call | tf_op jit(solution)/shard_map/unpack/pallas_call | solution.py:873
Async XLA Ops:
  16.0 1.7 %collective-permute-start = (f32[19,4,8,128]{3,2,1,0:T(8,128)S(1)}, f32[19,4,8,128]{3,2,1,0:T(8,128)S(1)}, u32[]{:S(2)}, u32[]{:S(2)}) collective-permute-start(f32[19,4,8,128]{3,2,1,0:T(8,128)S(1)} %get-tuple-element.38), channel_id=1, source_target_pairs={{0,4},{8,12},{24,28},{16,20},{21,17},{29,25},{13,9},{5,1},{2,6},{1... | collective-permute-start | bytes 933896 | tf_op jit(solution)/shard_map/ppermute | solution.py:893
  16.1 1.6 %collective-permute-start.1 = (f32[19,4,8,128]{3,2,1,0:T(8,128)S(1)}, f32[19,4,8,128]{3,2,1,0:T(8,128)S(1)}, u32[]{:S(2)}, u32[]{:S(2)}) collective-permute-start(f32[19,4,8,128]{3,2,1,0:T(8,128)S(1)} %get-tuple-element.39), channel_id=1, source_target_pairs={{4,8},{12,24},{28,16},{20,21},{17,29},{25,13},{9,5},{1,2},{6,10},{... | collective-permute-start | bytes 933896 | tf_op jit(solution)/shard_map/ppermute | solution.py:894
  20.1 20.0 %all-to-all-start.1 = ((f32[32,3,4,128]{3,2,1,0:T(4,128)}), f32[32,3,4,128]{3,2,1,0:T(4,128)S(1)}, u32[]{:S(2)}, u32[]{:S(2)}) async-start(f32[32,3,4,128]{3,2,1,0:T(4,128)} %get-tuple-element.56), calls=%async_computation.1 | async-start | bytes 393216 | tf_op jit(solution)/shard_map/all_to_all | solution.py:901
  30.8 11.8 %collective-permute-start.3 = (f32[28,8,128]{2,1,0:T(8,128)}, f32[28,8,128]{2,1,0:T(8,128)S(1)}, u32[]{:S(2)}, u32[]{:S(2)}) collective-permute-start(f32[28,8,128]{2,1,0:T(8,128)} %get-tuple-element.57), channel_id=1, source_target_pairs={{4,8},{12,24},{28,16},{20,21},{17,29},{25,13},{9,5},{1,2},{6,10},{... | collective-permute-start | bytes 344072 | tf_op jit(solution)/shard_map/ppermute | solution.py:899
  31.5 11.1 %collective-permute-start.2 = (f32[28,8,128]{2,1,0:T(8,128)}, f32[28,8,128]{2,1,0:T(8,128)S(1)}, u32[]{:S(2)}, u32[]{:S(2)}) collective-permute-start(f32[28,8,128]{2,1,0:T(8,128)} %get-tuple-element.57), channel_id=1, source_target_pairs={{0,4},{8,12},{24,28},{16,20},{21,17},{29,25},{13,9},{5,1},{2,6},{1... | collective-permute-start | bytes 344072 | tf_op jit(solution)/shard_map/ppermute | solution.py:898

commit v6 on v5

--- a/solution.py
+++ b/solution.py
@@ -319,7 +319,7 @@
     return jnp.where(from_even, even[tile], odd[tile])
 
 
-def slab_kernel(in_ref, out_ref, even_ref, odd_ref):
+def slab_kernel(in_ref, out_ref, b_ref, even_ref, odd_ref):
     lane, row = lane_ids(), row_ids()
     low = (lane // 32) % 2 == 0
     _, from_even = halo_masks()
@@ -334,7 +334,10 @@
                 part[1].append(jnp.where(low, lanes(first, -32), second))
             for pp in range(2):
                 planes[k + 4 * pp] = jnp.stack(regroup(part[pp], 0, 2, row))
-                out_ref[a, k + 4 * pp] = planes[k + 4 * pp]
+                if a == 2:
+                    b_ref[k + 4 * pp] = planes[k + 4 * pp]
+                else:
+                    out_ref[a, k + 4 * pp] = planes[k + 4 * pp]
         count = 7 if a == 1 else 6
         for near, ref in ((from_even, even_ref), (~from_even, odd_ref)):
             for t, tile in enumerate(message(planes, near, count)):
@@ -345,9 +348,9 @@
     vmem = pl.BlockSpec(memory_space=pltpu.VMEM)
     return pl.pallas_call(
         slab_kernel,
-        out_shape=[shape_of(3, 8, 4), shape_of(MESSAGE, 4), shape_of(MESSAGE, 4)],
+        out_shape=[shape_of(2, 8, 4), shape_of(8, 4), shape_of(MESSAGE, 4), shape_of(MESSAGE, 4)],
         in_specs=[vmem],
-        out_specs=[vmem] * 3,
+        out_specs=[vmem] * 4,
         compiler_params=pltpu.CompilerParams(vmem_limit_bytes=4 * 2**20),
         name="to_slab",
     )(received)
@@ -483,13 +486,13 @@
     return jnp.where(end, 0.0, 1.0)
 
 
-def call(kernel, name, operands, out_shape, scratch_shapes, hbm_outputs=0):
+def call(kernel, name, operands, out_shape, scratch_shapes):
     vmem = pl.BlockSpec(memory_space=pltpu.VMEM)
     return pl.pallas_call(
         kernel,
         out_shape=out_shape,
         in_specs=[vmem] * len(operands),
-        out_specs=[pl.BlockSpec(memory_space=pl.ANY)] * hbm_outputs + [vmem] * (len(out_shape) - hbm_outputs),
+        out_specs=[vmem] * len(out_shape),
         scratch_shapes=scratch_shapes,
         compiler_params=pltpu.CompilerParams(vmem_limit_bytes=16 * 2**20),
         name=name,
@@ -497,18 +500,28 @@
 
 
 PRE_SHAPES = [(7, 4), (7, 4), (8, 4), (7, 4), (7, 4), (3, 2), (3, 2), (4, 2), (3, 2), (3, 2)]
-MID_SHAPES = [(13, 4)] * 5 + [(7, 2)] * 5
-
-
-def coefficient_planes(pre, mid):
-    zero = [Planes(*([(4, mid[i])] if mid else []), *([(17, pre[i])] if pre else [])) for i in range(5)]
-    one = [Planes(*([(2, mid[i])] if mid else []), *([(9, pre[i])] if pre else [])) for i in range(5, 10)]
+MID_SHAPES = [(5, 4), (5, 4), (5, 4), (5, 4), (1, 4), (7, 2), (7, 2), (7, 2), (7, 2)]
+LOW_SHAPES = [(8, 4), (8, 4), (8, 4), (8, 4), (12, 4), (7, 2)]
+
+
+def coefficient_planes(pre, mid, low):
+    zero, one = [], []
+    for i in range(5):
+        parts = [(4, low[i])] if low else []
+        parts += [(16 if i == 4 else 12, mid[i])] if mid else []
+        zero.append(Planes(*parts, *([(17, pre[i])] if pre else [])))
+        parts = []
+        if mid and i < 4:
+            parts = [(2, mid[5 + i])]
+        elif low and i == 4:
+            parts = [(2, low[5])]
+        one.append(Planes(*parts, *([(9, pre[5 + i])] if pre and len(pre) > 5 + i else [])))
     return zero, one
 
 
-def pre_kernel(own, *refs):
+def pre_kernel(own, own_b, *refs):
     pre, (alpha1, beta1, v1, v2, v3, v4), (ghost, ghost1) = refs[:10], refs[10:16], refs[16:]
-    zero, one = coefficient_planes(pre, None)
+    zero, one = coefficient_planes(pre, None, None)
     alpha, beta = Planes((16, own.at[0])), Planes((16, own.at[1]), (24, ghost))
     alpha_one, beta_one = Planes((8, alpha1)), Planes((8, beta1), (12, ghost1))
     close(beta, PLANES)
@@ -517,7 +530,7 @@
     alpha_one.put(8, 0.125 * restrict(alpha.get, 8, PLANES1, 1))
     close(beta_one, PLANES1)
     level_coefficients(beta_one, alpha_one, 9, PLANES1, SHIFT_BASE * 4.0, 2, *one, None, 8, COEF_SPAN1)
-    b, coeffs, dinv = Planes((16, own.at[2])), zero[:3], zero[3]
+    b, coeffs, dinv = Planes((16, own_b)), zero[:3], zero[3]
     factors = chebyshev_factors(SWEEPS, SMOOTH_LOWER)
     iterates = [None, Planes((17, v1)), Planes((18, v2)), Planes((19, v3)), Planes((20, v4))]
     for p, q in spans(17, PLANES, 4):
@@ -528,9 +541,9 @@
         close(iterates[i], PLANES)
 
 
-def mid_part(own, even, odd, beta1_own, alpha1_own, mid, beta_s, alpha_s, beta1_s, alpha1_s):
+def mid_part(own, even, odd, beta1_own, alpha1_own, mid, low, beta_s, alpha_s, beta1_s, alpha1_s):
     _, from_even = halo_masks()
-    zero, one = coefficient_planes(None, mid)
+    zero, one = coefficient_planes(None, mid, low)
     for p in range(2, 16):
         beta_s[p] = halo_plane(even, odd, 1, 15 - p, from_even)
         if p >= 4:
@@ -546,15 +559,15 @@
     level_coefficients(beta_one, alpha_one, 2, 9, SHIFT_BASE * 4.0, 2, *one, ends, 8, COEF_SPAN1)
 
 
-def post_kernel(own, even, odd, *refs):
+def post_kernel(own, own_b, odd, even, *refs):
     pre, (alpha1, beta1, v1, v2, v3, v4), (gather, rim, halo_b, late, u1, b1) = refs[:10], refs[10:16], refs[16:22]
-    mid, (f1, f2, f3, b1_s, w_a, w_b, tile_s, rim_s, sent), scratch_mid = refs[22:32], refs[32:41], refs[41:]
-    mid_part(own, even, odd, beta1, alpha1, mid, *scratch_mid)
+    mid, low, (f1, f2, f3, f4, low_b, b1_s, w_a, w_b), scratch_mid = refs[22:31], refs[31:37], refs[37:45], refs[45:]
+    mid_part(own, even, odd, beta1, alpha1, mid, low, *scratch_mid)
     lane = lane_ids()
     _, from_even = halo_masks()
-    zero, one = coefficient_planes(pre, mid)
+    zero, one = coefficient_planes(pre, mid, low)
     coeffs, dinv, diag = zero[:3], zero[3], zero[4]
-    b = Planes((4, halo_b), (16, own.at[2]))
+    b = Planes((4, low_b), (12, halo_b), (16, own_b))
     for p in range(4, 16):
         b.put(p, halo_plane(even, odd, 2, 15 - p, from_even)[None])
     factors = chebyshev_factors(SWEEPS, SMOOTH_LOWER)
@@ -563,16 +576,14 @@
         Planes((4, f1), (17, v1)),
         Planes((5, f2), (18, v2)),
         Planes((6, f3), (19, v3)),
-        Planes((7, late), (20, v4)),
+        Planes((7, f4), (16, late), (20, v4)),
     ]
     for p, q in spans(4, 17, 4):
         iterates[1].put(p, factors[0][1] * (b.get(p, q) * dinv.get(p, q)))
     for i in range(2, 5):
         sweep(iterates[i], iterates[i - 1], iterates[i - 2], factors[i - 1], b, dinv, coeffs, 3 + i, 16 + i, 1, SPAN)
     v = iterates[4]
-    rim_s[0:20] = v.get(16, 21).reshape((20,) + TILE)
-    copies = [pltpu.make_async_copy(rim_s.at[0:20], rim.at[0:20], sent.at[0])]
-    copies[0].start()
+    rim[0:20] = v.get(16, 21).reshape((20,) + TILE)
 
     def residual(v, b, diag, coeffs, dup):
         return lambda p, q: (b.get(p, q) + couple(v, p, q, *coeffs, dup)) - diag.get(p, q) * v.get(p, q)
@@ -592,35 +603,24 @@
     both = jnp.where(slot < 2, *(jnp.where(slot % 2 == 0, field[0, 0], field[1, 0]) for field in (b_two, beta_two)))
     last = jnp.where(slot % 2 == 0, alpha_two[0, 0], alpha_two[1, 0])
     last = jnp.where(slot[:4] < 2, last[:4], last[4:])
-    for n in range(2):
+    for n in range(COUNT):
         for i, part in enumerate((both[:4], both[4:], last)):
-            tile_s[n, i] = part
-    copies += [pltpu.make_async_copy(tile_s, gather.at[n : n + 2], sent.at[n + 1]) for n in range(0, COUNT, 2)]
-    for copy in copies[1:]:
-        copy.start()
+            gather[n, i] = part
     u1[...] = w.get(8, PLANES1)
-    rim_s[20:28] = jnp.where(lane % 2 == 0, w.get(8, PLANES1), b_one.get(8, PLANES1)).reshape((8,) + TILE)
-    copies.append(pltpu.make_async_copy(rim_s.at[20:28], rim.at[20:28], sent.at[COUNT + 1]))
-    copies[-1].start()
-    for copy in copies:
-        copy.wait()
-
-
-def down_pre(own):
+    rim[20:28] = jnp.where(lane % 2 == 0, w.get(8, PLANES1), b_one.get(8, PLANES1)).reshape((8,) + TILE)
+
+
+def down_pre(own, own_b):
     shapes = PRE_SHAPES + [(4, 2), (4, 2), (8, 4), (7, 4), (6, 4), (5, 4)]
-    return call(pre_kernel, "down_pre", (own,), [shape_of(*n) for n in shapes], [scratch(1, 4), scratch(1, 2)])
-
-
-def down_post(own, even, odd, pre):
-    shapes = [shape_of(*n) for n in [(RIM,), (12, 4), (13, 4), (4, 2), (4, 2), *MID_SHAPES]]
+    return call(pre_kernel, "down_pre", (own, own_b), [shape_of(*n) for n in shapes], [scratch(1, 4), scratch(1, 2)])
+
+
+def down_post(own, own_b, even, odd, pre):
+    shapes = [shape_of(*n) for n in [(RIM,), (4, 4), (4, 4), (4, 2), (4, 2), *MID_SHAPES]]
+    spare = [(13, 4), (13, 4), (13, 4), (9, 4), (8, 4), (4, 2), (13, 2), (13, 2), (16, 4), (16, 4), (8, 2), (8, 2)]
     return call(
-        post_kernel, "down_post", (own, even, odd, *pre), [jax.ShapeDtypeStruct((COUNT, 3, 4, 128), jnp.float32), *shapes],
-        [
-            scratch(13, 4), scratch(13, 4), scratch(13, 4), scratch(4, 2), scratch(13, 2), scratch(13, 2),
-            pltpu.VMEM((2, 3, 4, 128), jnp.float32), scratch(28), pltpu.SemaphoreType.DMA((COUNT + 2,)),
-            scratch(16, 4), scratch(16, 4), scratch(8, 2), scratch(8, 2),
-        ],
-        hbm_outputs=2,
+        post_kernel, "down_post", (own, own_b, odd, even, *pre),
+        [jax.ShapeDtypeStruct((COUNT, 3, 4, 128), jnp.float32), *shapes], [scratch(*n) for n in LOW_SHAPES + spare],
     )
 
 
@@ -790,9 +790,9 @@
     )(gathered)
 
 
-def up_kernel(e_two, rim_even, rim_odd, own, halo_b, late, u1, b1, v4, *refs):
-    pre, mid, (out, v_a, v_b, w_a, w_b, bx_s) = refs[:10], refs[10:20], refs[20:]
-    zero, one = coefficient_planes(pre, mid)
+def up_kernel(e_two, rim_even, rim_odd, own_b, halo_b, late, u1, b1, v4, *refs):
+    pre, mid, (out, v_a, v_b, w_a, w_b, bx_s) = refs[:9], refs[9:18], refs[18:]
+    zero, one = coefficient_planes(pre, mid, None)
     lane, row = lane_ids(), row_ids()
     _, from_even = halo_masks()
     factors = chebyshev_factors(SWEEPS, SMOOTH_LOWER)
@@ -814,7 +814,7 @@
 
     for p in range(11, PLANES):
         if p >= 16:
-            start = Planes((7, late), (20, v4)).get(p, p + 1)[0]
+            start = Planes((16, late), (20, v4)).get(p, p + 1)[0]
         else:
             k = 4 * (15 - p)
             start = lanes(jnp.where(from_even, rim_odd[k : k + 4], rim_even[k : k + 4]), 64)
@@ -822,7 +822,7 @@
         e_one = jnp.concatenate([e_one[:1], e_one[:1], e_one[1:], e_one[1:]], axis=0)
         v_a[p] = start + e_one
     v_a[PLANES] = lanes(v_a[PLANES - 1], 64)
-    b, diag, coeffs = Planes((4, halo_b), (16, own.at[2])), zero[4], zero[:3]
+    b, diag, coeffs = Planes((12, halo_b), (16, own_b)), zero[4], zero[:3]
     v = smooth((Planes((0, v_b)), Planes((0, v_a)), None), b, zero[3], coeffs, factors, 12, PLANES, 1, SPAN)
     low = (lane // 32) % 2 == 0
     for k in range(4):
@@ -889,15 +889,15 @@
 def slab_shards(right_side, alpha_coef, beta_coef):
     even_pairs, odd_pairs = swap_pairs(False), swap_pairs(True)
     packed = pack(jnp.stack([alpha_coef, beta_coef, right_side]))
-    own, to_even, to_odd = to_slab(lax.all_to_all(packed, RING, 0, 0))
+    own, own_b, to_even, to_odd = to_slab(lax.all_to_all(packed, RING, 0, 0))
     even = lax.ppermute(to_even, ALL, even_pairs)
     odd = lax.ppermute(to_odd, ALL, odd_pairs)
-    found = down_pre(own)
-    pre, v4 = found[:10], found[15]
-    gather, rim, halo_b, late, u1, b1, *mid = down_post(own, even, odd, found)
+    found = down_pre(own, own_b)
+    pre, v4 = found[:9], found[15]
+    gather, rim, halo_b, late, u1, b1, *mid = down_post(own, own_b, even, odd, found)
     rim_even = lax.ppermute(rim, ALL, even_pairs)
     rim_odd = lax.ppermute(rim, ALL, odd_pairs)
-    kept = (own, halo_b, late, u1, b1, v4, *pre, *mid)
+    kept = (own_b, halo_b, late, u1, b1, v4, *pre, *mid)
     result = up(coarse(lax.all_to_all(gather, ALL, 0, 0)), rim_even, rim_odd, *kept)
     return tuple(unpack(lax.all_to_all(result, RING, 0, 0)))
 

time: 54.6 us -> 54.3 us (level)
    all_to_all x1, starting transfers between devices: 10.7 us -> 8.3 us  [slab_shards(): lax.all_to_all(gather, ALL, 0, 0)]
    ppermute x1, starting transfers between devices: 0.07 us -> 1.97 us  [slab_shards(): even = lax.ppermute(to_even, ALL, even_pairs)]
where the time goes in v6:
time: 54.3 us; the launch traced here: 54 us
  blocking collectives  22.7 us (42%)
  starting transfers between devices  14.8 us (27%)
  Pallas kernels  8.5 us (16%)
  waiting for transfers between devices  6.24 us (11%)
  other arithmetic  1.06 us (2%)
  between operations  0.71 us (1%)
    all_to_all x1, blocking collectives, slab_shards(): own, own_b, to_even, to_odd = to_slab(lax.all_to_all(packed, RING, 0, 0))  13.3 us
    all_to_all x1, blocking collectives, slab_shards(): return tuple(unpack(lax.all_to_all(result, RING, 0, 0)))  9.35 us
    all_to_all x1, starting transfers between devices, slab_shards(): lax.all_to_all(gather, ALL, 0, 0)  8.3 us
    all_to_all x1, waiting for transfers between devices, slab_shards(): lax.all_to_all(gather, ALL, 0, 0)  5.47 us
    pallas_call x3, Pallas kernels, call(): pl.pallas_call(kernel, out_shape=out_shape, in_specs=[vmem] * len(operand...  3.94 us
    ppermute x1, starting transfers between devices, slab_shards(): rim_even = lax.ppermute(rim, ALL, even_pairs)  3.19 us
    pallas_call x1, Pallas kernels, coarse(): pl.pallas_call(coarse_kernel, out_shape=shape_of(6), in_specs=[vmem], out...  2.46 us
    ppermute x1, starting transfers between devices, slab_shards(): even = lax.ppermute(to_even, ALL, even_pairs)  1.97 us
  transfers between devices with their start and end apart: 5, of which 2 were waited for; matrix products, arithmetic and copies ran while one was open for 0% of the time, Pallas kernels for 5%

profile of v6, /device:TPU:0, one launch (start us, length us, event | category | flops | bytes accessed | tf_op | source)
XLA Modules:
  0.0 54.0 jit_solution(10502600078071892646)
XLA Ops:
  0.6 1.1 %pad_maximum_fusion.fields = f32[3,8,32,128]{3,2,1,0:T(8,128)S(1)} fusion(f32[1,8,32,128]{3,2,1,0:T(8,128)} %bitcast.3, f32[1,8,32,128]{3,2,1,0:T(8,128)} %bitcast.4, f32[1,8,32,128]{3,2,1,0:T(8,128)} %bitcast.5), kind=kLoop, calls=%fused_computation | loop fusion | flops 196608 | bytes 786432 | tf_op jit(solution)/shard_map/stack | solution.py:891
  1.7 0.7 %pack.1 = f32[8,96,128]{2,1,0:T(8,128)S(1)} custom-call(f32[3,8,32,128]{3,2,1,0:T(8,128)S(1)} %pad_maximum_fusion.fields), custom_call_target="tpu_custom_call" | custom-call | tf_op jit(solution)/shard_map/pack/pallas_call | solution.py:274
  2.4 13.3 %all_to_all.15.in_ref = f32[8,96,128]{2,1,0:T(8,128)S(1)} all-to-all(f32[8,96,128]{2,1,0:T(8,128)S(1)} %pack.1), channel_id=1, replica_groups=mesh['gx'=4,'gy'=2,'gz'=4] {'gx','gy'}, dimensions={0} | all-to-all | bytes 786432 | tf_op jit(solution)/shard_map/all_to_all | solution.py:892
  15.7 0.3 to_slab.1
  16.0 0.7 %collective-permute-start = (f32[19,4,8,128]{3,2,1,0:T(8,128)S(1)}, f32[19,4,8,128]{3,2,1,0:T(8,128)S(1)}, u32[]{:S(2)}, u32[]{:S(2)}) collective-permute-start(f32[19,4,8,128]{3,2,1,0:T(8,128)S(1)} %get-tuple-element.39), channel_id=1, source_target_pairs={{4,8},{12,24},{28,16},{20,21},{17,29},{25,13},{9,5},{1,2},{6,10},{... | collective-permute-start | bytes 933896 | tf_op jit(solution)/shard_map/ppermute | solution.py:894
  16.7 2.0 %collective-permute-start.1 = (f32[19,4,8,128]{3,2,1,0:T(8,128)S(1)}, f32[19,4,8,128]{3,2,1,0:T(8,128)S(1)}, u32[]{:S(2)}, u32[]{:S(2)}) collective-permute-start(f32[19,4,8,128]{3,2,1,0:T(8,128)S(1)} %get-tuple-element.40), channel_id=1, source_target_pairs={{0,4},{8,12},{24,28},{16,20},{21,17},{29,25},{13,9},{5,1},{2,6},{1... | collective-permute-start | bytes 933896 | tf_op jit(solution)/shard_map/ppermute | solution.py:893
  18.6 0.4 down_pre.1
  19.1 0.0 collective-permute-done.odd
  19.1 0.8 %collective-permute-done.1.even = f32[19,4,8,128]{3,2,1,0:T(8,128)S(1)} collective-permute-done((f32[19,4,8,128]{3,2,1,0:T(8,128)S(1)}, f32[19,4,8,128]{3,2,1,0:T(8,128)S(1)}, u32[]{:S(2)}, u32[]{:S(2)}) %collective-permute-start.1) | collective-permute-done | bytes 311328 | tf_op jit(solution)/shard_map/ppermute | solution.py:893
  19.9 2.2 %down_post.1 = (f32[32,3,4,128]{3,2,1,0:T(4,128)}, f32[28,8,128]{2,1,0:T(8,128)S(1)}, f32[4,4,8,128]{3,2,1,0:T(8,128)S(1)}, f32[4,4,8,128]{3,2,1,0:T(8,128)S(1)}...) custom-call(f32[2,8,4,8,128]{4,3,2,1,0:T(8,128)S(1)} %get-tuple-elem, ...), custom_call_target="tpu_custom_call" | custom-call | tf_op jit(solution)/shard_map/down_post/pallas_call | solution.py:491
  22.1 8.3 %all-to-all-start.1 = ((f32[32,3,4,128]{3,2,1,0:T(4,128)}), f32[32,3,4,128]{3,2,1,0:T(4,128)S(1)}, u32[]{:S(2)}, u32[]{:S(2)}) async-start(f32[32,3,4,128]{3,2,1,0:T(4,128)} %get-tuple-element.57), calls=%async_computation.1 | async-start | bytes 393216 | tf_op jit(solution)/shard_map/all_to_all | solution.py:901
  30.4 0.7 %collective-permute-start.3 = (f32[28,8,128]{2,1,0:T(8,128)S(1)}, f32[28,8,128]{2,1,0:T(8,128)S(1)}, u32[]{:S(2)}, u32[]{:S(2)}) collective-permute-start(f32[28,8,128]{2,1,0:T(8,128)S(1)} %get-tuple-element.58), channel_id=1, source_target_pairs={{4,8},{12,24},{28,16},{20,21},{17,29},{25,13},{9,5},{1,2},{6,10},{... | collective-permute-start | bytes 344072 | tf_op jit(solution)/shard_map/ppermute | solution.py:899
  31.1 3.2 %collective-permute-start.2 = (f32[28,8,128]{2,1,0:T(8,128)S(1)}, f32[28,8,128]{2,1,0:T(8,128)S(1)}, u32[]{:S(2)}, u32[]{:S(2)}) collective-permute-start(f32[28,8,128]{2,1,0:T(8,128)S(1)} %get-tuple-element.58), channel_id=1, source_target_pairs={{0,4},{8,12},{24,28},{16,20},{21,17},{29,25},{13,9},{5,1},{2,6},{1... | collective-permute-start | bytes 344072 | tf_op jit(solution)/shard_map/ppermute | solution.py:898
  34.3 5.5 %all-to-all-done.1.gathered = f32[32,3,4,128]{3,2,1,0:T(4,128)S(1)} async-done(((f32[32,3,4,128]{3,2,1,0:T(4,128)}), f32[32,3,4,128]{3,2,1,0:T(4,128)S(1)}, u32[]{:S(2)}, u32[]{:S(2)}) %all-to-all-start.1) | async-done | bytes 196640 | tf_op jit(solution)/shard_map/all_to_all | solution.py:901
  39.7 2.5 %coarse.1.e_two = f32[6,8,128]{2,1,0:T(8,128)S(1)} custom-call(f32[32,3,4,128]{3,2,1,0:T(4,128)S(1)} %all-to-all-done.1.gathered), custom_call_target="tpu_custom_call" | custom-call | tf_op jit(solution)/shard_map/coarse/pallas_call | solution.py:782
  42.2 0.0 collective-permute-done.3.rim_odd
  42.2 0.0 collective-permute-done.2.rim_even
  42.2 1.3 %up_strokes.1 = f32[8,64,128]{2,1,0:T(8,128)S(1)} custom-call(f32[6,8,128]{2,1,0:T(8,128)S(1)} %coarse.1.e_two, f32[28,8,128]{2,1,0:T(8,128)S(1)} %collective-permute-done.2.rim_even, f32[28,8,128]{2,1,0:T(8,128)S(1)} %collective-permute-done.3.rim_odd, f32[8,4,8,128]{3,2,1,0:T(8,128)S(1)} %get-tuple-element.38.own_b, ...), custom_call_target="tpu_custom_call" | custom-call | tf_op jit(solution)/shard_map/up_strokes/pallas_call | solution.py:491
  43.5 9.3 %all_to_all.16.in_ref = f32[8,64,128]{2,1,0:T(8,128)S(1)} all-to-all(f32[8,64,128]{2,1,0:T(8,128)S(1)} %up_strokes.1), channel_id=1, replica_groups=mesh['gx'=4,'gy'=2,'gz'=4] {'gx','gy'}, dimensions={0} | all-to-all | bytes 524288 | tf_op jit(solution)/shard_map/all_to_all | solution.py:902
  52.8 1.1 %unpack.1 = (f32[8,32,128]{2,1,0:T(8,128)}, f32[8,32,128]{2,1,0:T(8,128)}) custom-call(f32[8,64,128]{2,1,0:T(8,128)S(1)} %all_to_all.16.in_ref), custom_call_target="tpu_custom_call" | custom-call | tf_op jit(solution)/shard_map/unpack/pallas_call | solution.py:873
Async XLA Ops:
  16.0 3.1 %collective-permute-start = (f32[19,4,8,128]{3,2,1,0:T(8,128)S(1)}, f32[19,4,8,128]{3,2,1,0:T(8,128)S(1)}, u32[]{:S(2)}, u32[]{:S(2)}) collective-permute-start(f32[19,4,8,128]{3,2,1,0:T(8,128)S(1)} %get-tuple-element.39), channel_id=1, source_target_pairs={{4,8},{12,24},{28,16},{20,21},{17,29},{25,13},{9,5},{1,2},{6,10},{... | collective-permute-start | bytes 933896 | tf_op jit(solution)/shard_map/ppermute | solution.py:894
  16.7 3.2 %collective-permute-start.1 = (f32[19,4,8,128]{3,2,1,0:T(8,128)S(1)}, f32[19,4,8,128]{3,2,1,0:T(8,128)S(1)}, u32[]{:S(2)}, u32[]{:S(2)}) collective-permute-start(f32[19,4,8,128]{3,2,1,0:T(8,128)S(1)} %get-tuple-element.40), channel_id=1, source_target_pairs={{0,4},{8,12},{24,28},{16,20},{21,17},{29,25},{13,9},{5,1},{2,6},{1... | collective-permute-start | bytes 933896 | tf_op jit(solution)/shard_map/ppermute | solution.py:893
  22.1 17.6 %all-to-all-start.1 = ((f32[32,3,4,128]{3,2,1,0:T(4,128)}), f32[32,3,4,128]{3,2,1,0:T(4,128)S(1)}, u32[]{:S(2)}, u32[]{:S(2)}) async-start(f32[32,3,4,128]{3,2,1,0:T(4,128)} %get-tuple-element.57), calls=%async_computation.1 | async-start | bytes 393216 | tf_op jit(solution)/shard_map/all_to_all | solution.py:901
  30.4 11.8 %collective-permute-start.3 = (f32[28,8,128]{2,1,0:T(8,128)S(1)}, f32[28,8,128]{2,1,0:T(8,128)S(1)}, u32[]{:S(2)}, u32[]{:S(2)}) collective-permute-start(f32[28,8,128]{2,1,0:T(8,128)S(1)} %get-tuple-element.58), channel_id=1, source_target_pairs={{4,8},{12,24},{28,16},{20,21},{17,29},{25,13},{9,5},{1,2},{6,10},{... | collective-permute-start | bytes 344072 | tf_op jit(solution)/shard_map/ppermute | solution.py:899
  31.1 11.1 %collective-permute-start.2 = (f32[28,8,128]{2,1,0:T(8,128)S(1)}, f32[28,8,128]{2,1,0:T(8,128)S(1)}, u32[]{:S(2)}, u32[]{:S(2)}) collective-permute-start(f32[28,8,128]{2,1,0:T(8,128)S(1)} %get-tuple-element.58), channel_id=1, source_target_pairs={{0,4},{8,12},{24,28},{16,20},{21,17},{29,25},{13,9},{5,1},{2,6},{1... | collective-permute-start | bytes 344072 | tf_op jit(solution)/shard_map/ppermute | solution.py:898

commit v7 on v6

--- a/solution.py
+++ b/solution.py
@@ -183,7 +183,7 @@
 COUNT = GX * GY * GZ
 RIM = 28
 BLOCK = (8, 32, 128)
-RING = ("gx", "gy")
+RING = ("gy", "gx")
 ALL = ("gx", "gy", "gz")
 TILE = (8, 128)
 PLANES = 24
@@ -267,7 +267,7 @@
     for x in range(GX):
         for y in range(GY):
             start = pl.multiple_of(chunk_of(x, y, z) * 96, 96)
-            out_ref[x * GY + y] = staged[pl.ds(start, 96), :]
+            out_ref[y * GX + x] = staged[pl.ds(start, 96), :]
 
 
 def pack(fields):
@@ -328,8 +328,8 @@
         for k in range(4):
             part = ([], [])
             for x in range(GX):
-                first = in_ref[2 * x, pl.ds(a * 32 + k * 8, 8), :]
-                second = in_ref[2 * x + 1, pl.ds(a * 32 + k * 8, 8), :]
+                first = in_ref[x, pl.ds(a * 32 + k * 8, 8), :]
+                second = in_ref[GX + x, pl.ds(a * 32 + k * 8, 8), :]
                 part[0].append(jnp.where(low, first, lanes(second, 32)))
                 part[1].append(jnp.where(low, lanes(first, -32), second))
             for pp in range(2):
@@ -646,7 +646,7 @@
             for q in range(GZ):
                 natural = 7 - group if q % 2 else group
                 rank, core = natural // 2, natural % 2
-                n = ((rank ^ (rank >> 1)) * GY + core) * GZ + q
+                n = ((rank ^ (rank >> 1)) * GZ + q) * GY + core
                 piece = tiles_s[n, tile] if q == slot else lanes(tiles_s[n, tile], q - slot)
                 joined = piece if joined is None else jnp.where(lane % 4 == q, piece, joined)
             out.append(joined)
@@ -836,8 +836,8 @@
                 parts.append(regroup([value[0, i] for i in range(4)], 0, 2, row))
             for i in range(GX):
                 one, two = parts[0][i], parts[1][i]
-                out[2 * i, pl.ds(o * 32 + k * 8, 8), :] = jnp.where(low, one, lanes(two, 32))
-                out[2 * i + 1, pl.ds(o * 32 + k * 8, 8), :] = jnp.where(low, lanes(one, -32), two)
+                out[i, pl.ds(o * 32 + k * 8, 8), :] = jnp.where(low, one, lanes(two, 32))
+                out[GX + i, pl.ds(o * 32 + k * 8, 8), :] = jnp.where(low, lanes(one, -32), two)
 
 
 def up(*operands):
@@ -853,7 +853,7 @@
     for x in range(GX):
         for y in range(GY):
             start = pl.multiple_of(chunk_of(x, y, z) * 64, 64)
-            staged[pl.ds(start, 64), :] = in_ref[x * GY + y]
+            staged[pl.ds(start, 64), :] = in_ref[y * GX + x]
     copies = [pltpu.make_async_copy(fields.at[o], ref, left.at[o]) for o, ref in enumerate((v_ref, r_ref))]
     for o, copy in enumerate(copies):
         for xg in range(2):
@@ -898,7 +898,7 @@
     rim_even = lax.ppermute(rim, ALL, even_pairs)
     rim_odd = lax.ppermute(rim, ALL, odd_pairs)
     kept = (own_b, halo_b, late, u1, b1, v4, *pre, *mid)
-    result = up(coarse(lax.all_to_all(gather, ALL, 0, 0)), rim_even, rim_odd, *kept)
+    result = up(coarse(lax.all_to_all(gather, ("gx", "gz", "gy"), 0, 0)), rim_even, rim_odd, *kept)
     return tuple(unpack(lax.all_to_all(result, RING, 0, 0)))
 
 

time: 54.3 us -> 53.4 us (0.983)
  waiting for transfers between devices: 6.24 us -> 5.66 us
    all_to_all x1, waiting for transfers between devices: 5.47 us -> 4.88 us  [slab_shards(): lax.all_to_all(gather, ('gx', 'gz', 'gy'), 0, 0)]
where the time goes in v7:
time: 53.4 us; the launch traced here: 53.1 us
  blocking collectives  22.2 us (42%)
  starting transfers between devices  15 us (28%)
  Pallas kernels  8.5 us (16%)
  waiting for transfers between devices  5.66 us (11%)
  other arithmetic  1.06 us (2%)
  between operations  0.71 us (1%)
    all_to_all x1, blocking collectives, slab_shards(): own, own_b, to_even, to_odd = to_slab(lax.all_to_all(packed, RING, 0, 0))  13.1 us
    all_to_all x1, blocking collectives, slab_shards(): return tuple(unpack(lax.all_to_all(result, RING, 0, 0)))  9.1 us
    all_to_all x1, starting transfers between devices, slab_shards(): lax.all_to_all(gather, ('gx', 'gz', 'gy'), 0, 0)  8.35 us
    all_to_all x1, waiting for transfers between devices, slab_shards(): lax.all_to_all(gather, ('gx', 'gz', 'gy'), 0, 0)  4.88 us
    pallas_call x3, Pallas kernels, call(): pl.pallas_call(kernel, out_shape=out_shape, in_specs=[vmem] * len(operand...  3.94 us
    ppermute x1, starting transfers between devices, slab_shards(): rim_even = lax.ppermute(rim, ALL, even_pairs)  3.19 us
    pallas_call x1, Pallas kernels, coarse(): pl.pallas_call(coarse_kernel, out_shape=shape_of(6), in_specs=[vmem], out...  2.46 us
    ppermute x1, starting transfers between devices, slab_shards(): even = lax.ppermute(to_even, ALL, even_pairs)  2.1 us
  transfers between devices with their start and end apart: 5, of which 2 were waited for; matrix products, arithmetic and copies ran while one was open for 0% of the time, Pallas kernels for 5%

profile of v7, /device:TPU:0, one launch (start us, length us, event | category | flops | bytes accessed | tf_op | source)
XLA Modules:
  0.0 53.1 jit_solution(6113507271157697106)
XLA Ops:
  0.6 1.1 %pad_maximum_fusion.fields = f32[3,8,32,128]{3,2,1,0:T(8,128)S(1)} fusion(f32[1,8,32,128]{3,2,1,0:T(8,128)} %bitcast.3, f32[1,8,32,128]{3,2,1,0:T(8,128)} %bitcast.4, f32[1,8,32,128]{3,2,1,0:T(8,128)} %bitcast.5), kind=kLoop, calls=%fused_computation | loop fusion | flops 196608 | bytes 786432 | tf_op jit(solution)/shard_map/stack | solution.py:891
  1.7 0.7 %pack.1 = f32[8,96,128]{2,1,0:T(8,128)S(1)} custom-call(f32[3,8,32,128]{3,2,1,0:T(8,128)S(1)} %pad_maximum_fusion.fields), custom_call_target="tpu_custom_call" | custom-call | tf_op jit(solution)/shard_map/pack/pallas_call | solution.py:274
  2.4 13.1 %all_to_all.15.in_ref = f32[8,96,128]{2,1,0:T(8,128)S(1)} all-to-all(f32[8,96,128]{2,1,0:T(8,128)S(1)} %pack.1), channel_id=1, replica_groups=mesh['gx'=4,'gy'=2,'gz'=4] {'gy','gx'}, dimensions={0} | all-to-all | bytes 786432 | tf_op jit(solution)/shard_map/all_to_all | solution.py:892
  15.5 0.3 to_slab.1
  15.8 0.7 %collective-permute-start = (f32[19,4,8,128]{3,2,1,0:T(8,128)S(1)}, f32[19,4,8,128]{3,2,1,0:T(8,128)S(1)}, u32[]{:S(2)}, u32[]{:S(2)}) collective-permute-start(f32[19,4,8,128]{3,2,1,0:T(8,128)S(1)} %get-tuple-element.39), channel_id=1, source_target_pairs={{4,8},{12,24},{28,16},{20,21},{17,29},{25,13},{9,5},{1,2},{6,10},{... | collective-permute-start | bytes 933896 | tf_op jit(solution)/shard_map/ppermute | solution.py:894
  16.5 2.1 %collective-permute-start.1 = (f32[19,4,8,128]{3,2,1,0:T(8,128)S(1)}, f32[19,4,8,128]{3,2,1,0:T(8,128)S(1)}, u32[]{:S(2)}, u32[]{:S(2)}) collective-permute-start(f32[19,4,8,128]{3,2,1,0:T(8,128)S(1)} %get-tuple-element.40), channel_id=1, source_target_pairs={{0,4},{8,12},{24,28},{16,20},{21,17},{29,25},{13,9},{5,1},{2,6},{1... | collective-permute-start | bytes 933896 | tf_op jit(solution)/shard_map/ppermute | solution.py:893
  18.6 0.4 down_pre.1
  19.0 0.0 collective-permute-done.odd
  19.0 0.8 %collective-permute-done.1.even = f32[19,4,8,128]{3,2,1,0:T(8,128)S(1)} collective-permute-done((f32[19,4,8,128]{3,2,1,0:T(8,128)S(1)}, f32[19,4,8,128]{3,2,1,0:T(8,128)S(1)}, u32[]{:S(2)}, u32[]{:S(2)}) %collective-permute-start.1) | collective-permute-done | bytes 311328 | tf_op jit(solution)/shard_map/ppermute | solution.py:893
  19.8 2.2 %down_post.1 = (f32[32,3,4,128]{3,2,1,0:T(4,128)}, f32[28,8,128]{2,1,0:T(8,128)S(1)}, f32[4,4,8,128]{3,2,1,0:T(8,128)S(1)}, f32[4,4,8,128]{3,2,1,0:T(8,128)S(1)}...) custom-call(f32[2,8,4,8,128]{4,3,2,1,0:T(8,128)S(1)} %get-tuple-elem, ...), custom_call_target="tpu_custom_call" | custom-call | tf_op jit(solution)/shard_map/down_post/pallas_call | solution.py:491
  22.0 8.4 %all-to-all-start.1 = ((f32[32,3,4,128]{3,2,1,0:T(4,128)}), f32[32,3,4,128]{3,2,1,0:T(4,128)S(1)}, u32[]{:S(2)}, u32[]{:S(2)}) async-start(f32[32,3,4,128]{3,2,1,0:T(4,128)} %get-tuple-element.57), calls=%async_computation.1 | async-start | bytes 393216 | tf_op jit(solution)/shard_map/all_to_all | solution.py:901
  30.4 0.7 %collective-permute-start.3 = (f32[28,8,128]{2,1,0:T(8,128)S(1)}, f32[28,8,128]{2,1,0:T(8,128)S(1)}, u32[]{:S(2)}, u32[]{:S(2)}) collective-permute-start(f32[28,8,128]{2,1,0:T(8,128)S(1)} %get-tuple-element.58), channel_id=1, source_target_pairs={{4,8},{12,24},{28,16},{20,21},{17,29},{25,13},{9,5},{1,2},{6,10},{... | collective-permute-start | bytes 344072 | tf_op jit(solution)/shard_map/ppermute | solution.py:899
  31.1 3.2 %collective-permute-start.2 = (f32[28,8,128]{2,1,0:T(8,128)S(1)}, f32[28,8,128]{2,1,0:T(8,128)S(1)}, u32[]{:S(2)}, u32[]{:S(2)}) collective-permute-start(f32[28,8,128]{2,1,0:T(8,128)S(1)} %get-tuple-element.58), channel_id=1, source_target_pairs={{0,4},{8,12},{24,28},{16,20},{21,17},{29,25},{13,9},{5,1},{2,6},{1... | collective-permute-start | bytes 344072 | tf_op jit(solution)/shard_map/ppermute | solution.py:898
  34.3 4.9 %all-to-all-done.1.gathered = f32[32,3,4,128]{3,2,1,0:T(4,128)S(1)} async-done(((f32[32,3,4,128]{3,2,1,0:T(4,128)}), f32[32,3,4,128]{3,2,1,0:T(4,128)S(1)}, u32[]{:S(2)}, u32[]{:S(2)}) %all-to-all-start.1) | async-done | bytes 196640 | tf_op jit(solution)/shard_map/all_to_all | solution.py:901
  39.1 2.5 %coarse.1.e_two = f32[6,8,128]{2,1,0:T(8,128)S(1)} custom-call(f32[32,3,4,128]{3,2,1,0:T(4,128)S(1)} %all-to-all-done.1.gathered), custom_call_target="tpu_custom_call" | custom-call | tf_op jit(solution)/shard_map/coarse/pallas_call | solution.py:782
  41.6 0.0 collective-permute-done.3.rim_odd
  41.6 0.0 collective-permute-done.2.rim_even
  41.6 1.3 %up_strokes.1 = f32[8,64,128]{2,1,0:T(8,128)S(1)} custom-call(f32[6,8,128]{2,1,0:T(8,128)S(1)} %coarse.1.e_two, f32[28,8,128]{2,1,0:T(8,128)S(1)} %collective-permute-done.2.rim_even, f32[28,8,128]{2,1,0:T(8,128)S(1)} %collective-permute-done.3.rim_odd, f32[8,4,8,128]{3,2,1,0:T(8,128)S(1)} %get-tuple-element.38.own_b, ...), custom_call_target="tpu_custom_call" | custom-call | tf_op jit(solution)/shard_map/up_strokes/pallas_call | solution.py:491
  42.9 9.1 %all_to_all.16.in_ref = f32[8,64,128]{2,1,0:T(8,128)S(1)} all-to-all(f32[8,64,128]{2,1,0:T(8,128)S(1)} %up_strokes.1), channel_id=1, replica_groups=mesh['gx'=4,'gy'=2,'gz'=4] {'gy','gx'}, dimensions={0} | all-to-all | bytes 524288 | tf_op jit(solution)/shard_map/all_to_all | solution.py:902
  52.0 1.1 %unpack.1 = (f32[8,32,128]{2,1,0:T(8,128)}, f32[8,32,128]{2,1,0:T(8,128)}) custom-call(f32[8,64,128]{2,1,0:T(8,128)S(1)} %all_to_all.16.in_ref), custom_call_target="tpu_custom_call" | custom-call | tf_op jit(solution)/shard_map/unpack/pallas_call | solution.py:873
Async XLA Ops:
  15.8 3.2 %collective-permute-start = (f32[19,4,8,128]{3,2,1,0:T(8,128)S(1)}, f32[19,4,8,128]{3,2,1,0:T(8,128)S(1)}, u32[]{:S(2)}, u32[]{:S(2)}) collective-permute-start(f32[19,4,8,128]{3,2,1,0:T(8,128)S(1)} %get-tuple-element.39), channel_id=1, source_target_pairs={{4,8},{12,24},{28,16},{20,21},{17,29},{25,13},{9,5},{1,2},{6,10},{... | collective-permute-start | bytes 933896 | tf_op jit(solution)/shard_map/ppermute | solution.py:894
  16.5 3.3 %collective-permute-start.1 = (f32[19,4,8,128]{3,2,1,0:T(8,128)S(1)}, f32[19,4,8,128]{3,2,1,0:T(8,128)S(1)}, u32[]{:S(2)}, u32[]{:S(2)}) collective-permute-start(f32[19,4,8,128]{3,2,1,0:T(8,128)S(1)} %get-tuple-element.40), channel_id=1, source_target_pairs={{0,4},{8,12},{24,28},{16,20},{21,17},{29,25},{13,9},{5,1},{2,6},{1... | collective-permute-start | bytes 933896 | tf_op jit(solution)/shard_map/ppermute | solution.py:893
  22.0 17.1 %all-to-all-start.1 = ((f32[32,3,4,128]{3,2,1,0:T(4,128)}), f32[32,3,4,128]{3,2,1,0:T(4,128)S(1)}, u32[]{:S(2)}, u32[]{:S(2)}) async-start(f32[32,3,4,128]{3,2,1,0:T(4,128)} %get-tuple-element.57), calls=%async_computation.1 | async-start | bytes 393216 | tf_op jit(solution)/shard_map/all_to_all | solution.py:901
  30.4 11.2 %collective-permute-start.3 = (f32[28,8,128]{2,1,0:T(8,128)S(1)}, f32[28,8,128]{2,1,0:T(8,128)S(1)}, u32[]{:S(2)}, u32[]{:S(2)}) collective-permute-start(f32[28,8,128]{2,1,0:T(8,128)S(1)} %get-tuple-element.58), channel_id=1, source_target_pairs={{4,8},{12,24},{28,16},{20,21},{17,29},{25,13},{9,5},{1,2},{6,10},{... | collective-permute-start | bytes 344072 | tf_op jit(solution)/shard_map/ppermute | solution.py:899
  31.1 10.6 %collective-permute-start.2 = (f32[28,8,128]{2,1,0:T(8,128)S(1)}, f32[28,8,128]{2,1,0:T(8,128)S(1)}, u32[]{:S(2)}, u32[]{:S(2)}) collective-permute-start(f32[28,8,128]{2,1,0:T(8,128)S(1)} %get-tuple-element.58), channel_id=1, source_target_pairs={{0,4},{8,12},{24,28},{16,20},{21,17},{29,25},{13,9},{5,1},{2,6},{1... | collective-permute-start | bytes 344072 | tf_op jit(solution)/shard_map/ppermute | solution.py:898

commit v8 on v7

--- a/solution.py
+++ b/solution.py
@@ -256,12 +256,15 @@
 def pack_kernel(fields, out_ref, turned, staged):
     z = lax.axis_index("gz")
     lane = lane_ids()
+    trade = lane < jnp.where(lax.axis_index("gy") == 0, 128, 0)
     for a in range(3):
         for xg in range(2):
             slot = turned.at[2 * a + xg]
             slot[...] = fields[a, 4 * xg : 4 * xg + 4].reshape(128, 128).T
             for k in range(4):
                 tiles = [slot[pl.ds(depth_of(k, g), 8, stride=16), :] for g in range(4)]
+                a1, a3 = tiles[1], tiles[3]
+                tiles[1], tiles[3] = jnp.where(trade, a3, a1), jnp.where(trade, a1, a3)
                 for x4, tile in enumerate(regroup(tiles, 1, 32, lane)):
                     staged[pl.ds(a * 32 + k * 8 + 2 * x4 + xg, 8, stride=96), :] = tile
     for x in range(GX):
@@ -330,8 +333,9 @@
             for x in range(GX):
                 first = in_ref[x, pl.ds(a * 32 + k * 8, 8), :]
                 second = in_ref[GX + x, pl.ds(a * 32 + k * 8, 8), :]
-                part[0].append(jnp.where(low, first, lanes(second, 32)))
-                part[1].append(jnp.where(low, lanes(first, -32), second))
+                turned = lanes(jnp.where(low, second, first), 32)
+                part[0].append(jnp.where(low, first, turned))
+                part[1].append(jnp.where(low, turned, second))
             for pp in range(2):
                 planes[k + 4 * pp] = jnp.stack(regroup(part[pp], 0, 2, row))
                 if a == 2:
@@ -836,8 +840,9 @@
                 parts.append(regroup([value[0, i] for i in range(4)], 0, 2, row))
             for i in range(GX):
                 one, two = parts[0][i], parts[1][i]
-                out[i, pl.ds(o * 32 + k * 8, 8), :] = jnp.where(low, one, lanes(two, 32))
-                out[GX + i, pl.ds(o * 32 + k * 8, 8), :] = jnp.where(low, lanes(one, -32), two)
+                turned = lanes(jnp.where(low, two, one), 32)
+                out[i, pl.ds(o * 32 + k * 8, 8), :] = jnp.where(low, one, turned)
+                out[GX + i, pl.ds(o * 32 + k * 8, 8), :] = jnp.where(low, turned, two)
 
 
 def up(*operands):
@@ -850,6 +855,7 @@
 def unpack_kernel(in_ref, v_ref, r_ref, fields, turned, staged, left):
     z = lax.axis_index("gz")
     lane = lane_ids()
+    trade = lane < jnp.where(lax.axis_index("gy") == 1, 128, 0)
     for x in range(GX):
         for y in range(GY):
             start = pl.multiple_of(chunk_of(x, y, z) * 64, 64)
@@ -860,7 +866,10 @@
             slot = turned.at[2 * o + xg]
             for k in range(4):
                 tiles = [staged[pl.ds(o * 32 + k * 8 + 2 * x4 + xg, 8, stride=64), :] for x4 in range(4)]
-                for g, tile in enumerate(regroup(tiles, 1, 32, lane)):
+                tiles = regroup(tiles, 1, 32, lane)
+                a0, a2 = tiles[0], tiles[2]
+                tiles[0], tiles[2] = jnp.where(trade, a2, a0), jnp.where(trade, a0, a2)
+                for g, tile in enumerate(tiles):
                     slot[pl.ds(depth_of(k, g), 8, stride=16), :] = tile
             fields[o, 4 * xg : 4 * xg + 4] = slot[...].T.reshape(4, 32, 128)
         copy.start()

time: 53.4 us -> 53.3 us (level)
  no operation moved by 1% of the time
where the time goes in v8:
time: 53.3 us; the launch traced here: 53 us
  blocking collectives  22.2 us (42%)
  starting transfers between devices  15 us (28%)
  Pallas kernels  8.37 us (16%)
  waiting for transfers between devices  5.66 us (11%)
  other arithmetic  1.06 us (2%)
  between operations  0.71 us (1%)
    all_to_all x1, blocking collectives, slab_shards(): own, own_b, to_even, to_odd = to_slab(lax.all_to_all(packed, RING, 0, 0))  13.1 us
    all_to_all x1, blocking collectives, slab_shards(): return tuple(unpack(lax.all_to_all(result, RING, 0, 0)))  9.1 us
    all_to_all x1, starting transfers between devices, slab_shards(): lax.all_to_all(gather, ('gx', 'gz', 'gy'), 0, 0)  8.35 us
    all_to_all x1, waiting for transfers between devices, slab_shards(): lax.all_to_all(gather, ('gx', 'gz', 'gy'), 0, 0)  4.88 us
    pallas_call x3, Pallas kernels, call(): pl.pallas_call(kernel, out_shape=out_shape, in_specs=[vmem] * len(operand...  3.94 us
    ppermute x1, starting transfers between devices, slab_shards(): rim_even = lax.ppermute(rim, ALL, even_pairs)  3.19 us
    pallas_call x1, Pallas kernels, coarse(): pl.pallas_call(coarse_kernel, out_shape=shape_of(6), in_specs=[vmem], out...  2.46 us
    ppermute x1, starting transfers between devices, slab_shards(): even = lax.ppermute(to_even, ALL, even_pairs)  2.1 us
  transfers between devices with their start and end apart: 5, of which 2 were waited for; matrix products, arithmetic and copies ran while one was open for 0% of the time, Pallas kernels for 5%

profile of v8, /device:TPU:0, one launch (start us, length us, event | category | flops | bytes accessed | tf_op | source)
XLA Modules:
  0.0 53.0 jit_solution(11216801439045667716)
XLA Ops:
  0.6 1.1 %pad_maximum_fusion.fields = f32[3,8,32,128]{3,2,1,0:T(8,128)S(1)} fusion(f32[1,8,32,128]{3,2,1,0:T(8,128)} %bitcast.3, f32[1,8,32,128]{3,2,1,0:T(8,128)} %bitcast.4, f32[1,8,32,128]{3,2,1,0:T(8,128)} %bitcast.5), kind=kLoop, calls=%fused_computation | loop fusion | flops 196608 | bytes 786432 | tf_op jit(solution)/shard_map/stack | solution.py:900
  1.7 0.6 %pack.1 = f32[8,96,128]{2,1,0:T(8,128)S(1)} custom-call(f32[3,8,32,128]{3,2,1,0:T(8,128)S(1)} %pad_maximum_fusion.fields), custom_call_target="tpu_custom_call" | custom-call | tf_op jit(solution)/shard_map/pack/pallas_call | solution.py:277
  2.3 13.1 %all_to_all.15.in_ref = f32[8,96,128]{2,1,0:T(8,128)S(1)} all-to-all(f32[8,96,128]{2,1,0:T(8,128)S(1)} %pack.1), channel_id=1, replica_groups=mesh['gx'=4,'gy'=2,'gz'=4] {'gy','gx'}, dimensions={0} | all-to-all | bytes 786432 | tf_op jit(solution)/shard_map/all_to_all | solution.py:901
  15.5 0.2 to_slab.1
  15.7 0.7 %collective-permute-start = (f32[19,4,8,128]{3,2,1,0:T(8,128)S(1)}, f32[19,4,8,128]{3,2,1,0:T(8,128)S(1)}, u32[]{:S(2)}, u32[]{:S(2)}) collective-permute-start(f32[19,4,8,128]{3,2,1,0:T(8,128)S(1)} %get-tuple-element.39), channel_id=1, source_target_pairs={{4,8},{12,24},{28,16},{20,21},{17,29},{25,13},{9,5},{1,2},{6,10},{... | collective-permute-start | bytes 933896 | tf_op jit(solution)/shard_map/ppermute | solution.py:903
  16.4 2.1 %collective-permute-start.1 = (f32[19,4,8,128]{3,2,1,0:T(8,128)S(1)}, f32[19,4,8,128]{3,2,1,0:T(8,128)S(1)}, u32[]{:S(2)}, u32[]{:S(2)}) collective-permute-start(f32[19,4,8,128]{3,2,1,0:T(8,128)S(1)} %get-tuple-element.40), channel_id=1, source_target_pairs={{0,4},{8,12},{24,28},{16,20},{21,17},{29,25},{13,9},{5,1},{2,6},{1... | collective-permute-start | bytes 933896 | tf_op jit(solution)/shard_map/ppermute | solution.py:902
  18.5 0.4 down_pre.1
  18.9 0.0 collective-permute-done.odd
  18.9 0.8 %collective-permute-done.1.even = f32[19,4,8,128]{3,2,1,0:T(8,128)S(1)} collective-permute-done((f32[19,4,8,128]{3,2,1,0:T(8,128)S(1)}, f32[19,4,8,128]{3,2,1,0:T(8,128)S(1)}, u32[]{:S(2)}, u32[]{:S(2)}) %collective-permute-start.1) | collective-permute-done | bytes 311328 | tf_op jit(solution)/shard_map/ppermute | solution.py:902
  19.7 2.2 %down_post.1 = (f32[32,3,4,128]{3,2,1,0:T(4,128)}, f32[28,8,128]{2,1,0:T(8,128)S(1)}, f32[4,4,8,128]{3,2,1,0:T(8,128)S(1)}, f32[4,4,8,128]{3,2,1,0:T(8,128)S(1)}...) custom-call(f32[2,8,4,8,128]{4,3,2,1,0:T(8,128)S(1)} %get-tuple-elem, ...), custom_call_target="tpu_custom_call" | custom-call | tf_op jit(solution)/shard_map/down_post/pallas_call | solution.py:495
  21.9 8.3 %all-to-all-start.1 = ((f32[32,3,4,128]{3,2,1,0:T(4,128)}), f32[32,3,4,128]{3,2,1,0:T(4,128)S(1)}, u32[]{:S(2)}, u32[]{:S(2)}) async-start(f32[32,3,4,128]{3,2,1,0:T(4,128)} %get-tuple-element.57), calls=%async_computation.1 | async-start | bytes 393216 | tf_op jit(solution)/shard_map/all_to_all | solution.py:910
  30.3 0.7 %collective-permute-start.3 = (f32[28,8,128]{2,1,0:T(8,128)S(1)}, f32[28,8,128]{2,1,0:T(8,128)S(1)}, u32[]{:S(2)}, u32[]{:S(2)}) collective-permute-start(f32[28,8,128]{2,1,0:T(8,128)S(1)} %get-tuple-element.58), channel_id=1, source_target_pairs={{4,8},{12,24},{28,16},{20,21},{17,29},{25,13},{9,5},{1,2},{6,10},{... | collective-permute-start | bytes 344072 | tf_op jit(solution)/shard_map/ppermute | solution.py:908
  30.9 3.2 %collective-permute-start.2 = (f32[28,8,128]{2,1,0:T(8,128)S(1)}, f32[28,8,128]{2,1,0:T(8,128)S(1)}, u32[]{:S(2)}, u32[]{:S(2)}) collective-permute-start(f32[28,8,128]{2,1,0:T(8,128)S(1)} %get-tuple-element.58), channel_id=1, source_target_pairs={{0,4},{8,12},{24,28},{16,20},{21,17},{29,25},{13,9},{5,1},{2,6},{1... | collective-permute-start | bytes 344072 | tf_op jit(solution)/shard_map/ppermute | solution.py:907
  34.1 4.9 %all-to-all-done.1.gathered = f32[32,3,4,128]{3,2,1,0:T(4,128)S(1)} async-done(((f32[32,3,4,128]{3,2,1,0:T(4,128)}), f32[32,3,4,128]{3,2,1,0:T(4,128)S(1)}, u32[]{:S(2)}, u32[]{:S(2)}) %all-to-all-start.1) | async-done | bytes 196640 | tf_op jit(solution)/shard_map/all_to_all | solution.py:910
  39.0 2.5 %coarse.1.e_two = f32[6,8,128]{2,1,0:T(8,128)S(1)} custom-call(f32[32,3,4,128]{3,2,1,0:T(4,128)S(1)} %all-to-all-done.1.gathered), custom_call_target="tpu_custom_call" | custom-call | tf_op jit(solution)/shard_map/coarse/pallas_call | solution.py:786
  41.5 0.0 collective-permute-done.3.rim_odd
  41.5 0.0 collective-permute-done.2.rim_even
  41.5 1.3 %up_strokes.1 = f32[8,64,128]{2,1,0:T(8,128)S(1)} custom-call(f32[6,8,128]{2,1,0:T(8,128)S(1)} %coarse.1.e_two, f32[28,8,128]{2,1,0:T(8,128)S(1)} %collective-permute-done.2.rim_even, f32[28,8,128]{2,1,0:T(8,128)S(1)} %collective-permute-done.3.rim_odd, f32[8,4,8,128]{3,2,1,0:T(8,128)S(1)} %get-tuple-element.38.own_b, ...), custom_call_target="tpu_custom_call" | custom-call | tf_op jit(solution)/shard_map/up_strokes/pallas_call | solution.py:495
  42.8 9.1 %all_to_all.16.in_ref = f32[8,64,128]{2,1,0:T(8,128)S(1)} all-to-all(f32[8,64,128]{2,1,0:T(8,128)S(1)} %up_strokes.1), channel_id=1, replica_groups=mesh['gx'=4,'gy'=2,'gz'=4] {'gy','gx'}, dimensions={0} | all-to-all | bytes 524288 | tf_op jit(solution)/shard_map/all_to_all | solution.py:911
  51.9 1.1 %unpack.1 = (f32[8,32,128]{2,1,0:T(8,128)}, f32[8,32,128]{2,1,0:T(8,128)}) custom-call(f32[8,64,128]{2,1,0:T(8,128)S(1)} %all_to_all.16.in_ref), custom_call_target="tpu_custom_call" | custom-call | tf_op jit(solution)/shard_map/unpack/pallas_call | solution.py:882
Async XLA Ops:
  15.7 3.2 %collective-permute-start = (f32[19,4,8,128]{3,2,1,0:T(8,128)S(1)}, f32[19,4,8,128]{3,2,1,0:T(8,128)S(1)}, u32[]{:S(2)}, u32[]{:S(2)}) collective-permute-start(f32[19,4,8,128]{3,2,1,0:T(8,128)S(1)} %get-tuple-element.39), channel_id=1, source_target_pairs={{4,8},{12,24},{28,16},{20,21},{17,29},{25,13},{9,5},{1,2},{6,10},{... | collective-permute-start | bytes 933896 | tf_op jit(solution)/shard_map/ppermute | solution.py:903
  16.4 3.3 %collective-permute-start.1 = (f32[19,4,8,128]{3,2,1,0:T(8,128)S(1)}, f32[19,4,8,128]{3,2,1,0:T(8,128)S(1)}, u32[]{:S(2)}, u32[]{:S(2)}) collective-permute-start(f32[19,4,8,128]{3,2,1,0:T(8,128)S(1)} %get-tuple-element.40), channel_id=1, source_target_pairs={{0,4},{8,12},{24,28},{16,20},{21,17},{29,25},{13,9},{5,1},{2,6},{1... | collective-permute-start | bytes 933896 | tf_op jit(solution)/shard_map/ppermute | solution.py:902
  21.9 17.1 %all-to-all-start.1 = ((f32[32,3,4,128]{3,2,1,0:T(4,128)}), f32[32,3,4,128]{3,2,1,0:T(4,128)S(1)}, u32[]{:S(2)}, u32[]{:S(2)}) async-start(f32[32,3,4,128]{3,2,1,0:T(4,128)} %get-tuple-element.57), calls=%async_computation.1 | async-start | bytes 393216 | tf_op jit(solution)/shard_map/all_to_all | solution.py:910
  30.3 11.2 %collective-permute-start.3 = (f32[28,8,128]{2,1,0:T(8,128)S(1)}, f32[28,8,128]{2,1,0:T(8,128)S(1)}, u32[]{:S(2)}, u32[]{:S(2)}) collective-permute-start(f32[28,8,128]{2,1,0:T(8,128)S(1)} %get-tuple-element.58), channel_id=1, source_target_pairs={{4,8},{12,24},{28,16},{20,21},{17,29},{25,13},{9,5},{1,2},{6,10},{... | collective-permute-start | bytes 344072 | tf_op jit(solution)/shard_map/ppermute | solution.py:908
  30.9 10.6 %collective-permute-start.2 = (f32[28,8,128]{2,1,0:T(8,128)S(1)}, f32[28,8,128]{2,1,0:T(8,128)S(1)}, u32[]{:S(2)}, u32[]{:S(2)}) collective-permute-start(f32[28,8,128]{2,1,0:T(8,128)S(1)} %get-tuple-element.58), channel_id=1, source_target_pairs={{0,4},{8,12},{24,28},{16,20},{21,17},{29,25},{13,9},{5,1},{2,6},{1... | collective-permute-start | bytes 344072 | tf_op jit(solution)/shard_map/ppermute | solution.py:907

commit v9 on v8

--- a/solution.py
+++ b/solution.py
@@ -753,8 +753,9 @@
         base = (1.0 + carry - gain) * v + gain * rhs_low
         if before is not None:
             base = base - carry * before
-        total = flat(v, flat_low, 2, 8) + (inner_low * turned + rim_low * beyond)
-        before, v = v, base + gain * total
+        base = base + gain * (flat_low[0] * rows(v, -2) + flat_low[1] * rows(v, 2))
+        total = flat_low[2] * lanes(v, -8) + flat_low[3] * lanes(v, 8)
+        before, v = v, base + gain * (total + (inner_low * turned + rim_low * beyond))
     v = jnp.concatenate([jnp.where(second, lanes(v, 4), v), jnp.where(second, v, lanes(v, -4))], axis=0)
     va, vb = sweeps_two(None, (ua + v, ub + v), factors)
     for group in range(8):

time: 53.3 us -> 53.3 us (level)
  no operation moved by 1% of the time
where the time goes in v9:
time: 53.3 us; the launch traced here: 53 us
  blocking collectives  22.2 us (42%)
  starting transfers between devices  15 us (28%)
  Pallas kernels  8.36 us (16%)
  waiting for transfers between devices  5.66 us (11%)
  other arithmetic  1.06 us (2%)
  between operations  0.71 us (1%)
    all_to_all x1, blocking collectives, slab_shards(): own, own_b, to_even, to_odd = to_slab(lax.all_to_all(packed, RING, 0, 0))  13.1 us
    all_to_all x1, blocking collectives, slab_shards(): return tuple(unpack(lax.all_to_all(result, RING, 0, 0)))  9.1 us
    all_to_all x1, starting transfers between devices, slab_shards(): lax.all_to_all(gather, ('gx', 'gz', 'gy'), 0, 0)  8.35 us
    all_to_all x1, waiting for transfers between devices, slab_shards(): lax.all_to_all(gather, ('gx', 'gz', 'gy'), 0, 0)  4.88 us
    pallas_call x3, Pallas kernels, call(): pl.pallas_call(kernel, out_shape=out_shape, in_specs=[vmem] * len(operand...  3.94 us
    ppermute x1, starting transfers between devices, slab_shards(): rim_even = lax.ppermute(rim, ALL, even_pairs)  3.19 us
    pallas_call x1, Pallas kernels, coarse(): pl.pallas_call(coarse_kernel, out_shape=shape_of(6), in_specs=[vmem], out...  2.45 us
    ppermute x1, starting transfers between devices, slab_shards(): even = lax.ppermute(to_even, ALL, even_pairs)  2.1 us
  transfers between devices with their start and end apart: 5, of which 2 were waited for; matrix products, arithmetic and copies ran while one was open for 0% of the time, Pallas kernels for 5%

profile of v9, /device:TPU:0, one launch (start us, length us, event | category | flops | bytes accessed | tf_op | source)
XLA Modules:
  0.0 53.0 jit_solution(14310859960445302649)
XLA Ops:
  0.6 1.1 %pad_maximum_fusion.fields = f32[3,8,32,128]{3,2,1,0:T(8,128)S(1)} fusion(f32[1,8,32,128]{3,2,1,0:T(8,128)} %bitcast.3, f32[1,8,32,128]{3,2,1,0:T(8,128)} %bitcast.4, f32[1,8,32,128]{3,2,1,0:T(8,128)} %bitcast.5), kind=kLoop, calls=%fused_computation | loop fusion | flops 196608 | bytes 786432 | tf_op jit(solution)/shard_map/stack | solution.py:901
  1.7 0.6 %pack.1 = f32[8,96,128]{2,1,0:T(8,128)S(1)} custom-call(f32[3,8,32,128]{3,2,1,0:T(8,128)S(1)} %pad_maximum_fusion.fields), custom_call_target="tpu_custom_call" | custom-call | tf_op jit(solution)/shard_map/pack/pallas_call | solution.py:277
  2.3 13.1 %all_to_all.15.in_ref = f32[8,96,128]{2,1,0:T(8,128)S(1)} all-to-all(f32[8,96,128]{2,1,0:T(8,128)S(1)} %pack.1), channel_id=1, replica_groups=mesh['gx'=4,'gy'=2,'gz'=4] {'gy','gx'}, dimensions={0} | all-to-all | bytes 786432 | tf_op jit(solution)/shard_map/all_to_all | solution.py:902
  15.5 0.2 to_slab.1
  15.7 0.7 %collective-permute-start = (f32[19,4,8,128]{3,2,1,0:T(8,128)S(1)}, f32[19,4,8,128]{3,2,1,0:T(8,128)S(1)}, u32[]{:S(2)}, u32[]{:S(2)}) collective-permute-start(f32[19,4,8,128]{3,2,1,0:T(8,128)S(1)} %get-tuple-element.39), channel_id=1, source_target_pairs={{4,8},{12,24},{28,16},{20,21},{17,29},{25,13},{9,5},{1,2},{6,10},{... | collective-permute-start | bytes 933896 | tf_op jit(solution)/shard_map/ppermute | solution.py:904
  16.4 2.1 %collective-permute-start.1 = (f32[19,4,8,128]{3,2,1,0:T(8,128)S(1)}, f32[19,4,8,128]{3,2,1,0:T(8,128)S(1)}, u32[]{:S(2)}, u32[]{:S(2)}) collective-permute-start(f32[19,4,8,128]{3,2,1,0:T(8,128)S(1)} %get-tuple-element.40), channel_id=1, source_target_pairs={{0,4},{8,12},{24,28},{16,20},{21,17},{29,25},{13,9},{5,1},{2,6},{1... | collective-permute-start | bytes 933896 | tf_op jit(solution)/shard_map/ppermute | solution.py:903
  18.5 0.4 down_pre.1
  18.9 0.0 collective-permute-done.odd
  18.9 0.8 %collective-permute-done.1.even = f32[19,4,8,128]{3,2,1,0:T(8,128)S(1)} collective-permute-done((f32[19,4,8,128]{3,2,1,0:T(8,128)S(1)}, f32[19,4,8,128]{3,2,1,0:T(8,128)S(1)}, u32[]{:S(2)}, u32[]{:S(2)}) %collective-permute-start.1) | collective-permute-done | bytes 311328 | tf_op jit(solution)/shard_map/ppermute | solution.py:903
  19.7 2.2 %down_post.1 = (f32[32,3,4,128]{3,2,1,0:T(4,128)}, f32[28,8,128]{2,1,0:T(8,128)S(1)}, f32[4,4,8,128]{3,2,1,0:T(8,128)S(1)}, f32[4,4,8,128]{3,2,1,0:T(8,128)S(1)}...) custom-call(f32[2,8,4,8,128]{4,3,2,1,0:T(8,128)S(1)} %get-tuple-elem, ...), custom_call_target="tpu_custom_call" | custom-call | tf_op jit(solution)/shard_map/down_post/pallas_call | solution.py:495
  21.9 8.3 %all-to-all-start.1 = ((f32[32,3,4,128]{3,2,1,0:T(4,128)}), f32[32,3,4,128]{3,2,1,0:T(4,128)S(1)}, u32[]{:S(2)}, u32[]{:S(2)}) async-start(f32[32,3,4,128]{3,2,1,0:T(4,128)} %get-tuple-element.57), calls=%async_computation.1 | async-start | bytes 393216 | tf_op jit(solution)/shard_map/all_to_all | solution.py:911
  30.3 0.7 %collective-permute-start.3 = (f32[28,8,128]{2,1,0:T(8,128)S(1)}, f32[28,8,128]{2,1,0:T(8,128)S(1)}, u32[]{:S(2)}, u32[]{:S(2)}) collective-permute-start(f32[28,8,128]{2,1,0:T(8,128)S(1)} %get-tuple-element.58), channel_id=1, source_target_pairs={{4,8},{12,24},{28,16},{20,21},{17,29},{25,13},{9,5},{1,2},{6,10},{... | collective-permute-start | bytes 344072 | tf_op jit(solution)/shard_map/ppermute | solution.py:909
  30.9 3.2 %collective-permute-start.2 = (f32[28,8,128]{2,1,0:T(8,128)S(1)}, f32[28,8,128]{2,1,0:T(8,128)S(1)}, u32[]{:S(2)}, u32[]{:S(2)}) collective-permute-start(f32[28,8,128]{2,1,0:T(8,128)S(1)} %get-tuple-element.58), channel_id=1, source_target_pairs={{0,4},{8,12},{24,28},{16,20},{21,17},{29,25},{13,9},{5,1},{2,6},{1... | collective-permute-start | bytes 344072 | tf_op jit(solution)/shard_map/ppermute | solution.py:908
  34.1 4.9 %all-to-all-done.1.gathered = f32[32,3,4,128]{3,2,1,0:T(4,128)S(1)} async-done(((f32[32,3,4,128]{3,2,1,0:T(4,128)}), f32[32,3,4,128]{3,2,1,0:T(4,128)S(1)}, u32[]{:S(2)}, u32[]{:S(2)}) %all-to-all-start.1) | async-done | bytes 196640 | tf_op jit(solution)/shard_map/all_to_all | solution.py:911
  39.0 2.4 %coarse.1.e_two = f32[6,8,128]{2,1,0:T(8,128)S(1)} custom-call(f32[32,3,4,128]{3,2,1,0:T(4,128)S(1)} %all-to-all-done.1.gathered), custom_call_target="tpu_custom_call" | custom-call | tf_op jit(solution)/shard_map/coarse/pallas_call | solution.py:787
  41.5 0.0 collective-permute-done.3.rim_odd
  41.5 0.0 collective-permute-done.2.rim_even
  41.5 1.3 %up_strokes.1 = f32[8,64,128]{2,1,0:T(8,128)S(1)} custom-call(f32[6,8,128]{2,1,0:T(8,128)S(1)} %coarse.1.e_two, f32[28,8,128]{2,1,0:T(8,128)S(1)} %collective-permute-done.2.rim_even, f32[28,8,128]{2,1,0:T(8,128)S(1)} %collective-permute-done.3.rim_odd, f32[8,4,8,128]{3,2,1,0:T(8,128)S(1)} %get-tuple-element.38.own_b, ...), custom_call_target="tpu_custom_call" | custom-call | tf_op jit(solution)/shard_map/up_strokes/pallas_call | solution.py:495
  42.8 9.1 %all_to_all.16.in_ref = f32[8,64,128]{2,1,0:T(8,128)S(1)} all-to-all(f32[8,64,128]{2,1,0:T(8,128)S(1)} %up_strokes.1), channel_id=1, replica_groups=mesh['gx'=4,'gy'=2,'gz'=4] {'gy','gx'}, dimensions={0} | all-to-all | bytes 524288 | tf_op jit(solution)/shard_map/all_to_all | solution.py:912
  51.9 1.1 %unpack.1 = (f32[8,32,128]{2,1,0:T(8,128)}, f32[8,32,128]{2,1,0:T(8,128)}) custom-call(f32[8,64,128]{2,1,0:T(8,128)S(1)} %all_to_all.16.in_ref), custom_call_target="tpu_custom_call" | custom-call | tf_op jit(solution)/shard_map/unpack/pallas_call | solution.py:883
Async XLA Ops:
  15.7 3.2 %collective-permute-start = (f32[19,4,8,128]{3,2,1,0:T(8,128)S(1)}, f32[19,4,8,128]{3,2,1,0:T(8,128)S(1)}, u32[]{:S(2)}, u32[]{:S(2)}) collective-permute-start(f32[19,4,8,128]{3,2,1,0:T(8,128)S(1)} %get-tuple-element.39), channel_id=1, source_target_pairs={{4,8},{12,24},{28,16},{20,21},{17,29},{25,13},{9,5},{1,2},{6,10},{... | collective-permute-start | bytes 933896 | tf_op jit(solution)/shard_map/ppermute | solution.py:904
  16.4 3.3 %collective-permute-start.1 = (f32[19,4,8,128]{3,2,1,0:T(8,128)S(1)}, f32[19,4,8,128]{3,2,1,0:T(8,128)S(1)}, u32[]{:S(2)}, u32[]{:S(2)}) collective-permute-start(f32[19,4,8,128]{3,2,1,0:T(8,128)S(1)} %get-tuple-element.40), channel_id=1, source_target_pairs={{0,4},{8,12},{24,28},{16,20},{21,17},{29,25},{13,9},{5,1},{2,6},{1... | collective-permute-start | bytes 933896 | tf_op jit(solution)/shard_map/ppermute | solution.py:903
  21.9 17.1 %all-to-all-start.1 = ((f32[32,3,4,128]{3,2,1,0:T(4,128)}), f32[32,3,4,128]{3,2,1,0:T(4,128)S(1)}, u32[]{:S(2)}, u32[]{:S(2)}) async-start(f32[32,3,4,128]{3,2,1,0:T(4,128)} %get-tuple-element.57), calls=%async_computation.1 | async-start | bytes 393216 | tf_op jit(solution)/shard_map/all_to_all | solution.py:911
  30.3 11.2 %collective-permute-start.3 = (f32[28,8,128]{2,1,0:T(8,128)S(1)}, f32[28,8,128]{2,1,0:T(8,128)S(1)}, u32[]{:S(2)}, u32[]{:S(2)}) collective-permute-start(f32[28,8,128]{2,1,0:T(8,128)S(1)} %get-tuple-element.58), channel_id=1, source_target_pairs={{4,8},{12,24},{28,16},{20,21},{17,29},{25,13},{9,5},{1,2},{6,10},{... | collective-permute-start | bytes 344072 | tf_op jit(solution)/shard_map/ppermute | solution.py:909
  30.9 10.5 %collective-permute-start.2 = (f32[28,8,128]{2,1,0:T(8,128)S(1)}, f32[28,8,128]{2,1,0:T(8,128)S(1)}, u32[]{:S(2)}, u32[]{:S(2)}) collective-permute-start(f32[28,8,128]{2,1,0:T(8,128)S(1)} %get-tuple-element.58), channel_id=1, source_target_pairs={{0,4},{8,12},{24,28},{16,20},{21,17},{29,25},{13,9},{5,1},{2,6},{1... | collective-permute-start | bytes 344072 | tf_op jit(solution)/shard_map/ppermute | solution.py:908
